TPU v7x, 128 devices: a whole 4x4x4 slice. The times are simulated.
128 devices in a mesh: node: 16 (over x, z), dev: 8 (over y, core).
Axes of the slice: x: 4, y: 4, z: 4, core: 2. Of those that a mesh axis runs over, the one named last changes fastest.
Arguments:
- old_state: float32 [16384, 5, 512], P(('node', 'dev')), as said below
- old_tile_pos: int32 [16384], P(('node', 'dev')), may hold values from 0 to 16383, as said below
Outputs:
- stepped_state: float32 [5, 256, 256, 128], P(None, 'node', 'dev')
Inputs may be any that keep to these rules, and one draw needn't show every extreme that they name: Cells of old_state have density 0.5 to 2, velocity components -1 to 1 and pressure 0.5 to 2. A permutation. The tile in old slot s of device d goes to device old_tile_pos[s] // 128, which is d itself, a device within 4 of d in the order of node+dev (node slowest, no wrap), or the device (d + 64) mod 128. At most 8 tiles go from one device to another, and as many come back; every device exchanges exactly 8 tiles with the device 128 // 2 away, and in every draw some device exchanges exactly 8 tiles with each of the 8 devices within reach.
All inputs are finite; a program needn't handle non-finite values.
Results may differ from a plain program's by a relative error of at most 0.0003.
Values sent between devices are 32-bit elements; how exact they have to be, the bound alone decides.
No kernel may reach another device: no remote copies, remote signals or barrier semaphores. Data moves between devices by JAX's collectives and lax.ppermute only.
A program may use at most 128 MiB of HBM per device.

v0:
```python
import jax
import jax.numpy as jnp
from jax import lax
from jax.experimental import pallas as pl
from jax.experimental.pallas import tpu as pltpu
from jax.sharding import PartitionSpec as P

CX = 16
CY = 32
CZ = 128
FIELDS = 5
TILE = 8
MOVE = 8
TILES = 128
CELLS = 512
PARTS = CELLS // CZ
PLANES = FIELDS * PARTS + 1
ROWS = FIELDS * CX * CY
VMEM_LIMIT = 48 * 1024 * 1024

ROW_HALF = 64
ROW_FAR = 72
ROW_RELAY = 80
ROW_END = 112

AXES = ("node", "dev")


def iota(shape, dim):
    return lax.broadcasted_iota(jnp.int32, shape, dim)


def split3(value):
    high = value.astype(jnp.bfloat16)
    rest = value - high.astype(jnp.float32)
    mid = rest.astype(jnp.bfloat16)
    low = (rest - mid.astype(jnp.float32)).astype(jnp.bfloat16)
    return high, mid, low


def pick(choice, values):
    total = None
    for part in reversed(split3(values)):
        term = jnp.dot(choice, part, preferred_element_type=jnp.float32)
        total = term if total is None else total + term
    return total


def pack_kernel(me_ref, pos_ref, old_ref, near_ref, half_ref, far_ref, relay_ref):
    me = me_ref[0]
    node, dev = me // 8, me % 8
    pos = pos_ref[...]
    square = (TILES, TILES)
    by_lane = jnp.broadcast_to(pos // TILES, square)
    by_row = by_lane.T
    earlier = (by_lane == by_row) & (iota(square, 0) < iota(square, 1))
    rank = jnp.sum(earlier.astype(jnp.int32), axis=0, keepdims=True)
    owner = pos // TILES
    local = pos % TILES
    owner_node, owner_dev = owner // 8, owner % 8
    inside = jnp.where(jnp.abs(owner_dev - dev) == 4, ROW_HALF, owner_dev * MOVE)
    outside = jnp.where(owner_node == node ^ 8, ROW_FAR, ROW_RELAY + (owner_dev % 4) * MOVE)
    base = jnp.where(owner_node == node, inside, outside)
    target = jnp.where(owner == me, -1, base + rank)
    shape = (ROW_END, TILES)
    chosen = iota(shape, 0) == jnp.broadcast_to(target, shape)
    code = jnp.sum(
        jnp.where(chosen, jnp.broadcast_to(local + 1, shape), 0).astype(jnp.float32), axis=1, keepdims=True
    )
    code = jnp.broadcast_to(code, shape)
    choice = chosen.astype(jnp.float32).astype(jnp.bfloat16)

    def put(plane, value):
        for block in range(8):
            near_ref[block, plane] = value[block * MOVE : (block + 1) * MOVE]
        half_ref[plane] = value[ROW_HALF:ROW_FAR]
        far_ref[plane] = value[ROW_FAR:ROW_RELAY]
        for block in range(4):
            first = ROW_RELAY + block * MOVE
            relay_ref[block, plane] = value[first : first + MOVE]

    put(PLANES - 1, code)
    for field in range(FIELDS):
        rows = pick(choice, old_ref[field])
        for part in range(PARTS):
            put(field * PARTS + part, rows[:, part * CZ : (part + 1) * CZ])


def pack(me, pos, old):
    buffer = jax.ShapeDtypeStruct((PLANES, MOVE, CZ), jnp.float32)
    near = jax.ShapeDtypeStruct((8,) + buffer.shape, jnp.float32)
    relay = jax.ShapeDtypeStruct((4,) + buffer.shape, jnp.float32)
    vmem = pl.BlockSpec(memory_space=pltpu.VMEM)
    return pl.pallas_call(
        pack_kernel,
        out_shape=(near, buffer, buffer, relay),
        in_specs=[pl.BlockSpec(memory_space=pltpu.SMEM), vmem, vmem],
        out_specs=(vmem, vmem, vmem, vmem),
        compiler_params=pltpu.CompilerParams(vmem_limit_bytes=VMEM_LIMIT),
        name="pack",
    )(me, pos, old)


def grains(first, second, half_low, row_pick, lane_picks):
    first = pltpu.roll(first, 0, 1, stride=TILE, stride_axis=0)
    second = pltpu.roll(second, 64, 1, stride=TILE, stride_axis=0)
    result = []
    for half in range(2):
        mixed = jnp.where(half_low, first, second) if half == 0 else jnp.where(half_low, second, first)
        mixed = jnp.take_along_axis(mixed, row_pick, axis=0)
        result.append(jnp.take_along_axis(mixed, lane_picks[half], axis=1))
    return result


def unpack_kernel(
    me_ref, pos_ref, old_ref, near_ref, half_ref, far_ref,
    state_ref, prim_ref, x_low_ref, x_high_ref, y_low_ref, y_high_ref, tiles_ref,
):
    me = me_ref[0]
    pos = pos_ref[...]
    square = (TILES, TILES)
    kept = jnp.where(pos // TILES == me, pos % TILES, -1)
    kept_choice = jnp.broadcast_to(kept, square) == iota(square, 0)

    def arrived(plane):
        return jnp.concatenate(
            [near_ref[block, plane] for block in range(8)] + [half_ref[plane], far_ref[plane]], axis=0
        )

    code = jnp.concatenate([arrived(PLANES - 1), jnp.zeros((48, CZ), jnp.float32)], axis=0)
    code = code.T.astype(jnp.int32)
    new_choice = code == iota(square, 0) + 1
    choice = jnp.concatenate([kept_choice, new_choice], axis=1).astype(jnp.float32).astype(jnp.bfloat16)
    blank = jnp.zeros((48, CELLS), jnp.float32)
    for field in range(FIELDS):
        moved = jnp.concatenate([arrived(field * PARTS + part) for part in range(PARTS)], axis=1)
        tiles_ref[field] = pick(choice, jnp.concatenate([old_ref[field], moved, blank], axis=0))

    row = iota((TILE, CZ), 0)
    grain = iota((TILE, CZ), 1) // TILE
    half_low = (grain - row) % 16 < 8
    row_pick = (grain - row) % 8
    lane = iota((TILE, CZ), 1)
    lane_picks = [(lane + TILE * row + 64 * half) % CZ for half in range(2)]

    def brick(index, carry):
        across, up = index // 4, index % 4
        for part in range(PARTS):
            blocks = []
            for field in range(FIELDS):
                lanes = slice(part * CZ, (part + 1) * CZ)
                first = tiles_ref[field, pl.ds(pl.multiple_of(index * 16, 16), 8), lanes]
                second = tiles_ref[field, pl.ds(pl.multiple_of(index * 16 + 8, 8), 8), lanes]
                blocks.append(grains(first, second, half_low, row_pick, lane_picks))
            for half in range(2):
                density, mom_x, mom_y, mom_z, energy = [blocks[field][half] for field in range(FIELDS)]
                inverse = 1.0 / density
                vel = [mom_x * inverse, mom_y * inverse, mom_z * inverse]
                square_sum = vel[0] * vel[0] + vel[1] * vel[1] + vel[2] * vel[2]
                pressure = (1.4 - 1.0) * (energy - 0.5 * density * square_sum)
                cell_x = across * TILE + part * 2 + half
                for field in range(FIELDS):
                    start = pl.multiple_of((field * CX + cell_x) * CY + up * TILE, TILE)
                    state_ref[pl.ds(start, TILE), :] = blocks[field][half]
                    prim_ref[pl.ds(start, TILE), :] = density if field == 0 else (
                        pressure if field == 4 else vel[field - 1]
                    )
        return carry

    lax.fori_loop(0, 8, brick, 0)
    for field in range(FIELDS):
        x_low_ref[pl.ds(field * 96, 96), :] = prim_ref[pl.ds(field * CX * CY, 96), :]
        x_high_ref[pl.ds(field * 96, 96), :] = prim_ref[pl.ds((field * CX + 13) * CY, 96), :]
        for layer in range(3):
            for block in range(2):
                start = (field * CX + block * 8) * CY
                rows = pl.ds((field * 3 + layer) * CX + block * 8, 8)
                y_low_ref[rows, :] = prim_ref[pl.ds(start + layer, 8, stride=CY), :]
                y_high_ref[rows, :] = prim_ref[pl.ds(start + CY - 3 + layer, 8, stride=CY), :]


def unpack(me, pos, old, near, half, far):
    vmem = pl.BlockSpec(memory_space=pltpu.VMEM)
    grid_rows = jax.ShapeDtypeStruct((ROWS, CZ), jnp.float32)
    x_side = jax.ShapeDtypeStruct((FIELDS * 3 * CY, CZ), jnp.float32)
    y_side = jax.ShapeDtypeStruct((FIELDS * 3 * CX, CZ), jnp.float32)
    return pl.pallas_call(
        unpack_kernel,
        out_shape=(grid_rows, grid_rows, x_side, x_side, y_side, y_side),
        in_specs=[pl.BlockSpec(memory_space=pltpu.SMEM)] + [vmem] * 5,
        out_specs=(vmem,) * 6,
        scratch_shapes=[pltpu.VMEM((FIELDS, TILES, CELLS), jnp.float32)],
        compiler_params=pltpu.CompilerParams(vmem_limit_bytes=VMEM_LIMIT),
        name="unpack",
    )(me, pos, old, near, half, far)


def median_zero(first_value, second_value):
    return jnp.maximum(
        jnp.minimum(first_value, 0.0), jnp.minimum(jnp.maximum(first_value, 0.0), second_value)
    )


def interface(prev, here, after, far):
    value = 7.0 / 12.0 * (here + after) - 1.0 / 12.0 * (prev + far)
    return jnp.minimum(jnp.maximum(value, jnp.minimum(here, after)), jnp.maximum(here, after))


def edges(centre, below, above):
    low, high = below - centre, above - centre
    return centre + median_zero(low, -2.0 * high), centre + median_zero(high, -2.0 * low)


def face_flux(left, right, normal):
    def speeds(side):
        scaled = 1.4 * side[4]
        sound = scaled * lax.rsqrt(scaled * side[0])
        return side[normal] - sound, side[normal] + sound

    left_low, left_high = speeds(left)
    right_low, right_high = speeds(right)
    slowest = jnp.minimum(jnp.minimum(left_low, right_low), 0.0)
    fastest = jnp.maximum(jnp.maximum(left_high, right_high), 0.0)
    inverse = 1.0 / (fastest - slowest)
    share_left = fastest * inverse
    share_right = -slowest * inverse
    spread = slowest * share_left
    rate_left = share_left * left[normal] - spread
    rate_right = share_right * right[normal] + spread
    mass_left, mass_right = rate_left * left[0], rate_right * right[0]
    push_left, push_right = share_left * left[4], share_right * right[4]
    flux = [mass_left + mass_right]
    for axis in range(1, 4):
        value = mass_left * left[axis] + mass_right * right[axis]
        if axis == normal:
            value = value + (push_left + push_right)
        flux.append(value)

    def carried(side, rate, mass, push):
        speed_square = side[1] * side[1] + side[2] * side[2] + side[3] * side[3]
        return 2.5 * (rate * side[4]) + 0.5 * (mass * speed_square) + push * side[normal]

    flux.append(
        carried(left, rate_left, mass_left, push_left) + carried(right, rate_right, mass_right, push_right)
    )
    return flux


def sweep(load, count, normal, emit):
    every = range(FIELDS)
    cells = {cell: load(cell) for cell in (-3, -2, -1, 0)}
    below = [interface(cells[-3][f], cells[-2][f], cells[-1][f], cells[0][f]) for f in every]
    left = flux_below = None
    for cell in range(-1, count + 1):
        cells[cell + 2] = load(cell + 2)
        above = [
            interface(cells[cell - 1][f], cells[cell][f], cells[cell + 1][f], cells[cell + 2][f]) for f in every
        ]
        pairs = [edges(cells[cell][f], below[f], above[f]) for f in every]
        if left is not None:
            flux = face_flux(left, [pair[0] for pair in pairs], normal)
            if flux_below is not None:
                emit(cell - 1, [flux[f] - flux_below[f] for f in every])
            flux_below = flux
        left = [pair[1] for pair in pairs]
        below = above


def z_kernel(state_ref, prim_ref, out_ref):
    def rolled(value, shift):
        return pltpu.roll(value, shift % CZ, 1)

    def step(cell_x, carry):
        for up in range(CY // 8):
            starts = [
                pl.multiple_of((f * CX + cell_x) * CY + up * 8, 8) for f in range(FIELDS)
            ]
            here = [prim_ref[pl.ds(start, 8), :] for start in starts]
            lows, highs = [], []
            for value in here:
                after = rolled(value, -1)
                above = interface(rolled(value, 1), value, after, rolled(after, -1))
                low, high = edges(value, rolled(above, 1), above)
                lows.append(rolled(low, -1))
                highs.append(high)
            flux = face_flux(highs, lows, 3)
            for f in range(FIELDS):
                change = flux[f] - rolled(flux[f], 1)
                out_ref[pl.ds(starts[f], 8), :] = state_ref[pl.ds(starts[f], 8), :] - 0.1 * change
        return carry

    lax.fori_loop(0, CX, step, 0)


def y_kernel(before_ref, prim_ref, low_ref, high_ref, out_ref):
    def step(block, carry):
        def load(cell):
            if cell < 0 or cell >= CY:
                ref, layer = (low_ref, cell + 3) if cell < 0 else (high_ref, cell - CY)
                return [
                    ref[pl.ds(pl.multiple_of((f * 3 + layer) * CX + block * 8, 8), 8), :] for f in range(FIELDS)
                ]
            return [prim_ref[pl.ds((f * CX + block * 8) * CY + cell, 8, stride=CY), :] for f in range(FIELDS)]

        def emit(cell, change):
            for f in range(FIELDS):
                rows = pl.ds((f * CX + block * 8) * CY + cell, 8, stride=CY)
                out_ref[rows, :] = before_ref[rows, :] - 0.1 * change[f]

        sweep(load, CY, 2, emit)
        return carry

    lax.fori_loop(0, CX // 8, step, 0)


def x_kernel(before_ref, prim_ref, low_ref, high_ref, out_ref):
    def step(block, carry):
        def load(cell):
            if cell < 0 or cell >= CX:
                ref, layer = (low_ref, cell + 3) if cell < 0 else (high_ref, cell - CX)
                return [
                    ref[pl.ds(pl.multiple_of((f * 3 + layer) * CY + block * 8, 8), 8), :] for f in range(FIELDS)
                ]
            return [
                prim_ref[pl.ds(pl.multiple_of((f * CX + cell) * CY + block * 8, 8), 8), :] for f in range(FIELDS)
            ]

        def emit(cell, change):
            for f in range(FIELDS):
                rows = pl.ds(pl.multiple_of((f * CX + cell) * CY + block * 8, 8), 8)
                out_ref[rows, :] = before_ref[rows, :] - 0.1 * change[f]

        sweep(load, CX, 1, emit)
        return carry

    lax.fori_loop(0, CY // 8, step, 0)


def stage(kernel, name, *operands):
    vmem = pl.BlockSpec(memory_space=pltpu.VMEM)
    return pl.pallas_call(
        kernel,
        out_shape=jax.ShapeDtypeStruct((ROWS, CZ), jnp.float32),
        in_specs=[vmem] * len(operands),
        out_specs=vmem,
        compiler_params=pltpu.CompilerParams(vmem_limit_bytes=VMEM_LIMIT),
        cost_estimate=pl.CostEstimate(flops=20_000_000, bytes_accessed=4_000_000, transcendentals=200_000),
        name=name,
    )(*operands)


def shifted(value, axes, count, target):
    pairs = [(i, target(i)) for i in range(count)]
    return lax.ppermute(value, axes, [pair for pair in pairs if 0 <= pair[1] < count])


def next_node(device):
    node, dev = device // 8, device % 8
    return (node + (1 if dev >= 4 else -1)) * 8 + dev


def body(old_state, old_tile_pos):
    dev = lax.axis_index("dev")
    me = (lax.axis_index("node") * 8 + dev).astype(jnp.int32).reshape(1)
    pos = old_tile_pos.reshape(1, TILES)
    old = old_state.transpose(1, 0, 2)
    near, half, far, relay = pack(me, pos, old)
    relay = shifted(relay, AXES, 128, next_node)
    half = shifted(half, AXES, 128, lambda device: device ^ 4)
    far = shifted(far, AXES, 128, lambda device: device ^ 64)
    blank = jnp.zeros_like(relay)
    near = near + jnp.concatenate([jnp.where(dev >= 4, relay, blank), jnp.where(dev < 4, relay, blank)], axis=0)
    near = lax.all_to_all(near, "dev", split_axis=0, concat_axis=0, tiled=True)
    state, prim, x_low, x_high, y_low, y_high = unpack(me, pos, old, near, half, far)
    y_before = shifted(y_high, "dev", 8, lambda i: (i + 1) % 8)
    y_after = shifted(y_low, "dev", 8, lambda i: (i - 1) % 8)
    x_before = shifted(x_high, "node", 16, lambda i: (i + 1) % 16)
    x_after = shifted(x_low, "node", 16, lambda i: (i - 1) % 16)
    result = stage(z_kernel, "flux_third", state, prim)
    result = stage(y_kernel, "flux_second", result, prim, y_before, y_after)
    result = stage(x_kernel, "flux_first", result, prim, x_before, x_after)
    return result.reshape(FIELDS, CX, CY, CZ)


def solution(mesh):
    in_specs = (P(AXES, None, None), P(AXES))
    out_specs = P(None, "node", "dev", None)
    return jax.shard_map(body, mesh=mesh, in_specs=in_specs, out_specs=out_specs, check_vma=False)
```

profile of v0, /device:TPU:0, one launch (start us, length us, event | category | flops | bytes accessed | tf_op | source)
XLA Modules:
  0.0 59.3 jit_solution(14671287206876473634)
XLA Ops:
  0.0 0.0 copy-start
  0.0 1.3 %copy-done = f32[128,5,512]{2,0,1:T(8,128)S(1)} copy-done((f32[128,5,512]{2,0,1:T(8,128)S(1)}, f32[128,5,512]{2,0,1:T(8,128)}, u32[]{:S(2)}) %copy-start) | copy-done | bytes 1310744
  1.3 0.0 copy-start.2
  1.3 0.7 %copy-done.2 = s32[128]{0:T(128)S(1)} copy-done((s32[128]{0:T(128)S(1)}, s32[128]{0:T(128)}, u32[]{:S(2)}) %copy-start.2) | copy-done | bytes 536
  2.0 0.7 %pack.1 = (f32[8,21,8,128]{3,2,1,0:T(8,128)S(1)}, f32[21,8,128]{2,1,0:T(8,128)S(1)}, f32[21,8,128]{2,1,0:T(8,128)S(1)}, f32[4,21,8,128]{3,2,1,0:T(8,128)S(1)}) custom-call(s32[1]{0:T(128)} %bitcast.me_ref, s32[1,128]{1,0:T(1,128)S(1)} %bitcast.6, f32[5,128,512]{2,1,0:T(8,128)S(1)} %bitcast.4), custom_call_target="tpu_custom_call" | custom-call | tf_op jit(solution)/shard_map/pack/pallas_call | solution.py:94
  2.7 1.3 %collective-permute-start = (f32[4,21,8,128]{3,2,1,0:T(8,128)S(1)}, f32[4,21,8,128]{3,2,1,0:T(8,128)S(1)}, u32[]{:S(2)}, u32[]{:S(2)}) collective-permute-start(f32[4,21,8,128]{3,2,1,0:T(8,128)S(1)} %get-tuple-element.16), channel_id=1, source_target_pairs={{4,12},{5,13},{6,14},{7,15},{8,0},{9,1},{10,2},{11,3},{12,20},{13,... | collective-permute-start | bytes 1032200 | tf_op jit(solution)/shard_map/ppermute | solution.py:354
  4.0 10.7 %collective-permute-done = f32[4,21,8,128]{3,2,1,0:T(8,128)S(1)} collective-permute-done((f32[4,21,8,128]{3,2,1,0:T(8,128)S(1)}, f32[4,21,8,128]{3,2,1,0:T(8,128)S(1)}, u32[]{:S(2)}, u32[]{:S(2)}) %collective-permute-start) | collective-permute-done | bytes 344096 | tf_op jit(solution)/shard_map/ppermute | solution.py:354
  14.7 0.0 copy-start.1
  14.7 0.0 copy-start.3
  14.7 0.9 %maximum_add_fusion = f32[8,21,8,128]{3,2,1,0:T(8,128)} fusion(f32[8,21,8,128]{3,2,1,0:T(8,128)S(1)} %get-tuple-element.15, f32[4,21,8,128]{3,2,1,0:T(8,128)S(1)} %get-tuple-element.26, f32[4,21,8,128]{3,2,1,0:T(8,128)S(1)} %get-tuple-element.25), kind=kLoop, calls=%fused_computation | loop fusion | flops 344064 | bytes 2064384 | tf_op jit(solution)/shard_map/add | solution.py:372
  15.6 3.7 %all-to-all-start = ((f32[8,21,8,128]{3,2,1,0:T(8,128)}), f32[8,21,8,128]{3,2,1,0:T(8,128)S(1)}, u32[]{:S(2)}, u32[]{:S(2)}) async-start(f32[8,21,8,128]{3,2,1,0:T(8,128)} %maximum_add_fusion), calls=%async_computation | async-start | bytes 1376256 | tf_op jit(solution)/shard_map/all_to_all | solution.py:373
  19.4 3.5 %collective-permute-start.1 = (f32[21,8,128]{2,1,0:T(8,128)S(1)}, f32[21,8,128]{2,1,0:T(8,128)S(1)}, u32[]{:S(2)}, u32[]{:S(2)}) collective-permute-start(f32[21,8,128]{2,1,0:T(8,128)S(1)} %get-tuple-element.17), channel_id=1, source_target_pairs={{0,4},{1,5},{2,6},{3,7},{4,0},{5,1},{6,2},{7,3},{8,12},{9,13},{10,... | collective-permute-start | bytes 258056 | tf_op jit(solution)/shard_map/ppermute | solution.py:354
  22.9 5.9 %collective-permute-start.2 = (f32[21,8,128]{2,1,0:T(8,128)S(1)}, f32[21,8,128]{2,1,0:T(8,128)S(1)}, u32[]{:S(2)}, u32[]{:S(2)}) collective-permute-start(f32[21,8,128]{2,1,0:T(8,128)S(1)} %get-tuple-element.18), channel_id=1, source_target_pairs={{0,64},{1,65},{2,66},{3,67},{4,68},{5,69},{6,70},{7,71},{8,72},{9,... | collective-permute-start | bytes 258056 | tf_op jit(solution)/shard_map/ppermute | solution.py:354
  28.8 4.6 %collective-permute-done.1.half_ref = f32[21,8,128]{2,1,0:T(8,128)S(1)} collective-permute-done((f32[21,8,128]{2,1,0:T(8,128)S(1)}, f32[21,8,128]{2,1,0:T(8,128)S(1)}, u32[]{:S(2)}, u32[]{:S(2)}) %collective-permute-start.1) | collective-permute-done | bytes 86048 | tf_op jit(solution)/shard_map/ppermute | solution.py:354
  33.3 0.0 collective-permute-done.2.far_ref
  33.3 0.0 all-to-all-done.near_ref
  33.3 0.0 copy-done.1
  33.3 0.0 copy-done.3
  33.3 2.8 %unpack.1 = (f32[2560,128]{1,0:T(8,128)S(1)}, f32[2560,128]{1,0:T(8,128)S(1)}, f32[480,128]{1,0:T(8,128)S(1)}, f32[480,128]{1,0:T(8,128)S(1)}, f32[240,128]{1,0:T(8,128)S(1)}, /*index=5*/f32[240,128]{1,0:T(8,128)S(1)}) custom-call(s32[1]{0:T(128)} %bitcast.me_ref, s32[1,128]{1,0:T(1,128)S(1)} %bitcast.7, f32[5,128,512]{2,1,0:T(8,128)S(1)} %bitcast.5, ...), custom_call_target="tpu_custom_call" | custom-call | tf_op jit(solution)/shard_map/unpack/pallas_call | solution.py:187
  36.1 2.5 %collective-permute-start.5 = (f32[480,128]{1,0:T(8,128)S(1)}, f32[480,128]{1,0:T(8,128)S(1)}, u32[]{:S(2)}, u32[]{:S(2)}) collective-permute-start(f32[480,128]{1,0:T(8,128)S(1)} %get-tuple-element.23), channel_id=1, source_target_pairs={{0,8},{8,16},{16,24},{24,32},{32,40},{40,48},{48,56},{56,64},{64,7... | collective-permute-start | bytes 737288 | tf_op jit(solution)/shard_map/ppermute | solution.py:354
  38.7 4.4 %collective-permute-start.6 = (f32[480,128]{1,0:T(8,128)S(1)}, f32[480,128]{1,0:T(8,128)S(1)}, u32[]{:S(2)}, u32[]{:S(2)}) collective-permute-start(f32[480,128]{1,0:T(8,128)S(1)} %get-tuple-element.24), channel_id=1, source_target_pairs={{0,120},{8,0},{16,8},{24,16},{32,24},{40,32},{48,40},{56,48},{64,5... | collective-permute-start | bytes 737288 | tf_op jit(solution)/shard_map/ppermute | solution.py:354
  43.1 0.0 collective-permute-start.3
  43.1 3.0 %collective-permute-start.4 = (f32[240,128]{1,0:T(8,128)S(1)}, f32[240,128]{1,0:T(8,128)S(1)}, u32[]{:S(2)}, u32[]{:S(2)}) collective-permute-start(f32[240,128]{1,0:T(8,128)S(1)} %get-tuple-element.22), channel_id=1, source_target_pairs={{0,7},{1,0},{2,1},{3,2},{4,3},{5,4},{6,5},{7,6},{8,15},{9,8},{10,9... | collective-permute-start | bytes 368648 | tf_op jit(solution)/shard_map/ppermute | solution.py:354
  46.0 6.5 %flux_third.1.before_ref = f32[2560,128]{1,0:T(8,128)S(1)} custom-call(f32[2560,128]{1,0:T(8,128)S(1)} %get-tuple-element.19.state_ref, f32[2560,128]{1,0:T(8,128)S(1)} %get-tuple-element.20.prim_ref), custom_call_target="tpu_custom_call" | custom-call | flops 20000000 | bytes 4000000 | tf_op jit(solution)/shard_map/flux_third/pallas_call | solution.py:341
  52.6 0.0 collective-permute-done.3.low_ref
  52.6 0.0 collective-permute-done.4.high_ref
  52.6 3.7 %flux_second.1.before_ref = f32[2560,128]{1,0:T(8,128)S(1)} custom-call(f32[2560,128]{1,0:T(8,128)S(1)} %flux_third.1.before_ref, f32[2560,128]{1,0:T(8,128)S(1)} %get-tuple-element.20.prim_ref, f32[240,128]{1,0:T(8,128)S(1)} %collective-permute-done.3.low_ref, f32[240,128]{1,0:T(8,128)S(1)} %collective-permute-done.4.high_ref), custom_call_target="tpu_custom_call" | custom-call | flops 20000000 | bytes 4000000 | tf_op jit(solution)/shard_map/flux_second/pallas_call | solution.py:341
  56.4 0.0 collective-permute-done.5.low_ref
  56.4 0.0 collective-permute-done.6.high_ref
  56.4 3.0 %flux_first.1 = f32[2560,128]{1,0:T(8,128)} custom-call(f32[2560,128]{1,0:T(8,128)S(1)} %flux_second.1.before_ref, f32[2560,128]{1,0:T(8,128)S(1)} %get-tuple-element.20.prim_ref, f32[480,128]{1,0:T(8,128)S(1)} %collective-permute-done.5.low_ref, f32[480,128]{1,0:T(8,128)S(1)} %collective-permute-done.6.high_ref), custom_call_target="tpu_custom_call" | custom-call | flops 20000000 | bytes 4000000 | tf_op jit(solution)/shard_map/flux_first/pallas_call | solution.py:341
  (1 shorter events, 0.0 us)
Async XLA Ops:
  0.0 1.3 %copy-start = (f32[128,5,512]{2,0,1:T(8,128)S(1)}, f32[128,5,512]{2,0,1:T(8,128)}, u32[]{:S(2)}) copy-start(f32[128,5,512]{2,0,1:T(8,128)} %param.2) | copy-start | bytes 3932164
  1.3 0.7 %copy-start.2 = (s32[128]{0:T(128)S(1)}, s32[128]{0:T(128)}, u32[]{:S(2)}) copy-start(s32[128]{0:T(128)} %param.3) | copy-start | bytes 1540
  2.7 12.0 %collective-permute-start = (f32[4,21,8,128]{3,2,1,0:T(8,128)S(1)}, f32[4,21,8,128]{3,2,1,0:T(8,128)S(1)}, u32[]{:S(2)}, u32[]{:S(2)}) collective-permute-start(f32[4,21,8,128]{3,2,1,0:T(8,128)S(1)} %get-tuple-element.16), channel_id=1, source_target_pairs={{4,12},{5,13},{6,14},{7,15},{8,0},{9,1},{10,2},{11,3},{12,20},{13,... | collective-permute-start | bytes 1032200 | tf_op jit(solution)/shard_map/ppermute | solution.py:354
  14.7 18.6 %copy-start.1 = (f32[128,5,512]{2,0,1:T(8,128)S(1)}, f32[128,5,512]{2,0,1:T(8,128)}, u32[]{:S(2)}) copy-start(f32[128,5,512]{2,0,1:T(8,128)} %param.2) | copy-start | bytes 3932164
  14.7 18.6 %copy-start.3 = (s32[128]{0:T(128)S(1)}, s32[128]{0:T(128)}, u32[]{:S(2)}) copy-start(s32[128]{0:T(128)} %param.3) | copy-start | bytes 1540
  15.6 17.7 %all-to-all-start = ((f32[8,21,8,128]{3,2,1,0:T(8,128)}), f32[8,21,8,128]{3,2,1,0:T(8,128)S(1)}, u32[]{:S(2)}, u32[]{:S(2)}) async-start(f32[8,21,8,128]{3,2,1,0:T(8,128)} %maximum_add_fusion), calls=%async_computation | async-start | bytes 1376256 | tf_op jit(solution)/shard_map/all_to_all | solution.py:373
  19.4 13.9 %collective-permute-start.1 = (f32[21,8,128]{2,1,0:T(8,128)S(1)}, f32[21,8,128]{2,1,0:T(8,128)S(1)}, u32[]{:S(2)}, u32[]{:S(2)}) collective-permute-start(f32[21,8,128]{2,1,0:T(8,128)S(1)} %get-tuple-element.17), channel_id=1, source_target_pairs={{0,4},{1,5},{2,6},{3,7},{4,0},{5,1},{6,2},{7,3},{8,12},{9,13},{10,... | collective-permute-start | bytes 258056 | tf_op jit(solution)/shard_map/ppermute | solution.py:354
  22.9 10.4 %collective-permute-start.2 = (f32[21,8,128]{2,1,0:T(8,128)S(1)}, f32[21,8,128]{2,1,0:T(8,128)S(1)}, u32[]{:S(2)}, u32[]{:S(2)}) collective-permute-start(f32[21,8,128]{2,1,0:T(8,128)S(1)} %get-tuple-element.18), channel_id=1, source_target_pairs={{0,64},{1,65},{2,66},{3,67},{4,68},{5,69},{6,70},{7,71},{8,72},{9,... | collective-permute-start | bytes 258056 | tf_op jit(solution)/shard_map/ppermute | solution.py:354
  36.1 20.2 %collective-permute-start.5 = (f32[480,128]{1,0:T(8,128)S(1)}, f32[480,128]{1,0:T(8,128)S(1)}, u32[]{:S(2)}, u32[]{:S(2)}) collective-permute-start(f32[480,128]{1,0:T(8,128)S(1)} %get-tuple-element.23), channel_id=1, source_target_pairs={{0,8},{8,16},{16,24},{24,32},{32,40},{40,48},{48,56},{56,64},{64,7... | collective-permute-start | bytes 737288 | tf_op jit(solution)/shard_map/ppermute | solution.py:354
  38.7 17.7 %collective-permute-start.6 = (f32[480,128]{1,0:T(8,128)S(1)}, f32[480,128]{1,0:T(8,128)S(1)}, u32[]{:S(2)}, u32[]{:S(2)}) collective-permute-start(f32[480,128]{1,0:T(8,128)S(1)} %get-tuple-element.24), channel_id=1, source_target_pairs={{0,120},{8,0},{16,8},{24,16},{32,24},{40,32},{48,40},{56,48},{64,5... | collective-permute-start | bytes 737288 | tf_op jit(solution)/shard_map/ppermute | solution.py:354
  43.1 9.5 %collective-permute-start.3 = (f32[240,128]{1,0:T(8,128)S(1)}, f32[240,128]{1,0:T(8,128)S(1)}, u32[]{:S(2)}, u32[]{:S(2)}) collective-permute-start(f32[240,128]{1,0:T(8,128)S(1)} %get-tuple-element.21), channel_id=1, source_target_pairs={{0,1},{1,2},{2,3},{3,4},{4,5},{5,6},{6,7},{7,0},{8,9},{9,10},{10,1... | collective-permute-start | bytes 368648 | tf_op jit(solution)/shard_map/ppermute | solution.py:354
  43.1 9.5 %collective-permute-start.4 = (f32[240,128]{1,0:T(8,128)S(1)}, f32[240,128]{1,0:T(8,128)S(1)}, u32[]{:S(2)}, u32[]{:S(2)}) collective-permute-start(f32[240,128]{1,0:T(8,128)S(1)} %get-tuple-element.22), channel_id=1, source_target_pairs={{0,7},{1,0},{2,1},{3,2},{4,3},{5,4},{6,5},{7,6},{8,15},{9,8},{10,9... | collective-permute-start | bytes 368648 | tf_op jit(solution)/shard_map/ppermute | solution.py:354
where the time goes:
time: 59.9 us; the launch traced here: 59.3 us
  starting transfers between devices  24.3 us (41%)
  Pallas kernels  16.8 us (28%)
  waiting for transfers between devices  15.2 us (25%)
  local copies, waits for them, and re-layouts  1.98 us (3%)
  other arithmetic  0.97 us (2%)
    ppermute x7, starting transfers between devices, shifted(): lax.ppermute(value, axes, [pair for pair in pairs if 0 <= pair[1] < count])  20.6 us
    ppermute x7, waiting for transfers between devices, shifted(): lax.ppermute(value, axes, [pair for pair in pairs if 0 <= pair[1] < count])  15.2 us
    pallas_call x3, Pallas kernels, stage(): pl.pallas_call(kernel, out_shape=jax.ShapeDtypeStruct((ROWS, CZ), jnp.flo...  13.2 us
    all_to_all x1, starting transfers between devices, body(): near = lax.all_to_all(near, 'dev', split_axis=0, concat_axis=0, tiled=True)  3.73 us
    pallas_call x1, Pallas kernels, unpack(): pl.pallas_call(unpack_kernel, out_shape=(grid_rows, grid_rows, x_side, x_...  2.8 us
    unnamed x8, local copies, waits for them, and re-layouts  1.98 us
  transfers between devices with their start and end apart: 8, of which 2 were waited for; matrix products, arithmetic and copies ran while one was open for 0% of the time, Pallas kernels for 17%

commit v1 on v0

--- a/solution.py
+++ b/solution.py
@@ -18,10 +18,11 @@
 ROWS = FIELDS * CX * CY
 VMEM_LIMIT = 48 * 1024 * 1024
 
-ROW_HALF = 64
-ROW_FAR = 72
-ROW_RELAY = 80
-ROW_END = 112
+EARLY_FAR = 3 * MOVE
+EARLY_RELAY = 4 * MOVE
+EARLY_ROWS = 8 * MOVE
+LATE_ROWS = 4 * MOVE
+ARRIVED = 9 * MOVE
 
 AXES = ("node", "dev")
 
@@ -46,59 +47,97 @@
     return total
 
 
-def pack_kernel(me_ref, pos_ref, old_ref, near_ref, half_ref, far_ref, relay_ref):
-    me = me_ref[0]
-    node, dev = me // 8, me % 8
-    pos = pos_ref[...]
+def place():
+    return lax.axis_index("node"), lax.axis_index("dev")
+
+
+def targets(pos):
     square = (TILES, TILES)
     by_lane = jnp.broadcast_to(pos // TILES, square)
     by_row = by_lane.T
     earlier = (by_lane == by_row) & (iota(square, 0) < iota(square, 1))
     rank = jnp.sum(earlier.astype(jnp.int32), axis=0, keepdims=True)
-    owner = pos // TILES
-    local = pos % TILES
-    owner_node, owner_dev = owner // 8, owner % 8
-    inside = jnp.where(jnp.abs(owner_dev - dev) == 4, ROW_HALF, owner_dev * MOVE)
-    outside = jnp.where(owner_node == node ^ 8, ROW_FAR, ROW_RELAY + (owner_dev % 4) * MOVE)
-    base = jnp.where(owner_node == node, inside, outside)
-    target = jnp.where(owner == me, -1, base + rank)
-    shape = (ROW_END, TILES)
+    return pos // TILES, pos % TILES, rank
+
+
+def packed(target, local, rows, old_ref, put):
+    shape = (rows, TILES)
     chosen = iota(shape, 0) == jnp.broadcast_to(target, shape)
     code = jnp.sum(
         jnp.where(chosen, jnp.broadcast_to(local + 1, shape), 0).astype(jnp.float32), axis=1, keepdims=True
     )
-    code = jnp.broadcast_to(code, shape)
+    put(PLANES - 1, jnp.broadcast_to(code, shape))
     choice = chosen.astype(jnp.float32).astype(jnp.bfloat16)
+    for field in range(FIELDS):
+        values = pick(choice, old_ref[field])
+        for part in range(PARTS):
+            put(field * PARTS + part, values[:, part * CZ : (part + 1) * CZ])
+
+
+def pack_early_kernel(pos_ref, old_ref, one_ref, two_ref, three_ref, far_ref, relay_ref):
+    node, dev = place()
+    owner, local, rank = targets(pos_ref[...])
+    mask = (owner % 8) ^ dev
+    inside = jnp.where((mask >= 1) & (mask < 4), (mask - 1) * MOVE + rank, -1)
+    outside = jnp.where(owner // 8 == node ^ 8, EARLY_FAR, EARLY_RELAY + (mask - 4) * MOVE) + rank
+    target = jnp.where(owner // 8 == node, inside, outside)
 
     def put(plane, value):
-        for block in range(8):
-            near_ref[block, plane] = value[block * MOVE : (block + 1) * MOVE]
-        half_ref[plane] = value[ROW_HALF:ROW_FAR]
-        far_ref[plane] = value[ROW_FAR:ROW_RELAY]
+        for block, ref in enumerate((one_ref, two_ref, three_ref, far_ref)):
+            ref[plane] = value[block * MOVE : (block + 1) * MOVE]
         for block in range(4):
-            first = ROW_RELAY + block * MOVE
+            first = EARLY_RELAY + block * MOVE
             relay_ref[block, plane] = value[first : first + MOVE]
 
-    put(PLANES - 1, code)
-    for field in range(FIELDS):
-        rows = pick(choice, old_ref[field])
-        for part in range(PARTS):
-            put(field * PARTS + part, rows[:, part * CZ : (part + 1) * CZ])
-
-
-def pack(me, pos, old):
-    buffer = jax.ShapeDtypeStruct((PLANES, MOVE, CZ), jnp.float32)
-    near = jax.ShapeDtypeStruct((8,) + buffer.shape, jnp.float32)
-    relay = jax.ShapeDtypeStruct((4,) + buffer.shape, jnp.float32)
-    vmem = pl.BlockSpec(memory_space=pltpu.VMEM)
+    packed(target, local, EARLY_ROWS, old_ref, put)
+
+
+def pack_late_kernel(
+    pos_ref, old_ref, relay_ref, one_ref, two_ref, three_ref, far_ref, four_ref, five_ref, six_ref, seven_ref
+):
+    node, dev = place()
+    owner, local, rank = targets(pos_ref[...])
+    mask = (owner % 8) ^ dev
+    target = jnp.where((owner // 8 == node) & (mask >= 4), (mask - 4) * MOVE + rank, -1)
+
+    def put(plane, value):
+        four_ref[0, plane] = value[:MOVE]
+        four_ref[1, plane] = relay_ref[0, plane]
+        for block, ref in enumerate((five_ref, six_ref, seven_ref), 1):
+            ref[plane] = value[block * MOVE : (block + 1) * MOVE] + relay_ref[block, plane]
+
+    packed(target, local, LATE_ROWS, old_ref, put)
+
+
+VMEM = pl.BlockSpec(memory_space=pltpu.VMEM)
+ANYWHERE = pl.BlockSpec(memory_space=pl.ANY)
+BUFFER = jax.ShapeDtypeStruct((PLANES, MOVE, CZ), jnp.float32)
+
+
+def buffers(count):
+    return jax.ShapeDtypeStruct((count,) + BUFFER.shape, jnp.float32)
+
+
+def call(kernel, name, out_shape, in_specs, **more):
     return pl.pallas_call(
-        pack_kernel,
-        out_shape=(near, buffer, buffer, relay),
-        in_specs=[pl.BlockSpec(memory_space=pltpu.SMEM), vmem, vmem],
-        out_specs=(vmem, vmem, vmem, vmem),
+        kernel,
+        out_shape=out_shape,
+        in_specs=in_specs,
+        out_specs=jax.tree.map(lambda _: VMEM, out_shape),
         compiler_params=pltpu.CompilerParams(vmem_limit_bytes=VMEM_LIMIT),
-        name="pack",
-    )(me, pos, old)
+        name=name,
+        **more,
+    )
+
+
+def pack_early(pos, old):
+    return call(pack_early_kernel, "pack_early", (BUFFER,) * 4 + (buffers(4),), [VMEM, VMEM])(pos, old)
+
+
+def pack_late(pos, old, relay, *before):
+    return call(
+        pack_late_kernel, "pack_late", (buffers(2),) + (BUFFER,) * 3, [VMEM] * 3 + [ANYWHERE] * 4
+    )(pos, old, relay, *before)
 
 
 def grains(first, second, half_low, row_pick, lane_picks):
@@ -113,25 +152,24 @@
 
 
 def unpack_kernel(
-    me_ref, pos_ref, old_ref, near_ref, half_ref, far_ref,
-    state_ref, prim_ref, x_low_ref, x_high_ref, y_low_ref, y_high_ref, tiles_ref,
+    pos_ref, old_ref, one_ref, two_ref, three_ref, far_ref, four_ref, five_ref, six_ref, seven_ref,
+    state_ref, prim_ref, x_first_ref, x_second_ref, y_first_ref, y_second_ref, tiles_ref,
 ):
-    me = me_ref[0]
+    node, dev = place()
     pos = pos_ref[...]
     square = (TILES, TILES)
-    kept = jnp.where(pos // TILES == me, pos % TILES, -1)
+    kept = jnp.where(pos // TILES == node * 8 + dev, pos % TILES, -1)
     kept_choice = jnp.broadcast_to(kept, square) == iota(square, 0)
 
     def arrived(plane):
-        return jnp.concatenate(
-            [near_ref[block, plane] for block in range(8)] + [half_ref[plane], far_ref[plane]], axis=0
-        )
-
-    code = jnp.concatenate([arrived(PLANES - 1), jnp.zeros((48, CZ), jnp.float32)], axis=0)
+        refs = (one_ref, two_ref, three_ref, far_ref, five_ref, six_ref, seven_ref)
+        return jnp.concatenate([ref[plane] for ref in refs] + [four_ref[0, plane], four_ref[1, plane]], axis=0)
+
+    code = jnp.concatenate([arrived(PLANES - 1), jnp.zeros((TILES - ARRIVED, CZ), jnp.float32)], axis=0)
     code = code.T.astype(jnp.int32)
     new_choice = code == iota(square, 0) + 1
     choice = jnp.concatenate([kept_choice, new_choice], axis=1).astype(jnp.float32).astype(jnp.bfloat16)
-    blank = jnp.zeros((48, CELLS), jnp.float32)
+    blank = jnp.zeros((TILES - ARRIVED, CELLS), jnp.float32)
     for field in range(FIELDS):
         moved = jnp.concatenate([arrived(field * PARTS + part) for part in range(PARTS)], axis=1)
         tiles_ref[field] = pick(choice, jnp.concatenate([old_ref[field], moved, blank], axis=0))
@@ -168,31 +206,34 @@
         return carry
 
     lax.fori_loop(0, 8, brick, 0)
-    for field in range(FIELDS):
-        x_low_ref[pl.ds(field * 96, 96), :] = prim_ref[pl.ds(field * CX * CY, 96), :]
-        x_high_ref[pl.ds(field * 96, 96), :] = prim_ref[pl.ds((field * CX + 13) * CY, 96), :]
-        for layer in range(3):
-            for block in range(2):
-                start = (field * CX + block * 8) * CY
-                rows = pl.ds((field * 3 + layer) * CX + block * 8, 8)
-                y_low_ref[rows, :] = prim_ref[pl.ds(start + layer, 8, stride=CY), :]
-                y_high_ref[rows, :] = prim_ref[pl.ds(start + CY - 3 + layer, 8, stride=CY), :]
-
-
-def unpack(me, pos, old, near, half, far):
-    vmem = pl.BlockSpec(memory_space=pltpu.VMEM)
+    x_odd, y_odd = node % 2 == 1, dev % 2 == 1
+    x_last, y_last = (CX - 3) * CY, CY - 3
+    for odd_x, odd_y, x_ref, y_ref in (
+        (x_odd, y_odd, x_first_ref, y_first_ref),
+        (~x_odd, ~y_odd, x_second_ref, y_second_ref),
+    ):
+        x_start = pl.multiple_of(jnp.where(odd_x, 0, x_last), TILE)
+        y_start = jnp.where(odd_y, 0, y_last)
+        for field in range(FIELDS):
+            x_ref[pl.ds(field * 96, 96), :] = prim_ref[pl.ds(field * CX * CY + x_start, 96), :]
+            for layer in range(3):
+                for block in range(2):
+                    start = (field * CX + block * 8) * CY + layer
+                    rows = pl.ds((field * 3 + layer) * CX + block * 8, 8)
+                    y_ref[rows, :] = prim_ref[pl.ds(start + y_start, 8, stride=CY), :]
+
+
+def unpack(*operands):
     grid_rows = jax.ShapeDtypeStruct((ROWS, CZ), jnp.float32)
     x_side = jax.ShapeDtypeStruct((FIELDS * 3 * CY, CZ), jnp.float32)
     y_side = jax.ShapeDtypeStruct((FIELDS * 3 * CX, CZ), jnp.float32)
-    return pl.pallas_call(
+    return call(
         unpack_kernel,
-        out_shape=(grid_rows, grid_rows, x_side, x_side, y_side, y_side),
-        in_specs=[pl.BlockSpec(memory_space=pltpu.SMEM)] + [vmem] * 5,
-        out_specs=(vmem,) * 6,
+        "unpack",
+        (grid_rows, grid_rows, x_side, x_side, y_side, y_side),
+        [VMEM] * len(operands),
         scratch_shapes=[pltpu.VMEM((FIELDS, TILES, CELLS), jnp.float32)],
-        compiler_params=pltpu.CompilerParams(vmem_limit_bytes=VMEM_LIMIT),
-        name="unpack",
-    )(me, pos, old, near, half, far)
+    )(*operands)
 
 
 def median_zero(first_value, second_value):
@@ -292,14 +333,20 @@
     lax.fori_loop(0, CX, step, 0)
 
 
-def y_kernel(before_ref, prim_ref, low_ref, high_ref, out_ref):
+def side(first_ref, second_ref, odd, before, rows):
+    first, second = first_ref[rows, :], second_ref[rows, :]
+    return jnp.where(odd, first, second) if before else jnp.where(odd, second, first)
+
+
+def y_kernel(before_ref, prim_ref, first_ref, second_ref, out_ref):
+    odd = lax.axis_index("dev") % 2 == 1
+
     def step(block, carry):
         def load(cell):
             if cell < 0 or cell >= CY:
-                ref, layer = (low_ref, cell + 3) if cell < 0 else (high_ref, cell - CY)
-                return [
-                    ref[pl.ds(pl.multiple_of((f * 3 + layer) * CX + block * 8, 8), 8), :] for f in range(FIELDS)
-                ]
+                layer = cell + 3 if cell < 0 else cell - CY
+                rows = [pl.ds(pl.multiple_of((f * 3 + layer) * CX + block * 8, 8), 8) for f in range(FIELDS)]
+                return [side(first_ref, second_ref, odd, cell < 0, row) for row in rows]
             return [prim_ref[pl.ds((f * CX + block * 8) * CY + cell, 8, stride=CY), :] for f in range(FIELDS)]
 
         def emit(cell, change):
@@ -313,14 +360,15 @@
     lax.fori_loop(0, CX // 8, step, 0)
 
 
-def x_kernel(before_ref, prim_ref, low_ref, high_ref, out_ref):
+def x_kernel(before_ref, prim_ref, first_ref, second_ref, out_ref):
+    odd = lax.axis_index("node") % 2 == 1
+
     def step(block, carry):
         def load(cell):
             if cell < 0 or cell >= CX:
-                ref, layer = (low_ref, cell + 3) if cell < 0 else (high_ref, cell - CX)
-                return [
-                    ref[pl.ds(pl.multiple_of((f * 3 + layer) * CY + block * 8, 8), 8), :] for f in range(FIELDS)
-                ]
+                layer = cell + 3 if cell < 0 else cell - CX
+                rows = [pl.ds(pl.multiple_of((f * 3 + layer) * CY + block * 8, 8), 8) for f in range(FIELDS)]
+                return [side(first_ref, second_ref, odd, cell < 0, row) for row in rows]
             return [
                 prim_ref[pl.ds(pl.multiple_of((f * CX + cell) * CY + block * 8, 8), 8), :] for f in range(FIELDS)
             ]
@@ -337,15 +385,12 @@
 
 
 def stage(kernel, name, *operands):
-    vmem = pl.BlockSpec(memory_space=pltpu.VMEM)
-    return pl.pallas_call(
+    return call(
         kernel,
-        out_shape=jax.ShapeDtypeStruct((ROWS, CZ), jnp.float32),
-        in_specs=[vmem] * len(operands),
-        out_specs=vmem,
-        compiler_params=pltpu.CompilerParams(vmem_limit_bytes=VMEM_LIMIT),
+        name,
+        jax.ShapeDtypeStruct((ROWS, CZ), jnp.float32),
+        [VMEM] * len(operands),
         cost_estimate=pl.CostEstimate(flops=20_000_000, bytes_accessed=4_000_000, transcendentals=200_000),
-        name=name,
     )(*operands)
 
 
@@ -359,26 +404,26 @@
     return (node + (1 if dev >= 4 else -1)) * 8 + dev
 
 
+def masked(value, mask):
+    return shifted(value, AXES, 128, lambda device: device ^ mask)
+
+
 def body(old_state, old_tile_pos):
-    dev = lax.axis_index("dev")
-    me = (lax.axis_index("node") * 8 + dev).astype(jnp.int32).reshape(1)
     pos = old_tile_pos.reshape(1, TILES)
     old = old_state.transpose(1, 0, 2)
-    near, half, far, relay = pack(me, pos, old)
+    one, two, three, far, relay = pack_early(pos, old)
     relay = shifted(relay, AXES, 128, next_node)
-    half = shifted(half, AXES, 128, lambda device: device ^ 4)
-    far = shifted(far, AXES, 128, lambda device: device ^ 64)
-    blank = jnp.zeros_like(relay)
-    near = near + jnp.concatenate([jnp.where(dev >= 4, relay, blank), jnp.where(dev < 4, relay, blank)], axis=0)
-    near = lax.all_to_all(near, "dev", split_axis=0, concat_axis=0, tiled=True)
-    state, prim, x_low, x_high, y_low, y_high = unpack(me, pos, old, near, half, far)
-    y_before = shifted(y_high, "dev", 8, lambda i: (i + 1) % 8)
-    y_after = shifted(y_low, "dev", 8, lambda i: (i - 1) % 8)
-    x_before = shifted(x_high, "node", 16, lambda i: (i + 1) % 16)
-    x_after = shifted(x_low, "node", 16, lambda i: (i - 1) % 16)
+    early = (masked(one, 1), masked(two, 2), masked(three, 3), masked(far, 64))
+    late = pack_late(pos, old, relay, *early)
+    late = [masked(value, 4 + index) for index, value in enumerate(late)]
+    state, prim, x_first, x_second, y_first, y_second = unpack(pos, old, *early, *late)
+    x_first = shifted(x_first, "node", 16, lambda i: i ^ 1)
+    x_second = shifted(x_second, "node", 16, lambda i: (i + 1) % 16 if i % 2 else (i - 1) % 16)
+    y_first = shifted(y_first, "dev", 8, lambda i: i ^ 1)
+    y_second = shifted(y_second, "dev", 8, lambda i: (i + 1) % 8 if i % 2 else (i - 1) % 8)
     result = stage(z_kernel, "flux_third", state, prim)
-    result = stage(y_kernel, "flux_second", result, prim, y_before, y_after)
-    result = stage(x_kernel, "flux_first", result, prim, x_before, x_after)
+    result = stage(y_kernel, "flux_second", result, prim, y_first, y_second)
+    result = stage(x_kernel, "flux_first", result, prim, x_first, x_second)
     return result.reshape(FIELDS, CX, CY, CZ)
 
 

time: 59.9 us -> 54.3 us (0.907)
  waiting for transfers between devices: 15.2 us -> 9.93 us
  other arithmetic: 0.97 us -> 0 us
    ppermute x7 -> x13, waiting for transfers between devices: 15.2 us -> 9.93 us  [shifted(): lax.ppermute(value, axes, [pair for pair in pairs if 0 <= pair[1] < count])]
    ppermute x7 -> x13, starting transfers between devices: 20.6 us -> 24.7 us  [shifted(): lax.ppermute(value, axes, [pair for pair in pairs if 0 <= pair[1] < count])]
    all_to_all x1 -> x0, starting transfers between devices: 3.73 us -> none  [body(): near = lax.all_to_all(near, 'dev', split_axis=0, concat_axis=0, tiled=True)]
    add x1 -> x0, other arithmetic: 0.92 us -> none  [body(): near + jnp.concatenate([jnp.where(dev >= 4, relay, blank), jnp.where(dev...]
    pallas_call x5 -> x6, Pallas kernels: 16.8 us -> 17.3 us  [the longest x3 13.4 us: stage(): call(kernel, name, jax.ShapeDtypeStruct((ROWS, CZ), jnp.float32), [VMEM]...]
    unnamed x8 -> x4, local copies, waits for them, and re-layouts: 1.98 us -> 1.97 us
  transfers between devices with their start and end apart: 8 -> 13, of which waited for: 2 -> 4; matrix products, arithmetic and copies ran while one was open for 0% -> 0% of each run, Pallas kernels for 17% -> 19%
where the time goes in v1:
time: 54.3 us; the launch traced here: 54 us
  starting transfers between devices  24.7 us (45%)
  Pallas kernels  17.3 us (32%)
  waiting for transfers between devices  9.93 us (18%)
  local copies, waits for them, and re-layouts  1.97 us (4%)
    ppermute x13, starting transfers between devices, shifted(): lax.ppermute(value, axes, [pair for pair in pairs if 0 <= pair[1] < count])  24.7 us
    pallas_call x3, Pallas kernels, stage(): call(kernel, name, jax.ShapeDtypeStruct((ROWS, CZ), jnp.float32), [VMEM]...  13.4 us
    ppermute x13, waiting for transfers between devices, shifted(): lax.ppermute(value, axes, [pair for pair in pairs if 0 <= pair[1] < count])  9.93 us
    pallas_call x1, Pallas kernels, unpack(): call(unpack_kernel, 'unpack', (grid_rows, grid_rows, x_side, x_side, y_si...  2.83 us
    unnamed x4, local copies, waits for them, and re-layouts  1.97 us
  transfers between devices with their start and end apart: 13, of which 4 were waited for; matrix products, arithmetic and copies ran while one was open for 0% of the time, Pallas kernels for 19%

profile of v1, /device:TPU:0, one launch (start us, length us, event | category | flops | bytes accessed | tf_op | source)
XLA Modules:
  0.0 54.0 jit_solution(12660789955195824574)
XLA Ops:
  0.0 1.3 %copy-done = f32[128,5,512]{2,0,1:T(8,128)S(1)} copy-done((f32[128,5,512]{2,0,1:T(8,128)S(1)}, f32[128,5,512]{2,0,1:T(8,128)}, u32[]{:S(2)}) %copy-start) | copy-done | bytes 1310744
  1.3 0.7 %copy-done.1 = s32[128]{0:T(128)S(1)} copy-done((s32[128]{0:T(128)S(1)}, s32[128]{0:T(128)}, u32[]{:S(2)}) %copy-start.1) | copy-done | bytes 536
  2.0 0.5 %pack_early.1 = (f32[21,8,128]{2,1,0:T(8,128)S(1)}, f32[21,8,128]{2,1,0:T(8,128)S(1)}, f32[21,8,128]{2,1,0:T(8,128)S(1)}, f32[21,8,128]{2,1,0:T(8,128)S(1)}, f32[4,21,8,128]{3,2,1,0:T(8,128)S(1)}) custom-call(s32[1,128]{1,0:T(1,128)S(1)} %bitcast.6, f32[5,128,512]{2,1,0:T(8,128)S(1)} %bitcast.3), custom_call_target="tpu_custom_call" | custom-call | tf_op jit(solution)/shard_map/pack_early/pallas_call | solution.py:134
  2.5 1.3 %collective-permute-start.4 = (f32[4,21,8,128]{3,2,1,0:T(8,128)S(1)}, f32[4,21,8,128]{3,2,1,0:T(8,128)S(1)}, u32[]{:S(2)}, u32[]{:S(2)}) collective-permute-start(f32[4,21,8,128]{3,2,1,0:T(8,128)S(1)} %get-tuple-element.24), channel_id=1, source_target_pairs={{4,12},{5,13},{6,14},{7,15},{8,0},{9,1},{10,2},{11,3},{12,20},{13,... | collective-permute-start | bytes 1032200 | tf_op jit(solution)/shard_map/ppermute | solution.py:399
  3.8 0.1 collective-permute-start
  3.9 1.7 %collective-permute-start.1 = (f32[21,8,128]{2,1,0:T(8,128)S(1)}, f32[21,8,128]{2,1,0:T(8,128)S(1)}, u32[]{:S(2)}, u32[]{:S(2)}) collective-permute-start(f32[21,8,128]{2,1,0:T(8,128)S(1)} %get-tuple-element.21), channel_id=1, source_target_pairs={{0,2},{1,3},{2,0},{3,1},{4,6},{5,7},{6,4},{7,5},{8,10},{9,11},{10,... | collective-permute-start | bytes 258056 | tf_op jit(solution)/shard_map/ppermute | solution.py:399
  5.7 0.1 collective-permute-start.2
  5.8 7.7 %collective-permute-start.3 = (f32[21,8,128]{2,1,0:T(8,128)S(1)}, f32[21,8,128]{2,1,0:T(8,128)S(1)}, u32[]{:S(2)}, u32[]{:S(2)}) collective-permute-start(f32[21,8,128]{2,1,0:T(8,128)S(1)} %get-tuple-element.23), channel_id=1, source_target_pairs={{0,64},{1,65},{2,66},{3,67},{4,68},{5,69},{6,70},{7,71},{8,72},{9,... | collective-permute-start | bytes 258056 | tf_op jit(solution)/shard_map/ppermute | solution.py:399
  13.5 0.0 collective-permute-done.one_ref
  13.5 0.0 collective-permute-done.1.two_ref
  13.5 0.0 collective-permute-done.2.three_ref
  13.5 3.0 %collective-permute-done.3.far_ref = f32[21,8,128]{2,1,0:T(8,128)S(1)} collective-permute-done((f32[21,8,128]{2,1,0:T(8,128)S(1)}, f32[21,8,128]{2,1,0:T(8,128)S(1)}, u32[]{:S(2)}, u32[]{:S(2)}) %collective-permute-start.3) | collective-permute-done | bytes 86048 | tf_op jit(solution)/shard_map/ppermute | solution.py:399
  16.6 0.0 collective-permute-done.4.relay_ref
  16.6 0.5 pack_late.1
  17.1 1.4 %collective-permute-start.5 = (f32[2,21,8,128]{3,2,1,0:T(8,128)S(1)}, f32[2,21,8,128]{3,2,1,0:T(8,128)S(1)}, u32[]{:S(2)}, u32[]{:S(2)}) collective-permute-start(f32[2,21,8,128]{3,2,1,0:T(8,128)S(1)} %get-tuple-element.25), channel_id=1, source_target_pairs={{0,4},{1,5},{2,6},{3,7},{4,0},{5,1},{6,2},{7,3},{8,12},{9,13},{10,... | collective-permute-start | bytes 516104 | tf_op jit(solution)/shard_map/ppermute | solution.py:399
  18.5 1.3 %collective-permute-start.6 = (f32[21,8,128]{2,1,0:T(8,128)S(1)}, f32[21,8,128]{2,1,0:T(8,128)S(1)}, u32[]{:S(2)}, u32[]{:S(2)}) collective-permute-start(f32[21,8,128]{2,1,0:T(8,128)S(1)} %get-tuple-element.26), channel_id=1, source_target_pairs={{0,5},{1,4},{2,7},{3,6},{4,1},{5,0},{6,3},{7,2},{8,13},{9,12},{10,... | collective-permute-start | bytes 258056 | tf_op jit(solution)/shard_map/ppermute | solution.py:399
  19.8 1.6 %collective-permute-start.7 = (f32[21,8,128]{2,1,0:T(8,128)S(1)}, f32[21,8,128]{2,1,0:T(8,128)S(1)}, u32[]{:S(2)}, u32[]{:S(2)}) collective-permute-start(f32[21,8,128]{2,1,0:T(8,128)S(1)} %get-tuple-element.27), channel_id=1, source_target_pairs={{0,6},{1,7},{2,4},{3,5},{4,2},{5,3},{6,0},{7,1},{8,14},{9,15},{10,... | collective-permute-start | bytes 258056 | tf_op jit(solution)/shard_map/ppermute | solution.py:399
  21.4 2.0 %collective-permute-start.8 = (f32[21,8,128]{2,1,0:T(8,128)S(1)}, f32[21,8,128]{2,1,0:T(8,128)S(1)}, u32[]{:S(2)}, u32[]{:S(2)}) collective-permute-start(f32[21,8,128]{2,1,0:T(8,128)S(1)} %get-tuple-element.28), channel_id=1, source_target_pairs={{0,7},{1,6},{2,5},{3,4},{4,3},{5,2},{6,1},{7,0},{8,15},{9,14},{10,... | collective-permute-start | bytes 258056 | tf_op jit(solution)/shard_map/ppermute | solution.py:399
  23.3 2.1 %collective-permute-done.6.five_ref = f32[21,8,128]{2,1,0:T(8,128)S(1)} collective-permute-done((f32[21,8,128]{2,1,0:T(8,128)S(1)}, f32[21,8,128]{2,1,0:T(8,128)S(1)}, u32[]{:S(2)}, u32[]{:S(2)}) %collective-permute-start.6) | collective-permute-done | bytes 86048 | tf_op jit(solution)/shard_map/ppermute | solution.py:399
  25.4 3.0 %collective-permute-done.7.six_ref = f32[21,8,128]{2,1,0:T(8,128)S(1)} collective-permute-done((f32[21,8,128]{2,1,0:T(8,128)S(1)}, f32[21,8,128]{2,1,0:T(8,128)S(1)}, u32[]{:S(2)}, u32[]{:S(2)}) %collective-permute-start.7) | collective-permute-done | bytes 86048 | tf_op jit(solution)/shard_map/ppermute | solution.py:399
  28.4 1.8 %collective-permute-done.8.seven_ref = f32[21,8,128]{2,1,0:T(8,128)S(1)} collective-permute-done((f32[21,8,128]{2,1,0:T(8,128)S(1)}, f32[21,8,128]{2,1,0:T(8,128)S(1)}, u32[]{:S(2)}, u32[]{:S(2)}) %collective-permute-start.8) | collective-permute-done | bytes 86048 | tf_op jit(solution)/shard_map/ppermute | solution.py:399
  30.2 0.0 collective-permute-done.5.four_ref
  30.2 2.8 %unpack.1 = (f32[2560,128]{1,0:T(8,128)S(1)}, f32[2560,128]{1,0:T(8,128)S(1)}, f32[480,128]{1,0:T(8,128)S(1)}, f32[480,128]{1,0:T(8,128)S(1)}, f32[240,128]{1,0:T(8,128)S(1)}, /*index=5*/f32[240,128]{1,0:T(8,128)S(1)}) custom-call(s32[1,128]{1,0:T(1,128)S(1)} %bitcast.8, f32[5,128,512]{2,1,0:T(8,128)S(1)} %bitcast.5, ...), custom_call_target="tpu_custom_call" | custom-call | tf_op jit(solution)/shard_map/unpack/pallas_call | solution.py:230
  33.1 0.1 collective-permute-start.11
  33.2 4.1 %collective-permute-start.12 = (f32[480,128]{1,0:T(8,128)S(1)}, f32[480,128]{1,0:T(8,128)S(1)}, u32[]{:S(2)}, u32[]{:S(2)}) collective-permute-start(f32[480,128]{1,0:T(8,128)S(1)} %get-tuple-element.34), channel_id=1, source_target_pairs={{0,120},{8,16},{16,8},{24,32},{32,24},{40,48},{48,40},{56,64},{64,... | collective-permute-start | bytes 737288 | tf_op jit(solution)/shard_map/ppermute | solution.py:399
  37.3 0.0 collective-permute-start.9
  37.3 3.2 %collective-permute-start.10 = (f32[240,128]{1,0:T(8,128)S(1)}, f32[240,128]{1,0:T(8,128)S(1)}, u32[]{:S(2)}, u32[]{:S(2)}) collective-permute-start(f32[240,128]{1,0:T(8,128)S(1)} %get-tuple-element.32), channel_id=1, source_target_pairs={{0,7},{1,2},{2,1},{3,4},{4,3},{5,6},{6,5},{7,0},{8,15},{9,10},{10,... | collective-permute-start | bytes 368648 | tf_op jit(solution)/shard_map/ppermute | solution.py:399
  40.5 6.5 %flux_third.1.before_ref = f32[2560,128]{1,0:T(8,128)S(1)} custom-call(f32[2560,128]{1,0:T(8,128)S(1)} %get-tuple-element.29.state_ref, f32[2560,128]{1,0:T(8,128)S(1)} %get-tuple-element.30.prim_ref), custom_call_target="tpu_custom_call" | custom-call | flops 20000000 | bytes 4000000 | tf_op jit(solution)/shard_map/flux_third/pallas_call | solution.py:388
  47.1 0.0 collective-permute-done.10.second_ref
  47.1 3.8 %flux_second.1.before_ref = f32[2560,128]{1,0:T(8,128)S(1)} custom-call(f32[2560,128]{1,0:T(8,128)S(1)} %flux_third.1.before_ref, f32[2560,128]{1,0:T(8,128)S(1)} %get-tuple-element.30.prim_ref, f32[240,128]{1,0:T(8,128)S(1)} %collective-permute-done.9.first_ref, f32[240,128]{1,0:T(8,128)S(1)} %collective-permute-done.10.second_ref), custom_call_target="tpu_custom_call" | custom-call | flops 20000000 | bytes 4000000 | tf_op jit(solution)/shard_map/flux_second/pallas_call | solution.py:388
  50.9 0.0 collective-permute-done.11.first_ref
  50.9 3.0 %flux_first.1 = f32[2560,128]{1,0:T(8,128)} custom-call(f32[2560,128]{1,0:T(8,128)S(1)} %flux_second.1.before_ref, f32[2560,128]{1,0:T(8,128)S(1)} %get-tuple-element.30.prim_ref, f32[480,128]{1,0:T(8,128)S(1)} %collective-permute-done.11.first_ref, f32[480,128]{1,0:T(8,128)S(1)} %collective-permute-done.12.second_ref), custom_call_target="tpu_custom_call" | custom-call | flops 20000000 | bytes 4000000 | tf_op jit(solution)/shard_map/flux_first/pallas_call | solution.py:388
  (4 shorter events, 0.0 us)
Async XLA Ops:
  0.0 1.3 %copy-start = (f32[128,5,512]{2,0,1:T(8,128)S(1)}, f32[128,5,512]{2,0,1:T(8,128)}, u32[]{:S(2)}) copy-start(f32[128,5,512]{2,0,1:T(8,128)} %param.2) | copy-start | bytes 3932164
  1.3 0.7 %copy-start.1 = (s32[128]{0:T(128)S(1)}, s32[128]{0:T(128)}, u32[]{:S(2)}) copy-start(s32[128]{0:T(128)} %param.3) | copy-start | bytes 1540
  2.5 14.0 %collective-permute-start.4 = (f32[4,21,8,128]{3,2,1,0:T(8,128)S(1)}, f32[4,21,8,128]{3,2,1,0:T(8,128)S(1)}, u32[]{:S(2)}, u32[]{:S(2)}) collective-permute-start(f32[4,21,8,128]{3,2,1,0:T(8,128)S(1)} %get-tuple-element.24), channel_id=1, source_target_pairs={{4,12},{5,13},{6,14},{7,15},{8,0},{9,1},{10,2},{11,3},{12,20},{13,... | collective-permute-start | bytes 1032200 | tf_op jit(solution)/shard_map/ppermute | solution.py:399
  3.8 9.7 %collective-permute-start = (f32[21,8,128]{2,1,0:T(8,128)S(1)}, f32[21,8,128]{2,1,0:T(8,128)S(1)}, u32[]{:S(2)}, u32[]{:S(2)}) collective-permute-start(f32[21,8,128]{2,1,0:T(8,128)S(1)} %get-tuple-element.20), channel_id=1, source_target_pairs={{0,1},{1,0},{2,3},{3,2},{4,5},{5,4},{6,7},{7,6},{8,9},{9,8},{10,11... | collective-permute-start | bytes 258056 | tf_op jit(solution)/shard_map/ppermute | solution.py:399
  3.9 9.6 %collective-permute-start.1 = (f32[21,8,128]{2,1,0:T(8,128)S(1)}, f32[21,8,128]{2,1,0:T(8,128)S(1)}, u32[]{:S(2)}, u32[]{:S(2)}) collective-permute-start(f32[21,8,128]{2,1,0:T(8,128)S(1)} %get-tuple-element.21), channel_id=1, source_target_pairs={{0,2},{1,3},{2,0},{3,1},{4,6},{5,7},{6,4},{7,5},{8,10},{9,11},{10,... | collective-permute-start | bytes 258056 | tf_op jit(solution)/shard_map/ppermute | solution.py:399
  5.7 7.9 %collective-permute-start.2 = (f32[21,8,128]{2,1,0:T(8,128)S(1)}, f32[21,8,128]{2,1,0:T(8,128)S(1)}, u32[]{:S(2)}, u32[]{:S(2)}) collective-permute-start(f32[21,8,128]{2,1,0:T(8,128)S(1)} %get-tuple-element.22), channel_id=1, source_target_pairs={{0,3},{1,2},{2,1},{3,0},{4,7},{5,6},{6,5},{7,4},{8,11},{9,10},{10,... | collective-permute-start | bytes 258056 | tf_op jit(solution)/shard_map/ppermute | solution.py:399
  5.8 10.8 %collective-permute-start.3 = (f32[21,8,128]{2,1,0:T(8,128)S(1)}, f32[21,8,128]{2,1,0:T(8,128)S(1)}, u32[]{:S(2)}, u32[]{:S(2)}) collective-permute-start(f32[21,8,128]{2,1,0:T(8,128)S(1)} %get-tuple-element.23), channel_id=1, source_target_pairs={{0,64},{1,65},{2,66},{3,67},{4,68},{5,69},{6,70},{7,71},{8,72},{9,... | collective-permute-start | bytes 258056 | tf_op jit(solution)/shard_map/ppermute | solution.py:399
  17.1 13.1 %collective-permute-start.5 = (f32[2,21,8,128]{3,2,1,0:T(8,128)S(1)}, f32[2,21,8,128]{3,2,1,0:T(8,128)S(1)}, u32[]{:S(2)}, u32[]{:S(2)}) collective-permute-start(f32[2,21,8,128]{3,2,1,0:T(8,128)S(1)} %get-tuple-element.25), channel_id=1, source_target_pairs={{0,4},{1,5},{2,6},{3,7},{4,0},{5,1},{6,2},{7,3},{8,12},{9,13},{10,... | collective-permute-start | bytes 516104 | tf_op jit(solution)/shard_map/ppermute | solution.py:399
  18.5 6.9 %collective-permute-start.6 = (f32[21,8,128]{2,1,0:T(8,128)S(1)}, f32[21,8,128]{2,1,0:T(8,128)S(1)}, u32[]{:S(2)}, u32[]{:S(2)}) collective-permute-start(f32[21,8,128]{2,1,0:T(8,128)S(1)} %get-tuple-element.26), channel_id=1, source_target_pairs={{0,5},{1,4},{2,7},{3,6},{4,1},{5,0},{6,3},{7,2},{8,13},{9,12},{10,... | collective-permute-start | bytes 258056 | tf_op jit(solution)/shard_map/ppermute | solution.py:399
  19.8 8.6 %collective-permute-start.7 = (f32[21,8,128]{2,1,0:T(8,128)S(1)}, f32[21,8,128]{2,1,0:T(8,128)S(1)}, u32[]{:S(2)}, u32[]{:S(2)}) collective-permute-start(f32[21,8,128]{2,1,0:T(8,128)S(1)} %get-tuple-element.27), channel_id=1, source_target_pairs={{0,6},{1,7},{2,4},{3,5},{4,2},{5,3},{6,0},{7,1},{8,14},{9,15},{10,... | collective-permute-start | bytes 258056 | tf_op jit(solution)/shard_map/ppermute | solution.py:399
  21.4 8.8 %collective-permute-start.8 = (f32[21,8,128]{2,1,0:T(8,128)S(1)}, f32[21,8,128]{2,1,0:T(8,128)S(1)}, u32[]{:S(2)}, u32[]{:S(2)}) collective-permute-start(f32[21,8,128]{2,1,0:T(8,128)S(1)} %get-tuple-element.28), channel_id=1, source_target_pairs={{0,7},{1,6},{2,5},{3,4},{4,3},{5,2},{6,1},{7,0},{8,15},{9,14},{10,... | collective-permute-start | bytes 258056 | tf_op jit(solution)/shard_map/ppermute | solution.py:399
  33.1 17.9 %collective-permute-start.11 = (f32[480,128]{1,0:T(8,128)S(1)}, f32[480,128]{1,0:T(8,128)S(1)}, u32[]{:S(2)}, u32[]{:S(2)}) collective-permute-start(f32[480,128]{1,0:T(8,128)S(1)} %get-tuple-element.33), channel_id=1, source_target_pairs={{0,8},{8,0},{16,24},{24,16},{32,40},{40,32},{48,56},{56,48},{64,72... | collective-permute-start | bytes 737288 | tf_op jit(solution)/shard_map/ppermute | solution.py:399
  33.2 17.8 %collective-permute-start.12 = (f32[480,128]{1,0:T(8,128)S(1)}, f32[480,128]{1,0:T(8,128)S(1)}, u32[]{:S(2)}, u32[]{:S(2)}) collective-permute-start(f32[480,128]{1,0:T(8,128)S(1)} %get-tuple-element.34), channel_id=1, source_target_pairs={{0,120},{8,16},{16,8},{24,32},{32,24},{40,48},{48,40},{56,64},{64,... | collective-permute-start | bytes 737288 | tf_op jit(solution)/shard_map/ppermute | solution.py:399
  37.3 9.8 %collective-permute-start.9 = (f32[240,128]{1,0:T(8,128)S(1)}, f32[240,128]{1,0:T(8,128)S(1)}, u32[]{:S(2)}, u32[]{:S(2)}) collective-permute-start(f32[240,128]{1,0:T(8,128)S(1)} %get-tuple-element.31), channel_id=1, source_target_pairs={{0,1},{1,0},{2,3},{3,2},{4,5},{5,4},{6,7},{7,6},{8,9},{9,8},{10,11... | collective-permute-start | bytes 368648 | tf_op jit(solution)/shard_map/ppermute | solution.py:399
  37.3 9.8 %collective-permute-start.10 = (f32[240,128]{1,0:T(8,128)S(1)}, f32[240,128]{1,0:T(8,128)S(1)}, u32[]{:S(2)}, u32[]{:S(2)}) collective-permute-start(f32[240,128]{1,0:T(8,128)S(1)} %get-tuple-element.32), channel_id=1, source_target_pairs={{0,7},{1,2},{2,1},{3,4},{4,3},{5,6},{6,5},{7,0},{8,15},{9,10},{10,... | collective-permute-start | bytes 368648 | tf_op jit(solution)/shard_map/ppermute | solution.py:399

commit v2 on v1

--- a/solution.py
+++ b/solution.py
@@ -18,9 +18,8 @@
 ROWS = FIELDS * CX * CY
 VMEM_LIMIT = 48 * 1024 * 1024
 
-EARLY_FAR = 3 * MOVE
 EARLY_RELAY = 4 * MOVE
-EARLY_ROWS = 8 * MOVE
+EARLY_ROWS = 6 * MOVE
 LATE_ROWS = 4 * MOVE
 ARRIVED = 9 * MOVE
 
@@ -60,7 +59,7 @@
     return pos // TILES, pos % TILES, rank
 
 
-def packed(target, local, rows, old_ref, put):
+def packed(target, local, rows, old_ref, put, ready=None):
     shape = (rows, TILES)
     chosen = iota(shape, 0) == jnp.broadcast_to(target, shape)
     code = jnp.sum(
@@ -68,49 +67,67 @@
     )
     put(PLANES - 1, jnp.broadcast_to(code, shape))
     choice = chosen.astype(jnp.float32).astype(jnp.bfloat16)
+    if ready is not None:
+        ready()
     for field in range(FIELDS):
         values = pick(choice, old_ref[field])
         for part in range(PARTS):
             put(field * PARTS + part, values[:, part * CZ : (part + 1) * CZ])
 
 
-def pack_early_kernel(pos_ref, old_ref, one_ref, two_ref, three_ref, far_ref, relay_ref):
+def pack_early_kernel(
+    pos_hbm, old_hbm, two_ref, three_ref, six_ref, seven_ref, relay_ref, pos_ref, old_ref, sems
+):
     node, dev = place()
+    pos_copy = pltpu.make_async_copy(pos_hbm, pos_ref, sems.at[0])
+    old_copy = pltpu.make_async_copy(old_hbm, old_ref, sems.at[1])
+    pos_copy.start()
+    old_copy.start()
+    pos_copy.wait()
     owner, local, rank = targets(pos_ref[...])
     mask = (owner % 8) ^ dev
-    inside = jnp.where((mask >= 1) & (mask < 4), (mask - 1) * MOVE + rank, -1)
-    outside = jnp.where(owner // 8 == node ^ 8, EARLY_FAR, EARLY_RELAY + (mask - 4) * MOVE) + rank
-    target = jnp.where(owner // 8 == node, inside, outside)
+    outer, low = mask >= 4, mask % 4
+    here = owner // 8 == node
+    by_mask = (mask // 4 * 2 + mask % 2) * MOVE + rank
+    relayed = EARLY_RELAY + mask % 2 * MOVE + rank
+    target = jnp.where(low >= 2, by_mask, jnp.where(outer & ~here, relayed, -1))
+    target = jnp.where(owner // 8 == node ^ 8, -1, target)
 
     def put(plane, value):
-        for block, ref in enumerate((one_ref, two_ref, three_ref, far_ref)):
+        for block, ref in enumerate((two_ref, three_ref, six_ref, seven_ref)):
             ref[plane] = value[block * MOVE : (block + 1) * MOVE]
-        for block in range(4):
+        for block in range(2):
             first = EARLY_RELAY + block * MOVE
             relay_ref[block, plane] = value[first : first + MOVE]
 
-    packed(target, local, EARLY_ROWS, old_ref, put)
+    packed(target, local, EARLY_ROWS, old_ref, put, old_copy.wait)
 
 
 def pack_late_kernel(
-    pos_ref, old_ref, relay_ref, one_ref, two_ref, three_ref, far_ref, four_ref, five_ref, six_ref, seven_ref
+    pos_ref, old_ref, relay_ref, six_ref, seven_ref, one_ref, four_ref, five_ref, far_ref, on_ref
 ):
     node, dev = place()
     owner, local, rank = targets(pos_ref[...])
     mask = (owner % 8) ^ dev
-    target = jnp.where((owner // 8 == node) & (mask >= 4), (mask - 4) * MOVE + rank, -1)
+    inside = jnp.where((mask == 1) | (mask == 4) | (mask == 5), (mask // 4 + mask % 2) * MOVE, -TILES)
+    inside = jnp.where(mask == 1, 0, inside)
+    target = jnp.where(owner // 8 == node, inside, jnp.where(owner // 8 == node ^ 8, 3 * MOVE, -TILES)) + rank
 
     def put(plane, value):
-        four_ref[0, plane] = value[:MOVE]
+        one_ref[plane] = value[:MOVE]
+        four_ref[0, plane] = value[MOVE : 2 * MOVE]
         four_ref[1, plane] = relay_ref[0, plane]
-        for block, ref in enumerate((five_ref, six_ref, seven_ref), 1):
-            ref[plane] = value[block * MOVE : (block + 1) * MOVE] + relay_ref[block, plane]
+        five_ref[plane] = value[2 * MOVE : 3 * MOVE] + relay_ref[1, plane]
+        far_ref[plane] = value[3 * MOVE :]
+        on_ref[0, plane] = six_ref[plane]
+        on_ref[1, plane] = seven_ref[plane]
 
     packed(target, local, LATE_ROWS, old_ref, put)
 
 
 VMEM = pl.BlockSpec(memory_space=pltpu.VMEM)
 ANYWHERE = pl.BlockSpec(memory_space=pl.ANY)
+HBM = pl.BlockSpec(memory_space=pltpu.HBM)
 BUFFER = jax.ShapeDtypeStruct((PLANES, MOVE, CZ), jnp.float32)
 
 
@@ -131,13 +148,26 @@
 
 
 def pack_early(pos, old):
-    return call(pack_early_kernel, "pack_early", (BUFFER,) * 4 + (buffers(4),), [VMEM, VMEM])(pos, old)
-
-
-def pack_late(pos, old, relay, *before):
     return call(
-        pack_late_kernel, "pack_late", (buffers(2),) + (BUFFER,) * 3, [VMEM] * 3 + [ANYWHERE] * 4
-    )(pos, old, relay, *before)
+        pack_early_kernel,
+        "pack_early",
+        (BUFFER,) * 4 + (buffers(2),),
+        [HBM, HBM],
+        scratch_shapes=[
+            pltpu.VMEM(pos.shape, jnp.int32),
+            pltpu.VMEM(old.shape, jnp.float32),
+            pltpu.SemaphoreType.DMA((2,)),
+        ],
+    )(pos, old)
+
+
+def pack_late(pos, old, relay, six, seven, *before):
+    return call(
+        pack_late_kernel,
+        "pack_late",
+        (BUFFER, buffers(2), BUFFER, BUFFER, buffers(2)),
+        [VMEM] * 5 + [ANYWHERE] * len(before),
+    )(pos, old, relay, six, seven, *before)
 
 
 def grains(first, second, half_low, row_pick, lane_picks):
@@ -152,7 +182,7 @@
 
 
 def unpack_kernel(
-    pos_ref, old_ref, one_ref, two_ref, three_ref, far_ref, four_ref, five_ref, six_ref, seven_ref,
+    pos_ref, old_ref, one_ref, two_ref, three_ref, four_ref, five_ref, six_ref, seven_ref, far_ref, on_ref,
     state_ref, prim_ref, x_first_ref, x_second_ref, y_first_ref, y_second_ref, tiles_ref,
 ):
     node, dev = place()
@@ -160,10 +190,14 @@
     square = (TILES, TILES)
     kept = jnp.where(pos // TILES == node * 8 + dev, pos % TILES, -1)
     kept_choice = jnp.broadcast_to(kept, square) == iota(square, 0)
+    middle = (dev >= 2) & (dev < 6)
 
     def arrived(plane):
-        refs = (one_ref, two_ref, three_ref, far_ref, five_ref, six_ref, seven_ref)
-        return jnp.concatenate([ref[plane] for ref in refs] + [four_ref[0, plane], four_ref[1, plane]], axis=0)
+        blocks = [ref[plane] for ref in (one_ref, two_ref, three_ref, five_ref, far_ref)]
+        blocks += [four_ref[0, plane], four_ref[1, plane]]
+        blocks.append(jnp.where(middle, six_ref[plane], on_ref[0, plane]))
+        blocks.append(jnp.where(middle, seven_ref[plane], on_ref[1, plane]))
+        return jnp.concatenate(blocks, axis=0)
 
     code = jnp.concatenate([arrived(PLANES - 1), jnp.zeros((TILES - ARRIVED, CZ), jnp.float32)], axis=0)
     code = code.T.astype(jnp.int32)
@@ -330,7 +364,7 @@
                 out_ref[pl.ds(starts[f], 8), :] = state_ref[pl.ds(starts[f], 8), :] - 0.1 * change
         return carry
 
-    lax.fori_loop(0, CX, step, 0)
+    lax.fori_loop(0, CX, step, 0, unroll=2)
 
 
 def side(first_ref, second_ref, odd, before, rows):
@@ -404,6 +438,11 @@
     return (node + (1 if dev >= 4 else -1)) * 8 + dev
 
 
+def onward_node(device):
+    node, dev = device // 8, device % 8
+    return -1 if 2 <= dev < 6 else (node + (1 if dev < 2 else -1)) * 8 + dev
+
+
 def masked(value, mask):
     return shifted(value, AXES, 128, lambda device: device ^ mask)
 
@@ -411,12 +450,15 @@
 def body(old_state, old_tile_pos):
     pos = old_tile_pos.reshape(1, TILES)
     old = old_state.transpose(1, 0, 2)
-    one, two, three, far, relay = pack_early(pos, old)
+    two, three, six, seven, relay = pack_early(pos, old)
     relay = shifted(relay, AXES, 128, next_node)
-    early = (masked(one, 1), masked(two, 2), masked(three, 3), masked(far, 64))
-    late = pack_late(pos, old, relay, *early)
-    late = [masked(value, 4 + index) for index, value in enumerate(late)]
-    state, prim, x_first, x_second, y_first, y_second = unpack(pos, old, *early, *late)
+    six, seven, two, three = masked(six, 6), masked(seven, 7), masked(two, 2), masked(three, 3)
+    one, four, five, far, onward = pack_late(pos, old, relay, six, seven)
+    onward = shifted(onward, AXES, 128, onward_node)
+    four, five, one, far = masked(four, 4), masked(five, 5), masked(one, 1), masked(far, 64)
+    state, prim, x_first, x_second, y_first, y_second = unpack(
+        pos, old, one, two, three, four, five, six, seven, far, onward
+    )
     x_first = shifted(x_first, "node", 16, lambda i: i ^ 1)
     x_second = shifted(x_second, "node", 16, lambda i: (i + 1) % 16 if i % 2 else (i - 1) % 16)
     y_first = shifted(y_first, "dev", 8, lambda i: i ^ 1)

time: 54.3 us -> 48.6 us (0.90)
  Pallas kernels: 17.3 us -> 14.6 us
  waiting for transfers between devices: 9.93 us -> 7.52 us
  starting transfers between devices: 24.7 us -> 23.7 us
    pallas_call x3, Pallas kernels: 13.4 us -> 10.5 us  [stage(): call(kernel, name, jax.ShapeDtypeStruct((ROWS, CZ), jnp.float32), [VMEM]...]
    ppermute x13 -> x14, waiting for transfers between devices: 9.93 us -> 7.52 us  [shifted(): lax.ppermute(value, axes, [pair for pair in pairs if 0 <= pair[1] < count])]
    ppermute x13 -> x14, starting transfers between devices: 24.7 us -> 23.7 us  [shifted(): lax.ppermute(value, axes, [pair for pair in pairs if 0 <= pair[1] < count])]
  transfers between devices with their start and end apart: 13 -> 14, of which waited for: 4 -> 5; matrix products, arithmetic and copies ran while one was open for 0% -> 0% of each run, Pallas kernels for 19% -> 17%
where the time goes in v2:
time: 48.6 us; the launch traced here: 47.9 us
  starting transfers between devices  23.7 us (49%)
  Pallas kernels  14.6 us (30%)
  waiting for transfers between devices  7.52 us (15%)
  local copies, waits for them, and re-layouts  1.97 us (4%)
    ppermute x14, starting transfers between devices, shifted(): lax.ppermute(value, axes, [pair for pair in pairs if 0 <= pair[1] < count])  23.7 us
    pallas_call x3, Pallas kernels, stage(): call(kernel, name, jax.ShapeDtypeStruct((ROWS, CZ), jnp.float32), [VMEM]...  10.5 us
    ppermute x14, waiting for transfers between devices, shifted(): lax.ppermute(value, axes, [pair for pair in pairs if 0 <= pair[1] < count])  7.52 us
    pallas_call x1, Pallas kernels, unpack(): call(unpack_kernel, 'unpack', (grid_rows, grid_rows, x_side, x_side, y_si...  2.86 us
    unnamed x4, local copies, waits for them, and re-layouts  1.97 us
  transfers between devices with their start and end apart: 14, of which 5 were waited for; matrix products, arithmetic and copies ran while one was open for 0% of the time, Pallas kernels for 17%

profile of v2, /device:TPU:0, one launch (start us, length us, event | category | flops | bytes accessed | tf_op | source)
XLA Modules:
  0.0 47.9 jit_solution(4512968200835016432)
XLA Ops:
  0.0 1.3 %copy-done = f32[128,5,512]{2,0,1:T(8,128)S(1)} copy-done((f32[128,5,512]{2,0,1:T(8,128)S(1)}, f32[128,5,512]{2,0,1:T(8,128)}, u32[]{:S(2)}) %copy-start) | copy-done | bytes 1310744
  1.3 0.7 %copy-done.1 = s32[128]{0:T(128)S(1)} copy-done((s32[128]{0:T(128)S(1)}, s32[128]{0:T(128)}, u32[]{:S(2)}) %copy-start.1) | copy-done | bytes 536
  2.0 0.8 %pack_early.1 = (f32[21,8,128]{2,1,0:T(8,128)S(1)}, f32[21,8,128]{2,1,0:T(8,128)S(1)}, f32[21,8,128]{2,1,0:T(8,128)S(1)}, f32[21,8,128]{2,1,0:T(8,128)S(1)}, f32[2,21,8,128]{3,2,1,0:T(8,128)S(1)}) custom-call(s32[1,128]{1,0:T(1,128)S(1)} %bitcast.6, f32[5,128,512]{2,1,0:T(8,128)S(1)} %bitcast.3), custom_call_target="tpu_custom_call" | custom-call | tf_op jit(solution)/shard_map/pack_early/pallas_call | solution.py:151
  2.7 1.3 %collective-permute-start = (f32[2,21,8,128]{3,2,1,0:T(8,128)S(1)}, f32[2,21,8,128]{3,2,1,0:T(8,128)S(1)}, u32[]{:S(2)}, u32[]{:S(2)}) collective-permute-start(f32[2,21,8,128]{3,2,1,0:T(8,128)S(1)} %get-tuple-element.21), channel_id=1, source_target_pairs={{4,12},{5,13},{6,14},{7,15},{8,0},{9,1},{10,2},{11,3},{12,20},{13,... | collective-permute-start | bytes 516104 | tf_op jit(solution)/shard_map/ppermute | solution.py:433
  4.0 5.7 %collective-permute-start.1 = (f32[21,8,128]{2,1,0:T(8,128)S(1)}, f32[21,8,128]{2,1,0:T(8,128)S(1)}, u32[]{:S(2)}, u32[]{:S(2)}) collective-permute-start(f32[21,8,128]{2,1,0:T(8,128)S(1)} %get-tuple-element.22), channel_id=1, source_target_pairs={{0,6},{1,7},{2,4},{3,5},{4,2},{5,3},{6,0},{7,1},{8,14},{9,15},{10,... | collective-permute-start | bytes 258056 | tf_op jit(solution)/shard_map/ppermute | solution.py:433
  9.8 0.0 collective-permute-start.2
  9.8 0.1 collective-permute-start.4
  9.9 1.4 %collective-permute-start.5 = (f32[21,8,128]{2,1,0:T(8,128)S(1)}, f32[21,8,128]{2,1,0:T(8,128)S(1)}, u32[]{:S(2)}, u32[]{:S(2)}) collective-permute-start(f32[21,8,128]{2,1,0:T(8,128)S(1)} %get-tuple-element.26), channel_id=1, source_target_pairs={{0,3},{1,2},{2,1},{3,0},{4,7},{5,6},{6,5},{7,4},{8,11},{9,10},{10,... | collective-permute-start | bytes 258056 | tf_op jit(solution)/shard_map/ppermute | solution.py:433
  11.3 0.9 %collective-permute-done.1.six_ref = f32[21,8,128]{2,1,0:T(8,128)S(1)} collective-permute-done((f32[21,8,128]{2,1,0:T(8,128)S(1)}, f32[21,8,128]{2,1,0:T(8,128)S(1)}, u32[]{:S(2)}, u32[]{:S(2)}) %collective-permute-start.1) | collective-permute-done | bytes 86048 | tf_op jit(solution)/shard_map/ppermute | solution.py:433
  12.2 3.0 %collective-permute-done.2.seven_ref = f32[21,8,128]{2,1,0:T(8,128)S(1)} collective-permute-done((f32[21,8,128]{2,1,0:T(8,128)S(1)}, f32[21,8,128]{2,1,0:T(8,128)S(1)}, u32[]{:S(2)}, u32[]{:S(2)}) %collective-permute-start.2) | collective-permute-done | bytes 86048 | tf_op jit(solution)/shard_map/ppermute | solution.py:433
  15.2 0.0 collective-permute-done.relay_ref
  15.3 0.5 %pack_late.1 = (f32[21,8,128]{2,1,0:T(8,128)S(1)}, f32[2,21,8,128]{3,2,1,0:T(8,128)S(1)}, f32[21,8,128]{2,1,0:T(8,128)S(1)}, f32[21,8,128]{2,1,0:T(8,128)S(1)}, f32[2,21,8,128]{3,2,1,0:T(8,128)S(1)}) custom-call(s32[1,128]{1,0:T(1,128)S(1)} %bitcast.7, f32[5,128,512]{2,1,0:T(8,128)S(1)} %bitcast.4, f32[2,21,8,128]{3,2,1,0:T(8,128)S(1)} %collective-permute-done.relay_ref, ...), custom_call_target="tpu_custom_call" | custom-call | tf_op jit(solution)/shard_map/pack_late/pallas_call | solution.py:165
  15.8 0.1 collective-permute-start.6
  15.8 3.8 %collective-permute-start.9 = (f32[2,21,8,128]{3,2,1,0:T(8,128)S(1)}, f32[2,21,8,128]{3,2,1,0:T(8,128)S(1)}, u32[]{:S(2)}, u32[]{:S(2)}) collective-permute-start(f32[2,21,8,128]{3,2,1,0:T(8,128)S(1)} %get-tuple-element.30), channel_id=1, source_target_pairs={{0,8},{1,9},{8,16},{9,17},{14,6},{15,7},{16,24},{17,25},{22,14},{2... | collective-permute-start | bytes 516104 | tf_op jit(solution)/shard_map/ppermute | solution.py:433
  19.7 0.1 collective-permute-start.3
  19.8 0.4 collective-permute-start.7
  20.2 0.0 collective-permute-done.5.three_ref
  20.2 3.4 %collective-permute-start.8 = (f32[21,8,128]{2,1,0:T(8,128)S(1)}, f32[21,8,128]{2,1,0:T(8,128)S(1)}, u32[]{:S(2)}, u32[]{:S(2)}) collective-permute-start(f32[21,8,128]{2,1,0:T(8,128)S(1)} %get-tuple-element.29), channel_id=1, source_target_pairs={{0,64},{1,65},{2,66},{3,67},{4,68},{5,69},{6,70},{7,71},{8,72},{9,... | collective-permute-start | bytes 258056 | tf_op jit(solution)/shard_map/ppermute | solution.py:433
  23.7 1.9 %collective-permute-done.7.five_ref = f32[21,8,128]{2,1,0:T(8,128)S(1)} collective-permute-done((f32[21,8,128]{2,1,0:T(8,128)S(1)}, f32[21,8,128]{2,1,0:T(8,128)S(1)}, u32[]{:S(2)}, u32[]{:S(2)}) %collective-permute-start.7) | collective-permute-done | bytes 86048 | tf_op jit(solution)/shard_map/ppermute | solution.py:433
  25.6 1.0 %collective-permute-done.8.far_ref = f32[21,8,128]{2,1,0:T(8,128)S(1)} collective-permute-done((f32[21,8,128]{2,1,0:T(8,128)S(1)}, f32[21,8,128]{2,1,0:T(8,128)S(1)}, u32[]{:S(2)}, u32[]{:S(2)}) %collective-permute-start.8) | collective-permute-done | bytes 86048 | tf_op jit(solution)/shard_map/ppermute | solution.py:433
  26.6 0.0 collective-permute-done.6.four_ref
  26.6 0.0 collective-permute-done.9.on_ref
  26.6 2.9 %unpack.1 = (f32[2560,128]{1,0:T(8,128)S(1)}, f32[2560,128]{1,0:T(8,128)S(1)}, f32[480,128]{1,0:T(8,128)S(1)}, f32[480,128]{1,0:T(8,128)S(1)}, f32[240,128]{1,0:T(8,128)S(1)}, /*index=5*/f32[240,128]{1,0:T(8,128)S(1)}) custom-call(s32[1,128]{1,0:T(1,128)S(1)} %bitcast.8, f32[5,128,512]{2,1,0:T(8,128)S(1)} %bitcast.5, ...), custom_call_target="tpu_custom_call" | custom-call | tf_op jit(solution)/shard_map/unpack/pallas_call | solution.py:264
  29.5 1.7 %collective-permute-start.12 = (f32[480,128]{1,0:T(8,128)S(1)}, f32[480,128]{1,0:T(8,128)S(1)}, u32[]{:S(2)}, u32[]{:S(2)}) collective-permute-start(f32[480,128]{1,0:T(8,128)S(1)} %get-tuple-element.35), channel_id=1, source_target_pairs={{0,8},{8,0},{16,24},{24,16},{32,40},{40,32},{48,56},{56,48},{64,72... | collective-permute-start | bytes 737288 | tf_op jit(solution)/shard_map/ppermute | solution.py:433
  31.1 4.4 %collective-permute-start.13 = (f32[480,128]{1,0:T(8,128)S(1)}, f32[480,128]{1,0:T(8,128)S(1)}, u32[]{:S(2)}, u32[]{:S(2)}) collective-permute-start(f32[480,128]{1,0:T(8,128)S(1)} %get-tuple-element.36), channel_id=1, source_target_pairs={{0,120},{8,16},{16,8},{24,32},{32,24},{40,48},{48,40},{56,64},{64,... | collective-permute-start | bytes 737288 | tf_op jit(solution)/shard_map/ppermute | solution.py:433
  35.5 0.0 collective-permute-start.10
  35.5 1.1 %collective-permute-start.11 = (f32[240,128]{1,0:T(8,128)S(1)}, f32[240,128]{1,0:T(8,128)S(1)}, u32[]{:S(2)}, u32[]{:S(2)}) collective-permute-start(f32[240,128]{1,0:T(8,128)S(1)} %get-tuple-element.34), channel_id=1, source_target_pairs={{0,7},{1,2},{2,1},{3,4},{4,3},{5,6},{6,5},{7,0},{8,15},{9,10},{10,... | collective-permute-start | bytes 368648 | tf_op jit(solution)/shard_map/ppermute | solution.py:433
  36.7 3.7 %flux_third.1.before_ref = f32[2560,128]{1,0:T(8,128)S(1)} custom-call(f32[2560,128]{1,0:T(8,128)S(1)} %get-tuple-element.31.state_ref, f32[2560,128]{1,0:T(8,128)S(1)} %get-tuple-element.32.prim_ref), custom_call_target="tpu_custom_call" | custom-call | flops 20000000 | bytes 4000000 | tf_op jit(solution)/shard_map/flux_third/pallas_call | solution.py:422
  40.4 0.0 collective-permute-done.10.first_ref
  40.4 0.7 %collective-permute-done.11.second_ref = f32[240,128]{1,0:T(8,128)S(1)} collective-permute-done((f32[240,128]{1,0:T(8,128)S(1)}, f32[240,128]{1,0:T(8,128)S(1)}, u32[]{:S(2)}, u32[]{:S(2)}) %collective-permute-start.11) | collective-permute-done | bytes 122912 | tf_op jit(solution)/shard_map/ppermute | solution.py:433
  41.1 3.8 %flux_second.1.before_ref = f32[2560,128]{1,0:T(8,128)S(1)} custom-call(f32[2560,128]{1,0:T(8,128)S(1)} %flux_third.1.before_ref, f32[2560,128]{1,0:T(8,128)S(1)} %get-tuple-element.32.prim_ref, f32[240,128]{1,0:T(8,128)S(1)} %collective-permute-done.10.first_ref, f32[240,128]{1,0:T(8,128)S(1)} %collective-permute-done.11.second_ref), custom_call_target="tpu_custom_call" | custom-call | flops 20000000 | bytes 4000000 | tf_op jit(solution)/shard_map/flux_second/pallas_call | solution.py:422
  44.9 3.0 %flux_first.1 = f32[2560,128]{1,0:T(8,128)} custom-call(f32[2560,128]{1,0:T(8,128)S(1)} %flux_second.1.before_ref, f32[2560,128]{1,0:T(8,128)S(1)} %get-tuple-element.32.prim_ref, f32[480,128]{1,0:T(8,128)S(1)} %collective-permute-done.12.first_ref, f32[480,128]{1,0:T(8,128)S(1)} %collective-permute-done.13.second_ref), custom_call_target="tpu_custom_call" | custom-call | flops 20000000 | bytes 4000000 | tf_op jit(solution)/shard_map/flux_first/pallas_call | solution.py:422
  (6 shorter events, 0.0 us)
Async XLA Ops:
  0.0 1.3 %copy-start = (f32[128,5,512]{2,0,1:T(8,128)S(1)}, f32[128,5,512]{2,0,1:T(8,128)}, u32[]{:S(2)}) copy-start(f32[128,5,512]{2,0,1:T(8,128)} %param.2) | copy-start | bytes 3932164
  1.3 0.7 %copy-start.1 = (s32[128]{0:T(128)S(1)}, s32[128]{0:T(128)}, u32[]{:S(2)}) copy-start(s32[128]{0:T(128)} %param.3) | copy-start | bytes 1540
  2.7 12.5 %collective-permute-start = (f32[2,21,8,128]{3,2,1,0:T(8,128)S(1)}, f32[2,21,8,128]{3,2,1,0:T(8,128)S(1)}, u32[]{:S(2)}, u32[]{:S(2)}) collective-permute-start(f32[2,21,8,128]{3,2,1,0:T(8,128)S(1)} %get-tuple-element.21), channel_id=1, source_target_pairs={{4,12},{5,13},{6,14},{7,15},{8,0},{9,1},{10,2},{11,3},{12,20},{13,... | collective-permute-start | bytes 516104 | tf_op jit(solution)/shard_map/ppermute | solution.py:433
  4.0 8.2 %collective-permute-start.1 = (f32[21,8,128]{2,1,0:T(8,128)S(1)}, f32[21,8,128]{2,1,0:T(8,128)S(1)}, u32[]{:S(2)}, u32[]{:S(2)}) collective-permute-start(f32[21,8,128]{2,1,0:T(8,128)S(1)} %get-tuple-element.22), channel_id=1, source_target_pairs={{0,6},{1,7},{2,4},{3,5},{4,2},{5,3},{6,0},{7,1},{8,14},{9,15},{10,... | collective-permute-start | bytes 258056 | tf_op jit(solution)/shard_map/ppermute | solution.py:433
  9.8 5.5 %collective-permute-start.2 = (f32[21,8,128]{2,1,0:T(8,128)S(1)}, f32[21,8,128]{2,1,0:T(8,128)S(1)}, u32[]{:S(2)}, u32[]{:S(2)}) collective-permute-start(f32[21,8,128]{2,1,0:T(8,128)S(1)} %get-tuple-element.23), channel_id=1, source_target_pairs={{0,7},{1,6},{2,5},{3,4},{4,3},{5,2},{6,1},{7,0},{8,15},{9,14},{10,... | collective-permute-start | bytes 258056 | tf_op jit(solution)/shard_map/ppermute | solution.py:433
  9.8 10.0 %collective-permute-start.4 = (f32[21,8,128]{2,1,0:T(8,128)S(1)}, f32[21,8,128]{2,1,0:T(8,128)S(1)}, u32[]{:S(2)}, u32[]{:S(2)}) collective-permute-start(f32[21,8,128]{2,1,0:T(8,128)S(1)} %get-tuple-element.25), channel_id=1, source_target_pairs={{0,2},{1,3},{2,0},{3,1},{4,6},{5,7},{6,4},{7,5},{8,10},{9,11},{10,... | collective-permute-start | bytes 258056 | tf_op jit(solution)/shard_map/ppermute | solution.py:433
  9.9 10.3 %collective-permute-start.5 = (f32[21,8,128]{2,1,0:T(8,128)S(1)}, f32[21,8,128]{2,1,0:T(8,128)S(1)}, u32[]{:S(2)}, u32[]{:S(2)}) collective-permute-start(f32[21,8,128]{2,1,0:T(8,128)S(1)} %get-tuple-element.26), channel_id=1, source_target_pairs={{0,3},{1,2},{2,1},{3,0},{4,7},{5,6},{6,5},{7,4},{8,11},{9,10},{10,... | collective-permute-start | bytes 258056 | tf_op jit(solution)/shard_map/ppermute | solution.py:433
  15.8 10.8 %collective-permute-start.6 = (f32[2,21,8,128]{3,2,1,0:T(8,128)S(1)}, f32[2,21,8,128]{3,2,1,0:T(8,128)S(1)}, u32[]{:S(2)}, u32[]{:S(2)}) collective-permute-start(f32[2,21,8,128]{3,2,1,0:T(8,128)S(1)} %get-tuple-element.27), channel_id=1, source_target_pairs={{0,4},{1,5},{2,6},{3,7},{4,0},{5,1},{6,2},{7,3},{8,12},{9,13},{10,... | collective-permute-start | bytes 516104 | tf_op jit(solution)/shard_map/ppermute | solution.py:433
  15.8 10.8 %collective-permute-start.9 = (f32[2,21,8,128]{3,2,1,0:T(8,128)S(1)}, f32[2,21,8,128]{3,2,1,0:T(8,128)S(1)}, u32[]{:S(2)}, u32[]{:S(2)}) collective-permute-start(f32[2,21,8,128]{3,2,1,0:T(8,128)S(1)} %get-tuple-element.30), channel_id=1, source_target_pairs={{0,8},{1,9},{8,16},{9,17},{14,6},{15,7},{16,24},{17,25},{22,14},{2... | collective-permute-start | bytes 516104 | tf_op jit(solution)/shard_map/ppermute | solution.py:433
  19.7 4.0 %collective-permute-start.3 = (f32[21,8,128]{2,1,0:T(8,128)S(1)}, f32[21,8,128]{2,1,0:T(8,128)S(1)}, u32[]{:S(2)}, u32[]{:S(2)}) collective-permute-start(f32[21,8,128]{2,1,0:T(8,128)S(1)} %get-tuple-element.24), channel_id=1, source_target_pairs={{0,1},{1,0},{2,3},{3,2},{4,5},{5,4},{6,7},{7,6},{8,9},{9,8},{10,11... | collective-permute-start | bytes 258056 | tf_op jit(solution)/shard_map/ppermute | solution.py:433
  19.8 5.8 %collective-permute-start.7 = (f32[21,8,128]{2,1,0:T(8,128)S(1)}, f32[21,8,128]{2,1,0:T(8,128)S(1)}, u32[]{:S(2)}, u32[]{:S(2)}) collective-permute-start(f32[21,8,128]{2,1,0:T(8,128)S(1)} %get-tuple-element.28), channel_id=1, source_target_pairs={{0,5},{1,4},{2,7},{3,6},{4,1},{5,0},{6,3},{7,2},{8,13},{9,12},{10,... | collective-permute-start | bytes 258056 | tf_op jit(solution)/shard_map/ppermute | solution.py:433
  20.2 6.3 %collective-permute-start.8 = (f32[21,8,128]{2,1,0:T(8,128)S(1)}, f32[21,8,128]{2,1,0:T(8,128)S(1)}, u32[]{:S(2)}, u32[]{:S(2)}) collective-permute-start(f32[21,8,128]{2,1,0:T(8,128)S(1)} %get-tuple-element.29), channel_id=1, source_target_pairs={{0,64},{1,65},{2,66},{3,67},{4,68},{5,69},{6,70},{7,71},{8,72},{9,... | collective-permute-start | bytes 258056 | tf_op jit(solution)/shard_map/ppermute | solution.py:433
  29.5 15.4 %collective-permute-start.12 = (f32[480,128]{1,0:T(8,128)S(1)}, f32[480,128]{1,0:T(8,128)S(1)}, u32[]{:S(2)}, u32[]{:S(2)}) collective-permute-start(f32[480,128]{1,0:T(8,128)S(1)} %get-tuple-element.35), channel_id=1, source_target_pairs={{0,8},{8,0},{16,24},{24,16},{32,40},{40,32},{48,56},{56,48},{64,72... | collective-permute-start | bytes 737288 | tf_op jit(solution)/shard_map/ppermute | solution.py:433
  31.1 13.7 %collective-permute-start.13 = (f32[480,128]{1,0:T(8,128)S(1)}, f32[480,128]{1,0:T(8,128)S(1)}, u32[]{:S(2)}, u32[]{:S(2)}) collective-permute-start(f32[480,128]{1,0:T(8,128)S(1)} %get-tuple-element.36), channel_id=1, source_target_pairs={{0,120},{8,16},{16,8},{24,32},{32,24},{40,48},{48,40},{56,64},{64,... | collective-permute-start | bytes 737288 | tf_op jit(solution)/shard_map/ppermute | solution.py:433
  35.5 4.8 %collective-permute-start.10 = (f32[240,128]{1,0:T(8,128)S(1)}, f32[240,128]{1,0:T(8,128)S(1)}, u32[]{:S(2)}, u32[]{:S(2)}) collective-permute-start(f32[240,128]{1,0:T(8,128)S(1)} %get-tuple-element.33), channel_id=1, source_target_pairs={{0,1},{1,0},{2,3},{3,2},{4,5},{5,4},{6,7},{7,6},{8,9},{9,8},{10,11... | collective-permute-start | bytes 368648 | tf_op jit(solution)/shard_map/ppermute | solution.py:433
  35.5 5.5 %collective-permute-start.11 = (f32[240,128]{1,0:T(8,128)S(1)}, f32[240,128]{1,0:T(8,128)S(1)}, u32[]{:S(2)}, u32[]{:S(2)}) collective-permute-start(f32[240,128]{1,0:T(8,128)S(1)} %get-tuple-element.34), channel_id=1, source_target_pairs={{0,7},{1,2},{2,1},{3,4},{4,3},{5,6},{6,5},{7,0},{8,15},{9,10},{10,... | collective-permute-start | bytes 368648 | tf_op jit(solution)/shard_map/ppermute | solution.py:433

commit v3 on v2

--- a/solution.py
+++ b/solution.py
@@ -59,7 +59,7 @@
     return pos // TILES, pos % TILES, rank
 
 
-def packed(target, local, rows, old_ref, put, ready=None):
+def packed(target, local, rows, old_ref, put):
     shape = (rows, TILES)
     chosen = iota(shape, 0) == jnp.broadcast_to(target, shape)
     code = jnp.sum(
@@ -67,23 +67,14 @@
     )
     put(PLANES - 1, jnp.broadcast_to(code, shape))
     choice = chosen.astype(jnp.float32).astype(jnp.bfloat16)
-    if ready is not None:
-        ready()
     for field in range(FIELDS):
         values = pick(choice, old_ref[field])
         for part in range(PARTS):
             put(field * PARTS + part, values[:, part * CZ : (part + 1) * CZ])
 
 
-def pack_early_kernel(
-    pos_hbm, old_hbm, two_ref, three_ref, six_ref, seven_ref, relay_ref, pos_ref, old_ref, sems
-):
+def pack_early_kernel(pos_ref, old_ref, two_ref, three_ref, six_ref, seven_ref, relay_ref):
     node, dev = place()
-    pos_copy = pltpu.make_async_copy(pos_hbm, pos_ref, sems.at[0])
-    old_copy = pltpu.make_async_copy(old_hbm, old_ref, sems.at[1])
-    pos_copy.start()
-    old_copy.start()
-    pos_copy.wait()
     owner, local, rank = targets(pos_ref[...])
     mask = (owner % 8) ^ dev
     outer, low = mask >= 4, mask % 4
@@ -100,7 +91,7 @@
             first = EARLY_RELAY + block * MOVE
             relay_ref[block, plane] = value[first : first + MOVE]
 
-    packed(target, local, EARLY_ROWS, old_ref, put, old_copy.wait)
+    packed(target, local, EARLY_ROWS, old_ref, put)
 
 
 def pack_late_kernel(
@@ -126,8 +117,6 @@
 
 
 VMEM = pl.BlockSpec(memory_space=pltpu.VMEM)
-ANYWHERE = pl.BlockSpec(memory_space=pl.ANY)
-HBM = pl.BlockSpec(memory_space=pltpu.HBM)
 BUFFER = jax.ShapeDtypeStruct((PLANES, MOVE, CZ), jnp.float32)
 
 
@@ -148,26 +137,13 @@
 
 
 def pack_early(pos, old):
+    return call(pack_early_kernel, "pack_early", (BUFFER,) * 4 + (buffers(2),), [VMEM, VMEM])(pos, old)
+
+
+def pack_late(pos, old, relay, six, seven):
     return call(
-        pack_early_kernel,
-        "pack_early",
-        (BUFFER,) * 4 + (buffers(2),),
-        [HBM, HBM],
-        scratch_shapes=[
-            pltpu.VMEM(pos.shape, jnp.int32),
-            pltpu.VMEM(old.shape, jnp.float32),
-            pltpu.SemaphoreType.DMA((2,)),
-        ],
-    )(pos, old)
-
-
-def pack_late(pos, old, relay, six, seven, *before):
-    return call(
-        pack_late_kernel,
-        "pack_late",
-        (BUFFER, buffers(2), BUFFER, BUFFER, buffers(2)),
-        [VMEM] * 5 + [ANYWHERE] * len(before),
-    )(pos, old, relay, six, seven, *before)
+        pack_late_kernel, "pack_late", (BUFFER, buffers(2), BUFFER, BUFFER, buffers(2)), [VMEM] * 5
+    )(pos, old, relay, six, seven)
 
 
 def grains(first, second, half_low, row_pick, lane_picks):
@@ -182,7 +158,7 @@
 
 
 def unpack_kernel(
-    pos_ref, old_ref, one_ref, two_ref, three_ref, four_ref, five_ref, six_ref, seven_ref, far_ref, on_ref,
+    pos_ref, old_ref, one_ref, two_ref, three_ref, four_ref, five_ref, far_ref, on_ref,
     state_ref, prim_ref, x_first_ref, x_second_ref, y_first_ref, y_second_ref, tiles_ref,
 ):
     node, dev = place()
@@ -190,13 +166,11 @@
     square = (TILES, TILES)
     kept = jnp.where(pos // TILES == node * 8 + dev, pos % TILES, -1)
     kept_choice = jnp.broadcast_to(kept, square) == iota(square, 0)
-    middle = (dev >= 2) & (dev < 6)
 
     def arrived(plane):
         blocks = [ref[plane] for ref in (one_ref, two_ref, three_ref, five_ref, far_ref)]
         blocks += [four_ref[0, plane], four_ref[1, plane]]
-        blocks.append(jnp.where(middle, six_ref[plane], on_ref[0, plane]))
-        blocks.append(jnp.where(middle, seven_ref[plane], on_ref[1, plane]))
+        blocks += [on_ref[0, plane], on_ref[1, plane]]
         return jnp.concatenate(blocks, axis=0)
 
     code = jnp.concatenate([arrived(PLANES - 1), jnp.zeros((TILES - ARRIVED, CZ), jnp.float32)], axis=0)
@@ -372,7 +346,7 @@
     return jnp.where(odd, first, second) if before else jnp.where(odd, second, first)
 
 
-def y_kernel(before_ref, prim_ref, first_ref, second_ref, out_ref):
+def y_kernel(prim_ref, first_ref, second_ref, change_ref):
     odd = lax.axis_index("dev") % 2 == 1
 
     def step(block, carry):
@@ -385,8 +359,8 @@
 
         def emit(cell, change):
             for f in range(FIELDS):
-                rows = pl.ds((f * CX + block * 8) * CY + cell, 8, stride=CY)
-                out_ref[rows, :] = before_ref[rows, :] - 0.1 * change[f]
+                rows = pl.ds(pl.multiple_of((f * CY + cell) * CX + block * 8, 8), 8)
+                change_ref[rows, :] = change[f]
 
         sweep(load, CY, 2, emit)
         return carry
@@ -394,7 +368,7 @@
     lax.fori_loop(0, CX // 8, step, 0)
 
 
-def x_kernel(before_ref, prim_ref, first_ref, second_ref, out_ref):
+def x_kernel(before_ref, prim_ref, change_ref, first_ref, second_ref, out_ref):
     odd = lax.axis_index("node") % 2 == 1
 
     def step(block, carry):
@@ -410,7 +384,8 @@
         def emit(cell, change):
             for f in range(FIELDS):
                 rows = pl.ds(pl.multiple_of((f * CX + cell) * CY + block * 8, 8), 8)
-                out_ref[rows, :] = before_ref[rows, :] - 0.1 * change[f]
+                other = change_ref[pl.ds((f * CY + block * 8) * CX + cell, 8, stride=CX), :]
+                out_ref[rows, :] = before_ref[rows, :] - 0.1 * (change[f] + other)
 
         sweep(load, CX, 1, emit)
         return carry
@@ -430,17 +405,21 @@
 
 def shifted(value, axes, count, target):
     pairs = [(i, target(i)) for i in range(count)]
-    return lax.ppermute(value, axes, [pair for pair in pairs if 0 <= pair[1] < count])
+    return lax.ppermute(value, axes, [pair for pair in pairs if pair[1] >= 0])
+
+
+def hop(device, step):
+    return device + 8 * step if 0 <= device // 8 + step < 16 else -1
 
 
 def next_node(device):
-    node, dev = device // 8, device % 8
-    return (node + (1 if dev >= 4 else -1)) * 8 + dev
+    other = hop(device, 1 if device % 8 >= 4 else -1)
+    return other if other >= 0 else device ^ 4
 
 
 def onward_node(device):
-    node, dev = device // 8, device % 8
-    return -1 if 2 <= dev < 6 else (node + (1 if dev < 2 else -1)) * 8 + dev
+    dev = device % 8
+    return device if 2 <= dev < 6 else hop(device, 1 if dev < 2 else -1)
 
 
 def masked(value, mask):
@@ -457,15 +436,15 @@
     onward = shifted(onward, AXES, 128, onward_node)
     four, five, one, far = masked(four, 4), masked(five, 5), masked(one, 1), masked(far, 64)
     state, prim, x_first, x_second, y_first, y_second = unpack(
-        pos, old, one, two, three, four, five, six, seven, far, onward
+        pos, old, one, two, three, four, five, far, onward
     )
     x_first = shifted(x_first, "node", 16, lambda i: i ^ 1)
     x_second = shifted(x_second, "node", 16, lambda i: (i + 1) % 16 if i % 2 else (i - 1) % 16)
     y_first = shifted(y_first, "dev", 8, lambda i: i ^ 1)
     y_second = shifted(y_second, "dev", 8, lambda i: (i + 1) % 8 if i % 2 else (i - 1) % 8)
     result = stage(z_kernel, "flux_third", state, prim)
-    result = stage(y_kernel, "flux_second", result, prim, y_first, y_second)
-    result = stage(x_kernel, "flux_first", result, prim, x_first, x_second)
+    change = stage(y_kernel, "flux_second", prim, y_first, y_second)
+    result = stage(x_kernel, "flux_first", result, prim, change, x_first, x_second)
     return result.reshape(FIELDS, CX, CY, CZ)
 
 

time: 48.6 us -> 46.1 us (0.949)
  starting transfers between devices: 23.7 us -> 21.7 us
  Pallas kernels: 14.6 us -> 13 us
  waiting for transfers between devices: 7.52 us -> 8.63 us
    ppermute x14, starting transfers between devices: 23.7 us -> 21.7 us  [shifted(): return lax.ppermute(value, axes, [pair for pair in pairs if pair[1] >= 0])]
    pallas_call x3, Pallas kernels: 10.5 us -> 9.12 us  [stage(): call(kernel, name, jax.ShapeDtypeStruct((ROWS, CZ), jnp.float32), [VMEM]...]
    ppermute x14, waiting for transfers between devices: 7.52 us -> 8.63 us  [shifted(): return lax.ppermute(value, axes, [pair for pair in pairs if pair[1] >= 0])]
  transfers between devices with their start and end apart: 14 -> 14, of which waited for: 5 -> 5; matrix products, arithmetic and copies ran while one was open for 0% -> 0% of each run, Pallas kernels for 17% -> 14%
where the time goes in v3:
time: 46.1 us; the launch traced here: 45.4 us
  starting transfers between devices  21.7 us (47%)
  Pallas kernels  13 us (28%)
  waiting for transfers between devices  8.63 us (19%)
  local copies, waits for them, and re-layouts  1.97 us (4%)
    ppermute x14, starting transfers between devices, shifted(): return lax.ppermute(value, axes, [pair for pair in pairs if pair[1] >= 0])  21.7 us
    pallas_call x3, Pallas kernels, stage(): call(kernel, name, jax.ShapeDtypeStruct((ROWS, CZ), jnp.float32), [VMEM]...  9.12 us
    ppermute x14, waiting for transfers between devices, shifted(): return lax.ppermute(value, axes, [pair for pair in pairs if pair[1] >= 0])  8.63 us
    pallas_call x1, Pallas kernels, unpack(): call(unpack_kernel, 'unpack', (grid_rows, grid_rows, x_side, x_side, y_si...  2.83 us
    unnamed x4, local copies, waits for them, and re-layouts  1.97 us
  transfers between devices with their start and end apart: 14, of which 5 were waited for; matrix products, arithmetic and copies ran while one was open for 0% of the time, Pallas kernels for 14%

profile of v3, /device:TPU:0, one launch (start us, length us, event | category | flops | bytes accessed | tf_op | source)
XLA Modules:
  0.0 45.4 jit_solution(15268174851748495718)
XLA Ops:
  0.0 1.3 %copy-done = f32[128,5,512]{2,0,1:T(8,128)S(1)} copy-done((f32[128,5,512]{2,0,1:T(8,128)S(1)}, f32[128,5,512]{2,0,1:T(8,128)}, u32[]{:S(2)}) %copy-start) | copy-done | bytes 1310744
  1.3 0.7 %copy-done.1 = s32[128]{0:T(128)S(1)} copy-done((s32[128]{0:T(128)S(1)}, s32[128]{0:T(128)}, u32[]{:S(2)}) %copy-start.1) | copy-done | bytes 536
  2.0 0.5 %pack_early.1 = (f32[21,8,128]{2,1,0:T(8,128)S(1)}, f32[21,8,128]{2,1,0:T(8,128)S(1)}, f32[21,8,128]{2,1,0:T(8,128)S(1)}, f32[21,8,128]{2,1,0:T(8,128)S(1)}, f32[2,21,8,128]{3,2,1,0:T(8,128)S(1)}) custom-call(s32[1,128]{1,0:T(1,128)S(1)} %bitcast.6, f32[5,128,512]{2,1,0:T(8,128)S(1)} %bitcast.3), custom_call_target="tpu_custom_call" | custom-call | tf_op jit(solution)/shard_map/pack_early/pallas_call | solution.py:140
  2.5 3.3 %collective-permute-start = (f32[2,21,8,128]{3,2,1,0:T(8,128)S(1)}, f32[2,21,8,128]{3,2,1,0:T(8,128)S(1)}, u32[]{:S(2)}, u32[]{:S(2)}) collective-permute-start(f32[2,21,8,128]{3,2,1,0:T(8,128)S(1)} %get-tuple-element.21), channel_id=1, source_target_pairs={{0,4},{1,5},{2,6},{3,7},{4,12},{5,13},{6,14},{7,15},{8,0},{9,1},{1... | collective-permute-start | bytes 516104 | tf_op jit(solution)/shard_map/ppermute | solution.py:408
  5.8 1.7 %collective-permute-start.1 = (f32[21,8,128]{2,1,0:T(8,128)S(1)}, f32[21,8,128]{2,1,0:T(8,128)S(1)}, u32[]{:S(2)}, u32[]{:S(2)}) collective-permute-start(f32[21,8,128]{2,1,0:T(8,128)S(1)} %get-tuple-element.22), channel_id=1, source_target_pairs={{0,6},{1,7},{2,4},{3,5},{4,2},{5,3},{6,0},{7,1},{8,14},{9,15},{10,... | collective-permute-start | bytes 258056 | tf_op jit(solution)/shard_map/ppermute | solution.py:408
  7.6 0.4 collective-permute-start.2
  7.9 0.0 collective-permute-start.4
  7.9 2.6 %collective-permute-start.5 = (f32[21,8,128]{2,1,0:T(8,128)S(1)}, f32[21,8,128]{2,1,0:T(8,128)S(1)}, u32[]{:S(2)}, u32[]{:S(2)}) collective-permute-start(f32[21,8,128]{2,1,0:T(8,128)S(1)} %get-tuple-element.26), channel_id=1, source_target_pairs={{0,3},{1,2},{2,1},{3,0},{4,7},{5,6},{6,5},{7,4},{8,11},{9,10},{10,... | collective-permute-start | bytes 258056 | tf_op jit(solution)/shard_map/ppermute | solution.py:408
  10.5 1.0 %collective-permute-done.1.six_ref = f32[21,8,128]{2,1,0:T(8,128)S(1)} collective-permute-done((f32[21,8,128]{2,1,0:T(8,128)S(1)}, f32[21,8,128]{2,1,0:T(8,128)S(1)}, u32[]{:S(2)}, u32[]{:S(2)}) %collective-permute-start.1) | collective-permute-done | bytes 86048 | tf_op jit(solution)/shard_map/ppermute | solution.py:408
  11.5 1.8 %collective-permute-done.2.seven_ref = f32[21,8,128]{2,1,0:T(8,128)S(1)} collective-permute-done((f32[21,8,128]{2,1,0:T(8,128)S(1)}, f32[21,8,128]{2,1,0:T(8,128)S(1)}, u32[]{:S(2)}, u32[]{:S(2)}) %collective-permute-start.2) | collective-permute-done | bytes 86048 | tf_op jit(solution)/shard_map/ppermute | solution.py:408
  13.4 0.0 collective-permute-done.relay_ref
  13.4 0.5 %pack_late.1 = (f32[21,8,128]{2,1,0:T(8,128)S(1)}, f32[2,21,8,128]{3,2,1,0:T(8,128)S(1)}, f32[21,8,128]{2,1,0:T(8,128)S(1)}, f32[21,8,128]{2,1,0:T(8,128)S(1)}, f32[2,21,8,128]{3,2,1,0:T(8,128)S(1)}) custom-call(s32[1,128]{1,0:T(1,128)S(1)} %bitcast.7, f32[5,128,512]{2,1,0:T(8,128)S(1)} %bitcast.4, f32[2,21,8,128]{3,2,1,0:T(8,128)S(1)} %collective-permute-done.relay_ref, ...), custom_call_target="tpu_custom_call" | custom-call | tf_op jit(solution)/shard_map/pack_late/pallas_call | solution.py:144
  13.9 3.7 %collective-permute-start.6 = (f32[2,21,8,128]{3,2,1,0:T(8,128)S(1)}, f32[2,21,8,128]{3,2,1,0:T(8,128)S(1)}, u32[]{:S(2)}, u32[]{:S(2)}) collective-permute-start(f32[2,21,8,128]{3,2,1,0:T(8,128)S(1)} %get-tuple-element.27), channel_id=1, source_target_pairs={{0,4},{1,5},{2,6},{3,7},{4,0},{5,1},{6,2},{7,3},{8,12},{9,13},{10,... | collective-permute-start | bytes 516104 | tf_op jit(solution)/shard_map/ppermute | solution.py:408
  17.6 1.3 %collective-permute-start.9 = (f32[2,21,8,128]{3,2,1,0:T(8,128)S(1)}, f32[2,21,8,128]{3,2,1,0:T(8,128)S(1)}, u32[]{:S(2)}, u32[]{:S(2)}) collective-permute-start(f32[2,21,8,128]{3,2,1,0:T(8,128)S(1)} %get-tuple-element.30), channel_id=1, source_target_pairs={{0,8},{1,9},{2,2},{3,3},{4,4},{5,5},{8,16},{9,17},{10,10},{11,11},... | collective-permute-start | bytes 516104 | tf_op jit(solution)/shard_map/ppermute | solution.py:408
  18.9 0.1 collective-permute-start.3
  19.0 0.0 collective-permute-done.4.two_ref
  19.0 0.1 collective-permute-start.7
  19.1 0.0 collective-permute-done.5.three_ref
  19.1 2.4 %collective-permute-start.8 = (f32[21,8,128]{2,1,0:T(8,128)S(1)}, f32[21,8,128]{2,1,0:T(8,128)S(1)}, u32[]{:S(2)}, u32[]{:S(2)}) collective-permute-start(f32[21,8,128]{2,1,0:T(8,128)S(1)} %get-tuple-element.29), channel_id=1, source_target_pairs={{0,64},{1,65},{2,66},{3,67},{4,68},{5,69},{6,70},{7,71},{8,72},{9,... | collective-permute-start | bytes 258056 | tf_op jit(solution)/shard_map/ppermute | solution.py:408
  21.5 0.0 collective-permute-done.3.one_ref
  21.5 3.4 %collective-permute-done.7.five_ref = f32[21,8,128]{2,1,0:T(8,128)S(1)} collective-permute-done((f32[21,8,128]{2,1,0:T(8,128)S(1)}, f32[21,8,128]{2,1,0:T(8,128)S(1)}, u32[]{:S(2)}, u32[]{:S(2)}) %collective-permute-start.7) | collective-permute-done | bytes 86048 | tf_op jit(solution)/shard_map/ppermute | solution.py:408
  24.9 0.7 %collective-permute-done.8.far_ref = f32[21,8,128]{2,1,0:T(8,128)S(1)} collective-permute-done((f32[21,8,128]{2,1,0:T(8,128)S(1)}, f32[21,8,128]{2,1,0:T(8,128)S(1)}, u32[]{:S(2)}, u32[]{:S(2)}) %collective-permute-start.8) | collective-permute-done | bytes 86048 | tf_op jit(solution)/shard_map/ppermute | solution.py:408
  25.5 2.8 %unpack.1 = (f32[2560,128]{1,0:T(8,128)S(1)}, f32[2560,128]{1,0:T(8,128)S(1)}, f32[480,128]{1,0:T(8,128)S(1)}, f32[480,128]{1,0:T(8,128)S(1)}, f32[240,128]{1,0:T(8,128)S(1)}, /*index=5*/f32[240,128]{1,0:T(8,128)S(1)}) custom-call(s32[1,128]{1,0:T(1,128)S(1)} %bitcast.8, f32[5,128,512]{2,1,0:T(8,128)S(1)} %bitcast.5, ...), custom_call_target="tpu_custom_call" | custom-call | tf_op jit(solution)/shard_map/unpack/pallas_call | solution.py:238
  28.4 0.5 %collective-permute-start.12 = (f32[480,128]{1,0:T(8,128)S(1)}, f32[480,128]{1,0:T(8,128)S(1)}, u32[]{:S(2)}, u32[]{:S(2)}) collective-permute-start(f32[480,128]{1,0:T(8,128)S(1)} %get-tuple-element.35), channel_id=1, source_target_pairs={{0,8},{8,0},{16,24},{24,16},{32,40},{40,32},{48,56},{56,48},{64,72... | collective-permute-start | bytes 737288 | tf_op jit(solution)/shard_map/ppermute | solution.py:408
  28.9 5.5 %collective-permute-start.13 = (f32[480,128]{1,0:T(8,128)S(1)}, f32[480,128]{1,0:T(8,128)S(1)}, u32[]{:S(2)}, u32[]{:S(2)}) collective-permute-start(f32[480,128]{1,0:T(8,128)S(1)} %get-tuple-element.36), channel_id=1, source_target_pairs={{0,120},{8,16},{16,8},{24,32},{32,24},{40,48},{48,40},{56,64},{64,... | collective-permute-start | bytes 737288 | tf_op jit(solution)/shard_map/ppermute | solution.py:408
  34.4 0.0 collective-permute-start.11
  34.5 3.7 %flux_third.1.before_ref = f32[2560,128]{1,0:T(8,128)S(1)} custom-call(f32[2560,128]{1,0:T(8,128)S(1)} %get-tuple-element.31.state_ref, f32[2560,128]{1,0:T(8,128)S(1)} %get-tuple-element.32.prim_ref), custom_call_target="tpu_custom_call" | custom-call | flops 20000000 | bytes 4000000 | tf_op jit(solution)/shard_map/flux_third/pallas_call | solution.py:397
  38.2 0.0 collective-permute-done.10.first_ref
  38.2 1.8 %collective-permute-done.11.second_ref = f32[240,128]{1,0:T(8,128)S(1)} collective-permute-done((f32[240,128]{1,0:T(8,128)S(1)}, f32[240,128]{1,0:T(8,128)S(1)}, u32[]{:S(2)}, u32[]{:S(2)}) %collective-permute-start.11) | collective-permute-done | bytes 122912 | tf_op jit(solution)/shard_map/ppermute | solution.py:408
  40.0 2.1 %flux_second.1.change_ref = f32[2560,128]{1,0:T(8,128)S(1)} custom-call(f32[2560,128]{1,0:T(8,128)S(1)} %get-tuple-element.32.prim_ref, f32[240,128]{1,0:T(8,128)S(1)} %collective-permute-done.10.first_ref, f32[240,128]{1,0:T(8,128)S(1)} %collective-permute-done.11.second_ref), custom_call_target="tpu_custom_call" | custom-call | flops 20000000 | bytes 4000000 | tf_op jit(solution)/shard_map/flux_second/pallas_call | solution.py:397
  42.1 0.0 collective-permute-done.12.first_ref
  42.1 3.3 %flux_first.1 = f32[2560,128]{1,0:T(8,128)} custom-call(f32[2560,128]{1,0:T(8,128)S(1)} %flux_third.1.before_ref, f32[2560,128]{1,0:T(8,128)S(1)} %get-tuple-element.32.prim_ref, f32[2560,128]{1,0:T(8,128)S(1)} %flux_second.1.change_ref, f32[480,128]{1,0:T(8,128)S(1)} %collective-permute-done.12.first_ref, f32[480,128]{1,0:T(8,128)S(1)} %collective-permute-done.13.second_ref), custom_call_target="tpu_custom_call" | custom-call | flops 20000000 | bytes 4000000 | tf_op jit(solution)/shard_map/flux_first/pallas_call | solution.py:397
  (6 shorter events, 0.0 us)
Async XLA Ops:
  0.0 1.3 %copy-start = (f32[128,5,512]{2,0,1:T(8,128)S(1)}, f32[128,5,512]{2,0,1:T(8,128)}, u32[]{:S(2)}) copy-start(f32[128,5,512]{2,0,1:T(8,128)} %param.2) | copy-start | bytes 3932164
  1.3 0.7 %copy-start.1 = (s32[128]{0:T(128)S(1)}, s32[128]{0:T(128)}, u32[]{:S(2)}) copy-start(s32[128]{0:T(128)} %param.3) | copy-start | bytes 1540
  2.5 10.9 %collective-permute-start = (f32[2,21,8,128]{3,2,1,0:T(8,128)S(1)}, f32[2,21,8,128]{3,2,1,0:T(8,128)S(1)}, u32[]{:S(2)}, u32[]{:S(2)}) collective-permute-start(f32[2,21,8,128]{3,2,1,0:T(8,128)S(1)} %get-tuple-element.21), channel_id=1, source_target_pairs={{0,4},{1,5},{2,6},{3,7},{4,12},{5,13},{6,14},{7,15},{8,0},{9,1},{1... | collective-permute-start | bytes 516104 | tf_op jit(solution)/shard_map/ppermute | solution.py:408
  5.8 5.7 %collective-permute-start.1 = (f32[21,8,128]{2,1,0:T(8,128)S(1)}, f32[21,8,128]{2,1,0:T(8,128)S(1)}, u32[]{:S(2)}, u32[]{:S(2)}) collective-permute-start(f32[21,8,128]{2,1,0:T(8,128)S(1)} %get-tuple-element.22), channel_id=1, source_target_pairs={{0,6},{1,7},{2,4},{3,5},{4,2},{5,3},{6,0},{7,1},{8,14},{9,15},{10,... | collective-permute-start | bytes 258056 | tf_op jit(solution)/shard_map/ppermute | solution.py:408
  7.6 5.8 %collective-permute-start.2 = (f32[21,8,128]{2,1,0:T(8,128)S(1)}, f32[21,8,128]{2,1,0:T(8,128)S(1)}, u32[]{:S(2)}, u32[]{:S(2)}) collective-permute-start(f32[21,8,128]{2,1,0:T(8,128)S(1)} %get-tuple-element.23), channel_id=1, source_target_pairs={{0,7},{1,6},{2,5},{3,4},{4,3},{5,2},{6,1},{7,0},{8,15},{9,14},{10,... | collective-permute-start | bytes 258056 | tf_op jit(solution)/shard_map/ppermute | solution.py:408
  7.9 11.0 %collective-permute-start.4 = (f32[21,8,128]{2,1,0:T(8,128)S(1)}, f32[21,8,128]{2,1,0:T(8,128)S(1)}, u32[]{:S(2)}, u32[]{:S(2)}) collective-permute-start(f32[21,8,128]{2,1,0:T(8,128)S(1)} %get-tuple-element.25), channel_id=1, source_target_pairs={{0,2},{1,3},{2,0},{3,1},{4,6},{5,7},{6,4},{7,5},{8,10},{9,11},{10,... | collective-permute-start | bytes 258056 | tf_op jit(solution)/shard_map/ppermute | solution.py:408
  7.9 11.1 %collective-permute-start.5 = (f32[21,8,128]{2,1,0:T(8,128)S(1)}, f32[21,8,128]{2,1,0:T(8,128)S(1)}, u32[]{:S(2)}, u32[]{:S(2)}) collective-permute-start(f32[21,8,128]{2,1,0:T(8,128)S(1)} %get-tuple-element.26), channel_id=1, source_target_pairs={{0,3},{1,2},{2,1},{3,0},{4,7},{5,6},{6,5},{7,4},{8,11},{9,10},{10,... | collective-permute-start | bytes 258056 | tf_op jit(solution)/shard_map/ppermute | solution.py:408
  13.9 11.6 %collective-permute-start.6 = (f32[2,21,8,128]{3,2,1,0:T(8,128)S(1)}, f32[2,21,8,128]{3,2,1,0:T(8,128)S(1)}, u32[]{:S(2)}, u32[]{:S(2)}) collective-permute-start(f32[2,21,8,128]{3,2,1,0:T(8,128)S(1)} %get-tuple-element.27), channel_id=1, source_target_pairs={{0,4},{1,5},{2,6},{3,7},{4,0},{5,1},{6,2},{7,3},{8,12},{9,13},{10,... | collective-permute-start | bytes 516104 | tf_op jit(solution)/shard_map/ppermute | solution.py:408
  17.6 7.9 %collective-permute-start.9 = (f32[2,21,8,128]{3,2,1,0:T(8,128)S(1)}, f32[2,21,8,128]{3,2,1,0:T(8,128)S(1)}, u32[]{:S(2)}, u32[]{:S(2)}) collective-permute-start(f32[2,21,8,128]{3,2,1,0:T(8,128)S(1)} %get-tuple-element.30), channel_id=1, source_target_pairs={{0,8},{1,9},{2,2},{3,3},{4,4},{5,5},{8,16},{9,17},{10,10},{11,11},... | collective-permute-start | bytes 516104 | tf_op jit(solution)/shard_map/ppermute | solution.py:408
  18.9 2.6 %collective-permute-start.3 = (f32[21,8,128]{2,1,0:T(8,128)S(1)}, f32[21,8,128]{2,1,0:T(8,128)S(1)}, u32[]{:S(2)}, u32[]{:S(2)}) collective-permute-start(f32[21,8,128]{2,1,0:T(8,128)S(1)} %get-tuple-element.24), channel_id=1, source_target_pairs={{0,1},{1,0},{2,3},{3,2},{4,5},{5,4},{6,7},{7,6},{8,9},{9,8},{10,11... | collective-permute-start | bytes 258056 | tf_op jit(solution)/shard_map/ppermute | solution.py:408
  19.0 5.9 %collective-permute-start.7 = (f32[21,8,128]{2,1,0:T(8,128)S(1)}, f32[21,8,128]{2,1,0:T(8,128)S(1)}, u32[]{:S(2)}, u32[]{:S(2)}) collective-permute-start(f32[21,8,128]{2,1,0:T(8,128)S(1)} %get-tuple-element.28), channel_id=1, source_target_pairs={{0,5},{1,4},{2,7},{3,6},{4,1},{5,0},{6,3},{7,2},{8,13},{9,12},{10,... | collective-permute-start | bytes 258056 | tf_op jit(solution)/shard_map/ppermute | solution.py:408
  19.1 6.4 %collective-permute-start.8 = (f32[21,8,128]{2,1,0:T(8,128)S(1)}, f32[21,8,128]{2,1,0:T(8,128)S(1)}, u32[]{:S(2)}, u32[]{:S(2)}) collective-permute-start(f32[21,8,128]{2,1,0:T(8,128)S(1)} %get-tuple-element.29), channel_id=1, source_target_pairs={{0,64},{1,65},{2,66},{3,67},{4,68},{5,69},{6,70},{7,71},{8,72},{9,... | collective-permute-start | bytes 258056 | tf_op jit(solution)/shard_map/ppermute | solution.py:408
  28.4 13.7 %collective-permute-start.12 = (f32[480,128]{1,0:T(8,128)S(1)}, f32[480,128]{1,0:T(8,128)S(1)}, u32[]{:S(2)}, u32[]{:S(2)}) collective-permute-start(f32[480,128]{1,0:T(8,128)S(1)} %get-tuple-element.35), channel_id=1, source_target_pairs={{0,8},{8,0},{16,24},{24,16},{32,40},{40,32},{48,56},{56,48},{64,72... | collective-permute-start | bytes 737288 | tf_op jit(solution)/shard_map/ppermute | solution.py:408
  28.9 13.2 %collective-permute-start.13 = (f32[480,128]{1,0:T(8,128)S(1)}, f32[480,128]{1,0:T(8,128)S(1)}, u32[]{:S(2)}, u32[]{:S(2)}) collective-permute-start(f32[480,128]{1,0:T(8,128)S(1)} %get-tuple-element.36), channel_id=1, source_target_pairs={{0,120},{8,16},{16,8},{24,32},{32,24},{40,48},{48,40},{56,64},{64,... | collective-permute-start | bytes 737288 | tf_op jit(solution)/shard_map/ppermute | solution.py:408
  34.4 3.8 %collective-permute-start.10 = (f32[240,128]{1,0:T(8,128)S(1)}, f32[240,128]{1,0:T(8,128)S(1)}, u32[]{:S(2)}, u32[]{:S(2)}) collective-permute-start(f32[240,128]{1,0:T(8,128)S(1)} %get-tuple-element.33), channel_id=1, source_target_pairs={{0,1},{1,0},{2,3},{3,2},{4,5},{5,4},{6,7},{7,6},{8,9},{9,8},{10,11... | collective-permute-start | bytes 368648 | tf_op jit(solution)/shard_map/ppermute | solution.py:408
  34.4 5.5 %collective-permute-start.11 = (f32[240,128]{1,0:T(8,128)S(1)}, f32[240,128]{1,0:T(8,128)S(1)}, u32[]{:S(2)}, u32[]{:S(2)}) collective-permute-start(f32[240,128]{1,0:T(8,128)S(1)} %get-tuple-element.34), channel_id=1, source_target_pairs={{0,7},{1,2},{2,1},{3,4},{4,3},{5,6},{6,5},{7,0},{8,15},{9,10},{10,... | collective-permute-start | bytes 368648 | tf_op jit(solution)/shard_map/ppermute | solution.py:408

commit v4 on v3

--- a/solution.py
+++ b/solution.py
@@ -38,12 +38,23 @@
     return high, mid, low
 
 
-def pick(choice, values):
+def added(terms):
     total = None
-    for part in reversed(split3(values)):
-        term = jnp.dot(choice, part, preferred_element_type=jnp.float32)
+    for term in terms:
         total = term if total is None else total + term
     return total
+
+
+def pick(choice, values):
+    return added(
+        jnp.dot(choice, part, preferred_element_type=jnp.float32) for part in reversed(split3(values))
+    )
+
+
+def weighted(values, weights):
+    return added(
+        jnp.dot(part, weights, preferred_element_type=jnp.float32) for part in reversed(split3(values))
+    )
 
 
 def place():
@@ -295,12 +306,12 @@
     return flux
 
 
-def sweep(load, count, normal, emit):
+def sweep(load, first, last, normal, emit):
     every = range(FIELDS)
-    cells = {cell: load(cell) for cell in (-3, -2, -1, 0)}
-    below = [interface(cells[-3][f], cells[-2][f], cells[-1][f], cells[0][f]) for f in every]
+    cells = {cell: load(cell) for cell in range(first - 3, first + 1)}
+    below = [interface(*[cells[cell][f] for cell in range(first - 3, first + 1)]) for f in every]
     left = flux_below = None
-    for cell in range(-1, count + 1):
+    for cell in range(first - 1, last + 2):
         cells[cell + 2] = load(cell + 2)
         above = [
             interface(cells[cell - 1][f], cells[cell][f], cells[cell + 1][f], cells[cell + 2][f]) for f in every
@@ -315,30 +326,44 @@
         below = above
 
 
-def z_kernel(state_ref, prim_ref, out_ref):
+def block_rows(f, cell, block):
+    return pl.ds(pl.multiple_of((f * CX + cell) * CY + block * 8, 8), 8)
+
+
+def inner_kernel(state_ref, prim_ref, out_ref):
     def rolled(value, shift):
         return pltpu.roll(value, shift % CZ, 1)
 
-    def step(cell_x, carry):
-        for up in range(CY // 8):
-            starts = [
-                pl.multiple_of((f * CX + cell_x) * CY + up * 8, 8) for f in range(FIELDS)
-            ]
-            here = [prim_ref[pl.ds(start, 8), :] for start in starts]
-            lows, highs = [], []
-            for value in here:
-                after = rolled(value, -1)
-                above = interface(rolled(value, 1), value, after, rolled(after, -1))
-                low, high = edges(value, rolled(above, 1), above)
-                lows.append(rolled(low, -1))
-                highs.append(high)
-            flux = face_flux(highs, lows, 3)
+    ahead = (iota((CZ, CZ), 0) - iota((CZ, CZ), 1)) % CZ
+    outer = jnp.where((ahead == CZ - 1) | (ahead == 2), -1.0, 0.0)
+    weights = jnp.where(ahead <= 1, 7.0, outer).astype(jnp.bfloat16)
+    lows, highs = [], []
+    for f in range(FIELDS):
+        value = prim_ref[pl.ds(f * CX * CY, CX * CY), :]
+        after = rolled(value, -1)
+        mean = weighted(value, weights) * (1.0 / 12.0)
+        above = jnp.minimum(jnp.maximum(mean, jnp.minimum(value, after)), jnp.maximum(value, after))
+        low, high = edges(value, rolled(above, 1), above)
+        lows.append(rolled(low, -1))
+        highs.append(high)
+    flux = face_flux(highs, lows, 3)
+    for f in range(FIELDS):
+        rows = pl.ds(f * CX * CY, CX * CY)
+        out_ref[rows, :] = state_ref[rows, :] - 0.1 * (flux[f] - rolled(flux[f], 1))
+
+    def step(block, carry):
+        def load(cell):
+            return [prim_ref[block_rows(f, cell, block), :] for f in range(FIELDS)]
+
+        def emit(cell, change):
             for f in range(FIELDS):
-                change = flux[f] - rolled(flux[f], 1)
-                out_ref[pl.ds(starts[f], 8), :] = state_ref[pl.ds(starts[f], 8), :] - 0.1 * change
+                rows = block_rows(f, cell, block)
+                out_ref[rows, :] = out_ref[rows, :] - 0.1 * change[f]
+
+        sweep(load, 3, CX - 4, 1, emit)
         return carry
 
-    lax.fori_loop(0, CX, step, 0, unroll=2)
+    lax.fori_loop(0, CY // 8, step, 0)
 
 
 def side(first_ref, second_ref, odd, before, rows):
@@ -362,14 +387,18 @@
                 rows = pl.ds(pl.multiple_of((f * CY + cell) * CX + block * 8, 8), 8)
                 change_ref[rows, :] = change[f]
 
-        sweep(load, CY, 2, emit)
+        sweep(load, 0, CY - 1, 2, emit)
         return carry
 
     lax.fori_loop(0, CX // 8, step, 0)
 
 
-def x_kernel(before_ref, prim_ref, change_ref, first_ref, second_ref, out_ref):
+def x_kernel(before_ref, prim_ref, change_ref, first_ref, second_ref, out_hbm, out_ref, sems):
     odd = lax.axis_index("node") % 2 == 1
+
+    def leaving(block, field):
+        part = (field, slice(None), pl.ds(pl.multiple_of(block * 8, 8), 8))
+        return pltpu.make_async_copy(out_ref.at[part], out_hbm.at[part], sems.at[block, field])
 
     def step(block, carry):
         def load(cell):
@@ -377,20 +406,28 @@
                 layer = cell + 3 if cell < 0 else cell - CX
                 rows = [pl.ds(pl.multiple_of((f * 3 + layer) * CY + block * 8, 8), 8) for f in range(FIELDS)]
                 return [side(first_ref, second_ref, odd, cell < 0, row) for row in rows]
-            return [
-                prim_ref[pl.ds(pl.multiple_of((f * CX + cell) * CY + block * 8, 8), 8), :] for f in range(FIELDS)
-            ]
-
-        def emit(cell, change):
+            return [prim_ref[block_rows(f, cell, block), :] for f in range(FIELDS)]
+
+        def emit(cell, change=None):
             for f in range(FIELDS):
-                rows = pl.ds(pl.multiple_of((f * CX + cell) * CY + block * 8, 8), 8)
-                other = change_ref[pl.ds((f * CY + block * 8) * CX + cell, 8, stride=CX), :]
-                out_ref[rows, :] = before_ref[rows, :] - 0.1 * (change[f] + other)
-
-        sweep(load, CX, 1, emit)
+                total = change_ref[pl.ds((f * CY + block * 8) * CX + cell, 8, stride=CX), :]
+                if change is not None:
+                    total = total + change[f]
+                value = before_ref[block_rows(f, cell, block), :] - 0.1 * total
+                out_ref[f, cell, pl.ds(pl.multiple_of(block * 8, 8), 8), :] = value
+
+        sweep(load, 0, 2, 1, emit)
+        for cell in range(3, CX - 3):
+            emit(cell)
+        sweep(load, CX - 3, CX - 1, 1, emit)
+        for field in range(FIELDS):
+            leaving(block, field).start()
         return carry
 
     lax.fori_loop(0, CY // 8, step, 0)
+    for block in range(CY // 8):
+        for field in range(FIELDS):
+            leaving(block, field).wait()
 
 
 def stage(kernel, name, *operands):
@@ -400,6 +437,19 @@
         jax.ShapeDtypeStruct((ROWS, CZ), jnp.float32),
         [VMEM] * len(operands),
         cost_estimate=pl.CostEstimate(flops=20_000_000, bytes_accessed=4_000_000, transcendentals=200_000),
+    )(*operands)
+
+
+def finish(*operands):
+    shape = (FIELDS, CX, CY, CZ)
+    return pl.pallas_call(
+        x_kernel,
+        out_shape=jax.ShapeDtypeStruct(shape, jnp.float32),
+        in_specs=[VMEM] * len(operands),
+        out_specs=pl.BlockSpec(memory_space=pl.ANY),
+        scratch_shapes=[pltpu.VMEM(shape, jnp.float32), pltpu.SemaphoreType.DMA((CY // 8, FIELDS))],
+        compiler_params=pltpu.CompilerParams(vmem_limit_bytes=VMEM_LIMIT),
+        name="flux_first",
     )(*operands)
 
 
@@ -442,10 +492,9 @@
     x_second = shifted(x_second, "node", 16, lambda i: (i + 1) % 16 if i % 2 else (i - 1) % 16)
     y_first = shifted(y_first, "dev", 8, lambda i: i ^ 1)
     y_second = shifted(y_second, "dev", 8, lambda i: (i + 1) % 8 if i % 2 else (i - 1) % 8)
-    result = stage(z_kernel, "flux_third", state, prim)
+    result = stage(inner_kernel, "flux_inner", state, prim)
     change = stage(y_kernel, "flux_second", prim, y_first, y_second)
-    result = stage(x_kernel, "flux_first", result, prim, change, x_first, x_second)
-    return result.reshape(FIELDS, CX, CY, CZ)
+    return finish(result, prim, change, x_first, x_second)
 
 
 def solution(mesh):

time: 46.1 us -> 45.1 us (0.978)
  Pallas kernels: 13 us -> 12.1 us
    pallas_call x3 -> x2, Pallas kernels: 9.12 us -> 5.86 us  [stage(): call(kernel, name, jax.ShapeDtypeStruct((ROWS, CZ), jnp.float32), [VMEM]...]
    pallas_call x0 -> x1, Pallas kernels: none -> 2.35 us  [finish(): pl.pallas_call(x_kernel, out_shape=jax.ShapeDtypeStruct(shape, jnp.float3...]
where the time goes in v4:
time: 45.1 us; the launch traced here: 44.5 us
  starting transfers between devices  21.7 us (48%)
  Pallas kernels  12.1 us (27%)
  waiting for transfers between devices  8.62 us (19%)
  local copies, waits for them, and re-layouts  1.97 us (4%)
    ppermute x14, starting transfers between devices, shifted(): return lax.ppermute(value, axes, [pair for pair in pairs if pair[1] >= 0])  21.7 us
    ppermute x14, waiting for transfers between devices, shifted(): return lax.ppermute(value, axes, [pair for pair in pairs if pair[1] >= 0])  8.62 us
    pallas_call x2, Pallas kernels, stage(): call(kernel, name, jax.ShapeDtypeStruct((ROWS, CZ), jnp.float32), [VMEM]...  5.86 us
    pallas_call x1, Pallas kernels, unpack(): call(unpack_kernel, 'unpack', (grid_rows, grid_rows, x_side, x_side, y_si...  2.83 us
    pallas_call x1, Pallas kernels, finish(): pl.pallas_call(x_kernel, out_shape=jax.ShapeDtypeStruct(shape, jnp.float3...  2.35 us
    unnamed x4, local copies, waits for them, and re-layouts  1.97 us
  transfers between devices with their start and end apart: 14, of which 5 were waited for; matrix products, arithmetic and copies ran while one was open for 0% of the time, Pallas kernels for 14%

profile of v4, /device:TPU:0, one launch (start us, length us, event | category | flops | bytes accessed | tf_op | source)
XLA Modules:
  0.0 44.5 jit_solution(13446710051829247277)
XLA Ops:
  0.0 1.3 %copy-done = f32[128,5,512]{2,0,1:T(8,128)S(1)} copy-done((f32[128,5,512]{2,0,1:T(8,128)S(1)}, f32[128,5,512]{2,0,1:T(8,128)}, u32[]{:S(2)}) %copy-start) | copy-done | bytes 1310744
  1.3 0.7 %copy-done.1 = s32[128]{0:T(128)S(1)} copy-done((s32[128]{0:T(128)S(1)}, s32[128]{0:T(128)}, u32[]{:S(2)}) %copy-start.1) | copy-done | bytes 536
  2.0 0.5 %pack_early.1 = (f32[21,8,128]{2,1,0:T(8,128)S(1)}, f32[21,8,128]{2,1,0:T(8,128)S(1)}, f32[21,8,128]{2,1,0:T(8,128)S(1)}, f32[21,8,128]{2,1,0:T(8,128)S(1)}, f32[2,21,8,128]{3,2,1,0:T(8,128)S(1)}) custom-call(s32[1,128]{1,0:T(1,128)S(1)} %bitcast.5, f32[5,128,512]{2,1,0:T(8,128)S(1)} %bitcast.2), custom_call_target="tpu_custom_call" | custom-call | tf_op jit(solution)/shard_map/pack_early/pallas_call | solution.py:151
  2.5 3.3 %collective-permute-start = (f32[2,21,8,128]{3,2,1,0:T(8,128)S(1)}, f32[2,21,8,128]{3,2,1,0:T(8,128)S(1)}, u32[]{:S(2)}, u32[]{:S(2)}) collective-permute-start(f32[2,21,8,128]{3,2,1,0:T(8,128)S(1)} %get-tuple-element.21), channel_id=1, source_target_pairs={{0,4},{1,5},{2,6},{3,7},{4,12},{5,13},{6,14},{7,15},{8,0},{9,1},{1... | collective-permute-start | bytes 516104 | tf_op jit(solution)/shard_map/ppermute | solution.py:458
  5.8 1.7 %collective-permute-start.1 = (f32[21,8,128]{2,1,0:T(8,128)S(1)}, f32[21,8,128]{2,1,0:T(8,128)S(1)}, u32[]{:S(2)}, u32[]{:S(2)}) collective-permute-start(f32[21,8,128]{2,1,0:T(8,128)S(1)} %get-tuple-element.22), channel_id=1, source_target_pairs={{0,6},{1,7},{2,4},{3,5},{4,2},{5,3},{6,0},{7,1},{8,14},{9,15},{10,... | collective-permute-start | bytes 258056 | tf_op jit(solution)/shard_map/ppermute | solution.py:458
  7.6 0.4 collective-permute-start.2
  7.9 0.0 collective-permute-start.4
  7.9 2.6 %collective-permute-start.5 = (f32[21,8,128]{2,1,0:T(8,128)S(1)}, f32[21,8,128]{2,1,0:T(8,128)S(1)}, u32[]{:S(2)}, u32[]{:S(2)}) collective-permute-start(f32[21,8,128]{2,1,0:T(8,128)S(1)} %get-tuple-element.26), channel_id=1, source_target_pairs={{0,3},{1,2},{2,1},{3,0},{4,7},{5,6},{6,5},{7,4},{8,11},{9,10},{10,... | collective-permute-start | bytes 258056 | tf_op jit(solution)/shard_map/ppermute | solution.py:458
  10.5 1.0 %collective-permute-done.1.six_ref = f32[21,8,128]{2,1,0:T(8,128)S(1)} collective-permute-done((f32[21,8,128]{2,1,0:T(8,128)S(1)}, f32[21,8,128]{2,1,0:T(8,128)S(1)}, u32[]{:S(2)}, u32[]{:S(2)}) %collective-permute-start.1) | collective-permute-done | bytes 86048 | tf_op jit(solution)/shard_map/ppermute | solution.py:458
  11.5 1.8 %collective-permute-done.2.seven_ref = f32[21,8,128]{2,1,0:T(8,128)S(1)} collective-permute-done((f32[21,8,128]{2,1,0:T(8,128)S(1)}, f32[21,8,128]{2,1,0:T(8,128)S(1)}, u32[]{:S(2)}, u32[]{:S(2)}) %collective-permute-start.2) | collective-permute-done | bytes 86048 | tf_op jit(solution)/shard_map/ppermute | solution.py:458
  13.4 0.0 collective-permute-done.relay_ref
  13.4 0.5 %pack_late.1 = (f32[21,8,128]{2,1,0:T(8,128)S(1)}, f32[2,21,8,128]{3,2,1,0:T(8,128)S(1)}, f32[21,8,128]{2,1,0:T(8,128)S(1)}, f32[21,8,128]{2,1,0:T(8,128)S(1)}, f32[2,21,8,128]{3,2,1,0:T(8,128)S(1)}) custom-call(s32[1,128]{1,0:T(1,128)S(1)} %bitcast.6, f32[5,128,512]{2,1,0:T(8,128)S(1)} %bitcast.3, f32[2,21,8,128]{3,2,1,0:T(8,128)S(1)} %collective-permute-done.relay_ref, ...), custom_call_target="tpu_custom_call" | custom-call | tf_op jit(solution)/shard_map/pack_late/pallas_call | solution.py:155
  13.9 3.7 %collective-permute-start.6 = (f32[2,21,8,128]{3,2,1,0:T(8,128)S(1)}, f32[2,21,8,128]{3,2,1,0:T(8,128)S(1)}, u32[]{:S(2)}, u32[]{:S(2)}) collective-permute-start(f32[2,21,8,128]{3,2,1,0:T(8,128)S(1)} %get-tuple-element.27), channel_id=1, source_target_pairs={{0,4},{1,5},{2,6},{3,7},{4,0},{5,1},{6,2},{7,3},{8,12},{9,13},{10,... | collective-permute-start | bytes 516104 | tf_op jit(solution)/shard_map/ppermute | solution.py:458
  17.6 1.3 %collective-permute-start.9 = (f32[2,21,8,128]{3,2,1,0:T(8,128)S(1)}, f32[2,21,8,128]{3,2,1,0:T(8,128)S(1)}, u32[]{:S(2)}, u32[]{:S(2)}) collective-permute-start(f32[2,21,8,128]{3,2,1,0:T(8,128)S(1)} %get-tuple-element.30), channel_id=1, source_target_pairs={{0,8},{1,9},{2,2},{3,3},{4,4},{5,5},{8,16},{9,17},{10,10},{11,11},... | collective-permute-start | bytes 516104 | tf_op jit(solution)/shard_map/ppermute | solution.py:458
  18.9 0.1 collective-permute-start.3
  19.0 0.0 collective-permute-done.4.two_ref
  19.0 0.1 collective-permute-start.7
  19.1 2.4 %collective-permute-start.8 = (f32[21,8,128]{2,1,0:T(8,128)S(1)}, f32[21,8,128]{2,1,0:T(8,128)S(1)}, u32[]{:S(2)}, u32[]{:S(2)}) collective-permute-start(f32[21,8,128]{2,1,0:T(8,128)S(1)} %get-tuple-element.29), channel_id=1, source_target_pairs={{0,64},{1,65},{2,66},{3,67},{4,68},{5,69},{6,70},{7,71},{8,72},{9,... | collective-permute-start | bytes 258056 | tf_op jit(solution)/shard_map/ppermute | solution.py:458
  21.5 3.4 %collective-permute-done.7.five_ref = f32[21,8,128]{2,1,0:T(8,128)S(1)} collective-permute-done((f32[21,8,128]{2,1,0:T(8,128)S(1)}, f32[21,8,128]{2,1,0:T(8,128)S(1)}, u32[]{:S(2)}, u32[]{:S(2)}) %collective-permute-start.7) | collective-permute-done | bytes 86048 | tf_op jit(solution)/shard_map/ppermute | solution.py:458
  24.9 0.7 %collective-permute-done.8.far_ref = f32[21,8,128]{2,1,0:T(8,128)S(1)} collective-permute-done((f32[21,8,128]{2,1,0:T(8,128)S(1)}, f32[21,8,128]{2,1,0:T(8,128)S(1)}, u32[]{:S(2)}, u32[]{:S(2)}) %collective-permute-start.8) | collective-permute-done | bytes 86048 | tf_op jit(solution)/shard_map/ppermute | solution.py:458
  25.5 0.0 collective-permute-done.6.four_ref
  25.5 0.0 collective-permute-done.9.on_ref
  25.5 2.8 %unpack.1 = (f32[2560,128]{1,0:T(8,128)S(1)}, f32[2560,128]{1,0:T(8,128)S(1)}, f32[480,128]{1,0:T(8,128)S(1)}, f32[480,128]{1,0:T(8,128)S(1)}, f32[240,128]{1,0:T(8,128)S(1)}, /*index=5*/f32[240,128]{1,0:T(8,128)S(1)}) custom-call(s32[1,128]{1,0:T(1,128)S(1)} %bitcast.7, f32[5,128,512]{2,1,0:T(8,128)S(1)} %bitcast.4, ...), custom_call_target="tpu_custom_call" | custom-call | tf_op jit(solution)/shard_map/unpack/pallas_call | solution.py:249
  28.4 0.5 %collective-permute-start.12 = (f32[480,128]{1,0:T(8,128)S(1)}, f32[480,128]{1,0:T(8,128)S(1)}, u32[]{:S(2)}, u32[]{:S(2)}) collective-permute-start(f32[480,128]{1,0:T(8,128)S(1)} %get-tuple-element.35), channel_id=1, source_target_pairs={{0,8},{8,0},{16,24},{24,16},{32,40},{40,32},{48,56},{56,48},{64,72... | collective-permute-start | bytes 737288 | tf_op jit(solution)/shard_map/ppermute | solution.py:458
  28.9 5.5 %collective-permute-start.13 = (f32[480,128]{1,0:T(8,128)S(1)}, f32[480,128]{1,0:T(8,128)S(1)}, u32[]{:S(2)}, u32[]{:S(2)}) collective-permute-start(f32[480,128]{1,0:T(8,128)S(1)} %get-tuple-element.36), channel_id=1, source_target_pairs={{0,120},{8,16},{16,8},{24,32},{32,24},{40,48},{48,40},{56,64},{64,... | collective-permute-start | bytes 737288 | tf_op jit(solution)/shard_map/ppermute | solution.py:458
  34.4 0.0 collective-permute-start.10
  34.4 0.0 collective-permute-start.11
  34.5 3.7 %flux_inner.1.before_ref = f32[2560,128]{1,0:T(8,128)S(1)} custom-call(f32[2560,128]{1,0:T(8,128)S(1)} %get-tuple-element.31.state_ref, f32[2560,128]{1,0:T(8,128)S(1)} %get-tuple-element.32.prim_ref), custom_call_target="tpu_custom_call" | custom-call | flops 20000000 | bytes 4000000 | tf_op jit(solution)/shard_map/flux_inner/pallas_call | solution.py:434
  38.2 0.0 collective-permute-done.10.first_ref
  38.2 1.7 %collective-permute-done.11.second_ref = f32[240,128]{1,0:T(8,128)S(1)} collective-permute-done((f32[240,128]{1,0:T(8,128)S(1)}, f32[240,128]{1,0:T(8,128)S(1)}, u32[]{:S(2)}, u32[]{:S(2)}) %collective-permute-start.11) | collective-permute-done | bytes 122912 | tf_op jit(solution)/shard_map/ppermute | solution.py:458
  40.0 2.1 %flux_second.1.change_ref = f32[2560,128]{1,0:T(8,128)S(1)} custom-call(f32[2560,128]{1,0:T(8,128)S(1)} %get-tuple-element.32.prim_ref, f32[240,128]{1,0:T(8,128)S(1)} %collective-permute-done.10.first_ref, f32[240,128]{1,0:T(8,128)S(1)} %collective-permute-done.11.second_ref), custom_call_target="tpu_custom_call" | custom-call | flops 20000000 | bytes 4000000 | tf_op jit(solution)/shard_map/flux_second/pallas_call | solution.py:434
  42.1 2.4 %flux_first.1 = f32[5,16,32,128]{3,2,1,0:T(8,128)} custom-call(f32[2560,128]{1,0:T(8,128)S(1)} %flux_inner.1.before_ref, f32[2560,128]{1,0:T(8,128)S(1)} %get-tuple-element.32.prim_ref, f32[2560,128]{1,0:T(8,128)S(1)} %flux_second.1.change_ref, f32[480,128]{1,0:T(8,128)S(1)} %collective-permute-done.12.first_ref, ...), custom_call_target="tpu_custom_call" | custom-call | tf_op jit(solution)/shard_map/flux_first/pallas_call | solution.py:445
  (6 shorter events, 0.0 us)
Async XLA Ops:
  0.0 1.3 %copy-start = (f32[128,5,512]{2,0,1:T(8,128)S(1)}, f32[128,5,512]{2,0,1:T(8,128)}, u32[]{:S(2)}) copy-start(f32[128,5,512]{2,0,1:T(8,128)} %param.2) | copy-start | bytes 3932164
  1.3 0.7 %copy-start.1 = (s32[128]{0:T(128)S(1)}, s32[128]{0:T(128)}, u32[]{:S(2)}) copy-start(s32[128]{0:T(128)} %param.3) | copy-start | bytes 1540
  2.5 10.9 %collective-permute-start = (f32[2,21,8,128]{3,2,1,0:T(8,128)S(1)}, f32[2,21,8,128]{3,2,1,0:T(8,128)S(1)}, u32[]{:S(2)}, u32[]{:S(2)}) collective-permute-start(f32[2,21,8,128]{3,2,1,0:T(8,128)S(1)} %get-tuple-element.21), channel_id=1, source_target_pairs={{0,4},{1,5},{2,6},{3,7},{4,12},{5,13},{6,14},{7,15},{8,0},{9,1},{1... | collective-permute-start | bytes 516104 | tf_op jit(solution)/shard_map/ppermute | solution.py:458
  5.8 5.7 %collective-permute-start.1 = (f32[21,8,128]{2,1,0:T(8,128)S(1)}, f32[21,8,128]{2,1,0:T(8,128)S(1)}, u32[]{:S(2)}, u32[]{:S(2)}) collective-permute-start(f32[21,8,128]{2,1,0:T(8,128)S(1)} %get-tuple-element.22), channel_id=1, source_target_pairs={{0,6},{1,7},{2,4},{3,5},{4,2},{5,3},{6,0},{7,1},{8,14},{9,15},{10,... | collective-permute-start | bytes 258056 | tf_op jit(solution)/shard_map/ppermute | solution.py:458
  7.6 5.8 %collective-permute-start.2 = (f32[21,8,128]{2,1,0:T(8,128)S(1)}, f32[21,8,128]{2,1,0:T(8,128)S(1)}, u32[]{:S(2)}, u32[]{:S(2)}) collective-permute-start(f32[21,8,128]{2,1,0:T(8,128)S(1)} %get-tuple-element.23), channel_id=1, source_target_pairs={{0,7},{1,6},{2,5},{3,4},{4,3},{5,2},{6,1},{7,0},{8,15},{9,14},{10,... | collective-permute-start | bytes 258056 | tf_op jit(solution)/shard_map/ppermute | solution.py:458
  7.9 11.0 %collective-permute-start.4 = (f32[21,8,128]{2,1,0:T(8,128)S(1)}, f32[21,8,128]{2,1,0:T(8,128)S(1)}, u32[]{:S(2)}, u32[]{:S(2)}) collective-permute-start(f32[21,8,128]{2,1,0:T(8,128)S(1)} %get-tuple-element.25), channel_id=1, source_target_pairs={{0,2},{1,3},{2,0},{3,1},{4,6},{5,7},{6,4},{7,5},{8,10},{9,11},{10,... | collective-permute-start | bytes 258056 | tf_op jit(solution)/shard_map/ppermute | solution.py:458
  7.9 11.1 %collective-permute-start.5 = (f32[21,8,128]{2,1,0:T(8,128)S(1)}, f32[21,8,128]{2,1,0:T(8,128)S(1)}, u32[]{:S(2)}, u32[]{:S(2)}) collective-permute-start(f32[21,8,128]{2,1,0:T(8,128)S(1)} %get-tuple-element.26), channel_id=1, source_target_pairs={{0,3},{1,2},{2,1},{3,0},{4,7},{5,6},{6,5},{7,4},{8,11},{9,10},{10,... | collective-permute-start | bytes 258056 | tf_op jit(solution)/shard_map/ppermute | solution.py:458
  13.9 11.6 %collective-permute-start.6 = (f32[2,21,8,128]{3,2,1,0:T(8,128)S(1)}, f32[2,21,8,128]{3,2,1,0:T(8,128)S(1)}, u32[]{:S(2)}, u32[]{:S(2)}) collective-permute-start(f32[2,21,8,128]{3,2,1,0:T(8,128)S(1)} %get-tuple-element.27), channel_id=1, source_target_pairs={{0,4},{1,5},{2,6},{3,7},{4,0},{5,1},{6,2},{7,3},{8,12},{9,13},{10,... | collective-permute-start | bytes 516104 | tf_op jit(solution)/shard_map/ppermute | solution.py:458
  17.6 7.9 %collective-permute-start.9 = (f32[2,21,8,128]{3,2,1,0:T(8,128)S(1)}, f32[2,21,8,128]{3,2,1,0:T(8,128)S(1)}, u32[]{:S(2)}, u32[]{:S(2)}) collective-permute-start(f32[2,21,8,128]{3,2,1,0:T(8,128)S(1)} %get-tuple-element.30), channel_id=1, source_target_pairs={{0,8},{1,9},{2,2},{3,3},{4,4},{5,5},{8,16},{9,17},{10,10},{11,11},... | collective-permute-start | bytes 516104 | tf_op jit(solution)/shard_map/ppermute | solution.py:458
  18.9 2.6 %collective-permute-start.3 = (f32[21,8,128]{2,1,0:T(8,128)S(1)}, f32[21,8,128]{2,1,0:T(8,128)S(1)}, u32[]{:S(2)}, u32[]{:S(2)}) collective-permute-start(f32[21,8,128]{2,1,0:T(8,128)S(1)} %get-tuple-element.24), channel_id=1, source_target_pairs={{0,1},{1,0},{2,3},{3,2},{4,5},{5,4},{6,7},{7,6},{8,9},{9,8},{10,11... | collective-permute-start | bytes 258056 | tf_op jit(solution)/shard_map/ppermute | solution.py:458
  19.0 5.9 %collective-permute-start.7 = (f32[21,8,128]{2,1,0:T(8,128)S(1)}, f32[21,8,128]{2,1,0:T(8,128)S(1)}, u32[]{:S(2)}, u32[]{:S(2)}) collective-permute-start(f32[21,8,128]{2,1,0:T(8,128)S(1)} %get-tuple-element.28), channel_id=1, source_target_pairs={{0,5},{1,4},{2,7},{3,6},{4,1},{5,0},{6,3},{7,2},{8,13},{9,12},{10,... | collective-permute-start | bytes 258056 | tf_op jit(solution)/shard_map/ppermute | solution.py:458
  19.1 6.4 %collective-permute-start.8 = (f32[21,8,128]{2,1,0:T(8,128)S(1)}, f32[21,8,128]{2,1,0:T(8,128)S(1)}, u32[]{:S(2)}, u32[]{:S(2)}) collective-permute-start(f32[21,8,128]{2,1,0:T(8,128)S(1)} %get-tuple-element.29), channel_id=1, source_target_pairs={{0,64},{1,65},{2,66},{3,67},{4,68},{5,69},{6,70},{7,71},{8,72},{9,... | collective-permute-start | bytes 258056 | tf_op jit(solution)/shard_map/ppermute | solution.py:458
  28.4 13.7 %collective-permute-start.12 = (f32[480,128]{1,0:T(8,128)S(1)}, f32[480,128]{1,0:T(8,128)S(1)}, u32[]{:S(2)}, u32[]{:S(2)}) collective-permute-start(f32[480,128]{1,0:T(8,128)S(1)} %get-tuple-element.35), channel_id=1, source_target_pairs={{0,8},{8,0},{16,24},{24,16},{32,40},{40,32},{48,56},{56,48},{64,72... | collective-permute-start | bytes 737288 | tf_op jit(solution)/shard_map/ppermute | solution.py:458
  28.9 13.2 %collective-permute-start.13 = (f32[480,128]{1,0:T(8,128)S(1)}, f32[480,128]{1,0:T(8,128)S(1)}, u32[]{:S(2)}, u32[]{:S(2)}) collective-permute-start(f32[480,128]{1,0:T(8,128)S(1)} %get-tuple-element.36), channel_id=1, source_target_pairs={{0,120},{8,16},{16,8},{24,32},{32,24},{40,48},{48,40},{56,64},{64,... | collective-permute-start | bytes 737288 | tf_op jit(solution)/shard_map/ppermute | solution.py:458
  34.4 3.8 %collective-permute-start.10 = (f32[240,128]{1,0:T(8,128)S(1)}, f32[240,128]{1,0:T(8,128)S(1)}, u32[]{:S(2)}, u32[]{:S(2)}) collective-permute-start(f32[240,128]{1,0:T(8,128)S(1)} %get-tuple-element.33), channel_id=1, source_target_pairs={{0,1},{1,0},{2,3},{3,2},{4,5},{5,4},{6,7},{7,6},{8,9},{9,8},{10,11... | collective-permute-start | bytes 368648 | tf_op jit(solution)/shard_map/ppermute | solution.py:458
  34.4 5.5 %collective-permute-start.11 = (f32[240,128]{1,0:T(8,128)S(1)}, f32[240,128]{1,0:T(8,128)S(1)}, u32[]{:S(2)}, u32[]{:S(2)}) collective-permute-start(f32[240,128]{1,0:T(8,128)S(1)} %get-tuple-element.34), channel_id=1, source_target_pairs={{0,7},{1,2},{2,1},{3,4},{4,3},{5,6},{6,5},{7,0},{8,15},{9,10},{10,... | collective-permute-start | bytes 368648 | tf_op jit(solution)/shard_map/ppermute | solution.py:458

commit v5 on v4

--- a/solution.py
+++ b/solution.py
@@ -464,7 +464,7 @@
 
 def next_node(device):
     other = hop(device, 1 if device % 8 >= 4 else -1)
-    return other if other >= 0 else device ^ 4
+    return other if other >= 0 else device ^ 6
 
 
 def onward_node(device):

time: 45.1 us -> 44.6 us (0.989)
  waiting for transfers between devices: 8.62 us -> 6.95 us
  starting transfers between devices: 21.7 us -> 22.8 us
    ppermute x14, waiting for transfers between devices: 8.62 us -> 6.95 us  [shifted(): return lax.ppermute(value, axes, [pair for pair in pairs if pair[1] >= 0])]
    ppermute x14, starting transfers between devices: 21.7 us -> 22.8 us  [shifted(): return lax.ppermute(value, axes, [pair for pair in pairs if pair[1] >= 0])]
  transfers between devices with their start and end apart: 14 -> 14, of which waited for: 5 -> 5; matrix products, arithmetic and copies ran while one was open for 0% -> 0% of each run, Pallas kernels for 14% -> 15%
where the time goes in v5:
time: 44.6 us; the launch traced here: 43.9 us
  starting transfers between devices  22.8 us (51%)
  Pallas kernels  12.1 us (27%)
  waiting for transfers between devices  6.95 us (16%)
  local copies, waits for them, and re-layouts  1.97 us (4%)
    ppermute x14, starting transfers between devices, shifted(): return lax.ppermute(value, axes, [pair for pair in pairs if pair[1] >= 0])  22.8 us
    ppermute x14, waiting for transfers between devices, shifted(): return lax.ppermute(value, axes, [pair for pair in pairs if pair[1] >= 0])  6.95 us
    pallas_call x2, Pallas kernels, stage(): call(kernel, name, jax.ShapeDtypeStruct((ROWS, CZ), jnp.float32), [VMEM]...  5.85 us
    pallas_call x1, Pallas kernels, unpack(): call(unpack_kernel, 'unpack', (grid_rows, grid_rows, x_side, x_side, y_si...  2.82 us
    pallas_call x1, Pallas kernels, finish(): pl.pallas_call(x_kernel, out_shape=jax.ShapeDtypeStruct(shape, jnp.float3...  2.35 us
    unnamed x4, local copies, waits for them, and re-layouts  1.97 us
  transfers between devices with their start and end apart: 14, of which 5 were waited for; matrix products, arithmetic and copies ran while one was open for 0% of the time, Pallas kernels for 15%

profile of v5, /device:TPU:0, one launch (start us, length us, event | category | flops | bytes accessed | tf_op | source)
XLA Modules:
  0.0 43.9 jit_solution(9033148915872022156)
XLA Ops:
  0.0 1.3 %copy-done = f32[128,5,512]{2,0,1:T(8,128)S(1)} copy-done((f32[128,5,512]{2,0,1:T(8,128)S(1)}, f32[128,5,512]{2,0,1:T(8,128)}, u32[]{:S(2)}) %copy-start) | copy-done | bytes 1310744
  1.3 0.7 %copy-done.1 = s32[128]{0:T(128)S(1)} copy-done((s32[128]{0:T(128)S(1)}, s32[128]{0:T(128)}, u32[]{:S(2)}) %copy-start.1) | copy-done | bytes 536
  2.0 0.5 %pack_early.1 = (f32[21,8,128]{2,1,0:T(8,128)S(1)}, f32[21,8,128]{2,1,0:T(8,128)S(1)}, f32[21,8,128]{2,1,0:T(8,128)S(1)}, f32[21,8,128]{2,1,0:T(8,128)S(1)}, f32[2,21,8,128]{3,2,1,0:T(8,128)S(1)}) custom-call(s32[1,128]{1,0:T(1,128)S(1)} %bitcast.5, f32[5,128,512]{2,1,0:T(8,128)S(1)} %bitcast.2), custom_call_target="tpu_custom_call" | custom-call | tf_op jit(solution)/shard_map/pack_early/pallas_call | solution.py:151
  2.5 3.1 %collective-permute-start = (f32[2,21,8,128]{3,2,1,0:T(8,128)S(1)}, f32[2,21,8,128]{3,2,1,0:T(8,128)S(1)}, u32[]{:S(2)}, u32[]{:S(2)}) collective-permute-start(f32[2,21,8,128]{3,2,1,0:T(8,128)S(1)} %get-tuple-element.21), channel_id=1, source_target_pairs={{0,6},{1,7},{2,4},{3,5},{4,12},{5,13},{6,14},{7,15},{8,0},{9,1},{1... | collective-permute-start | bytes 516104 | tf_op jit(solution)/shard_map/ppermute | solution.py:458
  5.6 1.9 %collective-permute-start.1 = (f32[21,8,128]{2,1,0:T(8,128)S(1)}, f32[21,8,128]{2,1,0:T(8,128)S(1)}, u32[]{:S(2)}, u32[]{:S(2)}) collective-permute-start(f32[21,8,128]{2,1,0:T(8,128)S(1)} %get-tuple-element.22), channel_id=1, source_target_pairs={{0,6},{1,7},{2,4},{3,5},{4,2},{5,3},{6,0},{7,1},{8,14},{9,15},{10,... | collective-permute-start | bytes 258056 | tf_op jit(solution)/shard_map/ppermute | solution.py:458
  7.6 0.2 collective-permute-start.2
  7.8 0.0 collective-permute-start.4
  7.8 2.6 %collective-permute-start.5 = (f32[21,8,128]{2,1,0:T(8,128)S(1)}, f32[21,8,128]{2,1,0:T(8,128)S(1)}, u32[]{:S(2)}, u32[]{:S(2)}) collective-permute-start(f32[21,8,128]{2,1,0:T(8,128)S(1)} %get-tuple-element.26), channel_id=1, source_target_pairs={{0,3},{1,2},{2,1},{3,0},{4,7},{5,6},{6,5},{7,4},{8,11},{9,10},{10,... | collective-permute-start | bytes 258056 | tf_op jit(solution)/shard_map/ppermute | solution.py:458
  10.3 1.7 %collective-permute-done.1.six_ref = f32[21,8,128]{2,1,0:T(8,128)S(1)} collective-permute-done((f32[21,8,128]{2,1,0:T(8,128)S(1)}, f32[21,8,128]{2,1,0:T(8,128)S(1)}, u32[]{:S(2)}, u32[]{:S(2)}) %collective-permute-start.1) | collective-permute-done | bytes 86048 | tf_op jit(solution)/shard_map/ppermute | solution.py:458
  12.0 1.1 %collective-permute-done.2.seven_ref = f32[21,8,128]{2,1,0:T(8,128)S(1)} collective-permute-done((f32[21,8,128]{2,1,0:T(8,128)S(1)}, f32[21,8,128]{2,1,0:T(8,128)S(1)}, u32[]{:S(2)}, u32[]{:S(2)}) %collective-permute-start.2) | collective-permute-done | bytes 86048 | tf_op jit(solution)/shard_map/ppermute | solution.py:458
  13.2 0.0 collective-permute-done.relay_ref
  13.2 0.5 %pack_late.1 = (f32[21,8,128]{2,1,0:T(8,128)S(1)}, f32[2,21,8,128]{3,2,1,0:T(8,128)S(1)}, f32[21,8,128]{2,1,0:T(8,128)S(1)}, f32[21,8,128]{2,1,0:T(8,128)S(1)}, f32[2,21,8,128]{3,2,1,0:T(8,128)S(1)}) custom-call(s32[1,128]{1,0:T(1,128)S(1)} %bitcast.6, f32[5,128,512]{2,1,0:T(8,128)S(1)} %bitcast.3, f32[2,21,8,128]{3,2,1,0:T(8,128)S(1)} %collective-permute-done.relay_ref, ...), custom_call_target="tpu_custom_call" | custom-call | tf_op jit(solution)/shard_map/pack_late/pallas_call | solution.py:155
  13.7 1.6 %collective-permute-start.6 = (f32[2,21,8,128]{3,2,1,0:T(8,128)S(1)}, f32[2,21,8,128]{3,2,1,0:T(8,128)S(1)}, u32[]{:S(2)}, u32[]{:S(2)}) collective-permute-start(f32[2,21,8,128]{3,2,1,0:T(8,128)S(1)} %get-tuple-element.27), channel_id=1, source_target_pairs={{0,4},{1,5},{2,6},{3,7},{4,0},{5,1},{6,2},{7,3},{8,12},{9,13},{10,... | collective-permute-start | bytes 516104 | tf_op jit(solution)/shard_map/ppermute | solution.py:458
  15.3 2.2 %collective-permute-start.9 = (f32[2,21,8,128]{3,2,1,0:T(8,128)S(1)}, f32[2,21,8,128]{3,2,1,0:T(8,128)S(1)}, u32[]{:S(2)}, u32[]{:S(2)}) collective-permute-start(f32[2,21,8,128]{3,2,1,0:T(8,128)S(1)} %get-tuple-element.30), channel_id=1, source_target_pairs={{0,8},{1,9},{2,2},{3,3},{4,4},{5,5},{8,16},{9,17},{10,10},{11,11},... | collective-permute-start | bytes 516104 | tf_op jit(solution)/shard_map/ppermute | solution.py:458
  17.5 0.1 collective-permute-start.3
  17.6 0.0 collective-permute-done.4.two_ref
  17.6 0.6 %collective-permute-start.7 = (f32[21,8,128]{2,1,0:T(8,128)S(1)}, f32[21,8,128]{2,1,0:T(8,128)S(1)}, u32[]{:S(2)}, u32[]{:S(2)}) collective-permute-start(f32[21,8,128]{2,1,0:T(8,128)S(1)} %get-tuple-element.28), channel_id=1, source_target_pairs={{0,5},{1,4},{2,7},{3,6},{4,1},{5,0},{6,3},{7,2},{8,13},{9,12},{10,... | collective-permute-start | bytes 258056 | tf_op jit(solution)/shard_map/ppermute | solution.py:458
  18.2 3.3 %collective-permute-start.8 = (f32[21,8,128]{2,1,0:T(8,128)S(1)}, f32[21,8,128]{2,1,0:T(8,128)S(1)}, u32[]{:S(2)}, u32[]{:S(2)}) collective-permute-start(f32[21,8,128]{2,1,0:T(8,128)S(1)} %get-tuple-element.29), channel_id=1, source_target_pairs={{0,64},{1,65},{2,66},{3,67},{4,68},{5,69},{6,70},{7,71},{8,72},{9,... | collective-permute-start | bytes 258056 | tf_op jit(solution)/shard_map/ppermute | solution.py:458
  21.5 0.0 collective-permute-done.3.one_ref
  21.5 1.9 %collective-permute-done.7.five_ref = f32[21,8,128]{2,1,0:T(8,128)S(1)} collective-permute-done((f32[21,8,128]{2,1,0:T(8,128)S(1)}, f32[21,8,128]{2,1,0:T(8,128)S(1)}, u32[]{:S(2)}, u32[]{:S(2)}) %collective-permute-start.7) | collective-permute-done | bytes 86048 | tf_op jit(solution)/shard_map/ppermute | solution.py:458
  23.4 1.0 %collective-permute-done.8.far_ref = f32[21,8,128]{2,1,0:T(8,128)S(1)} collective-permute-done((f32[21,8,128]{2,1,0:T(8,128)S(1)}, f32[21,8,128]{2,1,0:T(8,128)S(1)}, u32[]{:S(2)}, u32[]{:S(2)}) %collective-permute-start.8) | collective-permute-done | bytes 86048 | tf_op jit(solution)/shard_map/ppermute | solution.py:458
  24.4 0.0 collective-permute-done.6.four_ref
  24.4 0.0 collective-permute-done.9.on_ref
  24.4 2.8 %unpack.1 = (f32[2560,128]{1,0:T(8,128)S(1)}, f32[2560,128]{1,0:T(8,128)S(1)}, f32[480,128]{1,0:T(8,128)S(1)}, f32[480,128]{1,0:T(8,128)S(1)}, f32[240,128]{1,0:T(8,128)S(1)}, /*index=5*/f32[240,128]{1,0:T(8,128)S(1)}) custom-call(s32[1,128]{1,0:T(1,128)S(1)} %bitcast.7, f32[5,128,512]{2,1,0:T(8,128)S(1)} %bitcast.4, ...), custom_call_target="tpu_custom_call" | custom-call | tf_op jit(solution)/shard_map/unpack/pallas_call | solution.py:249
  27.2 1.7 %collective-permute-start.12 = (f32[480,128]{1,0:T(8,128)S(1)}, f32[480,128]{1,0:T(8,128)S(1)}, u32[]{:S(2)}, u32[]{:S(2)}) collective-permute-start(f32[480,128]{1,0:T(8,128)S(1)} %get-tuple-element.35), channel_id=1, source_target_pairs={{0,8},{8,0},{16,24},{24,16},{32,40},{40,32},{48,56},{56,48},{64,72... | collective-permute-start | bytes 737288 | tf_op jit(solution)/shard_map/ppermute | solution.py:458
  28.9 5.0 %collective-permute-start.13 = (f32[480,128]{1,0:T(8,128)S(1)}, f32[480,128]{1,0:T(8,128)S(1)}, u32[]{:S(2)}, u32[]{:S(2)}) collective-permute-start(f32[480,128]{1,0:T(8,128)S(1)} %get-tuple-element.36), channel_id=1, source_target_pairs={{0,120},{8,16},{16,8},{24,32},{32,24},{40,48},{48,40},{56,64},{64,... | collective-permute-start | bytes 737288 | tf_op jit(solution)/shard_map/ppermute | solution.py:458
  33.9 0.6 %collective-permute-start.11 = (f32[240,128]{1,0:T(8,128)S(1)}, f32[240,128]{1,0:T(8,128)S(1)}, u32[]{:S(2)}, u32[]{:S(2)}) collective-permute-start(f32[240,128]{1,0:T(8,128)S(1)} %get-tuple-element.34), channel_id=1, source_target_pairs={{0,7},{1,2},{2,1},{3,4},{4,3},{5,6},{6,5},{7,0},{8,15},{9,10},{10,... | collective-permute-start | bytes 368648 | tf_op jit(solution)/shard_map/ppermute | solution.py:458
  34.4 3.7 %flux_inner.1.before_ref = f32[2560,128]{1,0:T(8,128)S(1)} custom-call(f32[2560,128]{1,0:T(8,128)S(1)} %get-tuple-element.31.state_ref, f32[2560,128]{1,0:T(8,128)S(1)} %get-tuple-element.32.prim_ref), custom_call_target="tpu_custom_call" | custom-call | flops 20000000 | bytes 4000000 | tf_op jit(solution)/shard_map/flux_inner/pallas_call | solution.py:434
  38.2 1.2 %collective-permute-done.11.second_ref = f32[240,128]{1,0:T(8,128)S(1)} collective-permute-done((f32[240,128]{1,0:T(8,128)S(1)}, f32[240,128]{1,0:T(8,128)S(1)}, u32[]{:S(2)}, u32[]{:S(2)}) %collective-permute-start.11) | collective-permute-done | bytes 122912 | tf_op jit(solution)/shard_map/ppermute | solution.py:458
  39.4 2.1 %flux_second.1.change_ref = f32[2560,128]{1,0:T(8,128)S(1)} custom-call(f32[2560,128]{1,0:T(8,128)S(1)} %get-tuple-element.32.prim_ref, f32[240,128]{1,0:T(8,128)S(1)} %collective-permute-done.10.first_ref, f32[240,128]{1,0:T(8,128)S(1)} %collective-permute-done.11.second_ref), custom_call_target="tpu_custom_call" | custom-call | flops 20000000 | bytes 4000000 | tf_op jit(solution)/shard_map/flux_second/pallas_call | solution.py:434
  41.5 0.0 collective-permute-done.12.first_ref
  41.5 2.4 %flux_first.1 = f32[5,16,32,128]{3,2,1,0:T(8,128)} custom-call(f32[2560,128]{1,0:T(8,128)S(1)} %flux_inner.1.before_ref, f32[2560,128]{1,0:T(8,128)S(1)} %get-tuple-element.32.prim_ref, f32[2560,128]{1,0:T(8,128)S(1)} %flux_second.1.change_ref, f32[480,128]{1,0:T(8,128)S(1)} %collective-permute-done.12.first_ref, ...), custom_call_target="tpu_custom_call" | custom-call | tf_op jit(solution)/shard_map/flux_first/pallas_call | solution.py:445
  (6 shorter events, 0.0 us)
Async XLA Ops:
  0.0 1.3 %copy-start = (f32[128,5,512]{2,0,1:T(8,128)S(1)}, f32[128,5,512]{2,0,1:T(8,128)}, u32[]{:S(2)}) copy-start(f32[128,5,512]{2,0,1:T(8,128)} %param.2) | copy-start | bytes 3932164
  1.3 0.7 %copy-start.1 = (s32[128]{0:T(128)S(1)}, s32[128]{0:T(128)}, u32[]{:S(2)}) copy-start(s32[128]{0:T(128)} %param.3) | copy-start | bytes 1540
  2.5 10.7 %collective-permute-start = (f32[2,21,8,128]{3,2,1,0:T(8,128)S(1)}, f32[2,21,8,128]{3,2,1,0:T(8,128)S(1)}, u32[]{:S(2)}, u32[]{:S(2)}) collective-permute-start(f32[2,21,8,128]{3,2,1,0:T(8,128)S(1)} %get-tuple-element.21), channel_id=1, source_target_pairs={{0,6},{1,7},{2,4},{3,5},{4,12},{5,13},{6,14},{7,15},{8,0},{9,1},{1... | collective-permute-start | bytes 516104 | tf_op jit(solution)/shard_map/ppermute | solution.py:458
  5.6 6.4 %collective-permute-start.1 = (f32[21,8,128]{2,1,0:T(8,128)S(1)}, f32[21,8,128]{2,1,0:T(8,128)S(1)}, u32[]{:S(2)}, u32[]{:S(2)}) collective-permute-start(f32[21,8,128]{2,1,0:T(8,128)S(1)} %get-tuple-element.22), channel_id=1, source_target_pairs={{0,6},{1,7},{2,4},{3,5},{4,2},{5,3},{6,0},{7,1},{8,14},{9,15},{10,... | collective-permute-start | bytes 258056 | tf_op jit(solution)/shard_map/ppermute | solution.py:458
  7.6 5.6 %collective-permute-start.2 = (f32[21,8,128]{2,1,0:T(8,128)S(1)}, f32[21,8,128]{2,1,0:T(8,128)S(1)}, u32[]{:S(2)}, u32[]{:S(2)}) collective-permute-start(f32[21,8,128]{2,1,0:T(8,128)S(1)} %get-tuple-element.23), channel_id=1, source_target_pairs={{0,7},{1,6},{2,5},{3,4},{4,3},{5,2},{6,1},{7,0},{8,15},{9,14},{10,... | collective-permute-start | bytes 258056 | tf_op jit(solution)/shard_map/ppermute | solution.py:458
  7.8 9.9 %collective-permute-start.4 = (f32[21,8,128]{2,1,0:T(8,128)S(1)}, f32[21,8,128]{2,1,0:T(8,128)S(1)}, u32[]{:S(2)}, u32[]{:S(2)}) collective-permute-start(f32[21,8,128]{2,1,0:T(8,128)S(1)} %get-tuple-element.25), channel_id=1, source_target_pairs={{0,2},{1,3},{2,0},{3,1},{4,6},{5,7},{6,4},{7,5},{8,10},{9,11},{10,... | collective-permute-start | bytes 258056 | tf_op jit(solution)/shard_map/ppermute | solution.py:458
  7.8 10.4 %collective-permute-start.5 = (f32[21,8,128]{2,1,0:T(8,128)S(1)}, f32[21,8,128]{2,1,0:T(8,128)S(1)}, u32[]{:S(2)}, u32[]{:S(2)}) collective-permute-start(f32[21,8,128]{2,1,0:T(8,128)S(1)} %get-tuple-element.26), channel_id=1, source_target_pairs={{0,3},{1,2},{2,1},{3,0},{4,7},{5,6},{6,5},{7,4},{8,11},{9,10},{10,... | collective-permute-start | bytes 258056 | tf_op jit(solution)/shard_map/ppermute | solution.py:458
  13.7 10.7 %collective-permute-start.6 = (f32[2,21,8,128]{3,2,1,0:T(8,128)S(1)}, f32[2,21,8,128]{3,2,1,0:T(8,128)S(1)}, u32[]{:S(2)}, u32[]{:S(2)}) collective-permute-start(f32[2,21,8,128]{3,2,1,0:T(8,128)S(1)} %get-tuple-element.27), channel_id=1, source_target_pairs={{0,4},{1,5},{2,6},{3,7},{4,0},{5,1},{6,2},{7,3},{8,12},{9,13},{10,... | collective-permute-start | bytes 516104 | tf_op jit(solution)/shard_map/ppermute | solution.py:458
  15.3 9.1 %collective-permute-start.9 = (f32[2,21,8,128]{3,2,1,0:T(8,128)S(1)}, f32[2,21,8,128]{3,2,1,0:T(8,128)S(1)}, u32[]{:S(2)}, u32[]{:S(2)}) collective-permute-start(f32[2,21,8,128]{3,2,1,0:T(8,128)S(1)} %get-tuple-element.30), channel_id=1, source_target_pairs={{0,8},{1,9},{2,2},{3,3},{4,4},{5,5},{8,16},{9,17},{10,10},{11,11},... | collective-permute-start | bytes 516104 | tf_op jit(solution)/shard_map/ppermute | solution.py:458
  17.5 4.0 %collective-permute-start.3 = (f32[21,8,128]{2,1,0:T(8,128)S(1)}, f32[21,8,128]{2,1,0:T(8,128)S(1)}, u32[]{:S(2)}, u32[]{:S(2)}) collective-permute-start(f32[21,8,128]{2,1,0:T(8,128)S(1)} %get-tuple-element.24), channel_id=1, source_target_pairs={{0,1},{1,0},{2,3},{3,2},{4,5},{5,4},{6,7},{7,6},{8,9},{9,8},{10,11... | collective-permute-start | bytes 258056 | tf_op jit(solution)/shard_map/ppermute | solution.py:458
  17.6 5.8 %collective-permute-start.7 = (f32[21,8,128]{2,1,0:T(8,128)S(1)}, f32[21,8,128]{2,1,0:T(8,128)S(1)}, u32[]{:S(2)}, u32[]{:S(2)}) collective-permute-start(f32[21,8,128]{2,1,0:T(8,128)S(1)} %get-tuple-element.28), channel_id=1, source_target_pairs={{0,5},{1,4},{2,7},{3,6},{4,1},{5,0},{6,3},{7,2},{8,13},{9,12},{10,... | collective-permute-start | bytes 258056 | tf_op jit(solution)/shard_map/ppermute | solution.py:458
  18.2 6.2 %collective-permute-start.8 = (f32[21,8,128]{2,1,0:T(8,128)S(1)}, f32[21,8,128]{2,1,0:T(8,128)S(1)}, u32[]{:S(2)}, u32[]{:S(2)}) collective-permute-start(f32[21,8,128]{2,1,0:T(8,128)S(1)} %get-tuple-element.29), channel_id=1, source_target_pairs={{0,64},{1,65},{2,66},{3,67},{4,68},{5,69},{6,70},{7,71},{8,72},{9,... | collective-permute-start | bytes 258056 | tf_op jit(solution)/shard_map/ppermute | solution.py:458
  27.2 14.3 %collective-permute-start.12 = (f32[480,128]{1,0:T(8,128)S(1)}, f32[480,128]{1,0:T(8,128)S(1)}, u32[]{:S(2)}, u32[]{:S(2)}) collective-permute-start(f32[480,128]{1,0:T(8,128)S(1)} %get-tuple-element.35), channel_id=1, source_target_pairs={{0,8},{8,0},{16,24},{24,16},{32,40},{40,32},{48,56},{56,48},{64,72... | collective-permute-start | bytes 737288 | tf_op jit(solution)/shard_map/ppermute | solution.py:458
  28.9 12.6 %collective-permute-start.13 = (f32[480,128]{1,0:T(8,128)S(1)}, f32[480,128]{1,0:T(8,128)S(1)}, u32[]{:S(2)}, u32[]{:S(2)}) collective-permute-start(f32[480,128]{1,0:T(8,128)S(1)} %get-tuple-element.36), channel_id=1, source_target_pairs={{0,120},{8,16},{16,8},{24,32},{32,24},{40,48},{48,40},{56,64},{64,... | collective-permute-start | bytes 737288 | tf_op jit(solution)/shard_map/ppermute | solution.py:458
  33.9 4.3 %collective-permute-start.10 = (f32[240,128]{1,0:T(8,128)S(1)}, f32[240,128]{1,0:T(8,128)S(1)}, u32[]{:S(2)}, u32[]{:S(2)}) collective-permute-start(f32[240,128]{1,0:T(8,128)S(1)} %get-tuple-element.33), channel_id=1, source_target_pairs={{0,1},{1,0},{2,3},{3,2},{4,5},{5,4},{6,7},{7,6},{8,9},{9,8},{10,11... | collective-permute-start | bytes 368648 | tf_op jit(solution)/shard_map/ppermute | solution.py:458
  33.9 5.5 %collective-permute-start.11 = (f32[240,128]{1,0:T(8,128)S(1)}, f32[240,128]{1,0:T(8,128)S(1)}, u32[]{:S(2)}, u32[]{:S(2)}) collective-permute-start(f32[240,128]{1,0:T(8,128)S(1)} %get-tuple-element.34), channel_id=1, source_target_pairs={{0,7},{1,2},{2,1},{3,4},{4,3},{5,6},{6,5},{7,0},{8,15},{9,10},{10,... | collective-permute-start | bytes 368648 | tf_op jit(solution)/shard_map/ppermute | solution.py:458

commit v6 on v5

--- a/solution.py
+++ b/solution.py
@@ -371,7 +371,7 @@
     return jnp.where(odd, first, second) if before else jnp.where(odd, second, first)
 
 
-def y_kernel(prim_ref, first_ref, second_ref, change_ref):
+def y_kernel(prim_ref, second_ref, first_ref, change_ref):
     odd = lax.axis_index("dev") % 2 == 1
 
     def step(block, carry):
@@ -493,7 +493,7 @@
     y_first = shifted(y_first, "dev", 8, lambda i: i ^ 1)
     y_second = shifted(y_second, "dev", 8, lambda i: (i + 1) % 8 if i % 2 else (i - 1) % 8)
     result = stage(inner_kernel, "flux_inner", state, prim)
-    change = stage(y_kernel, "flux_second", prim, y_first, y_second)
+    change = stage(y_kernel, "flux_second", prim, y_second, y_first)
     return finish(result, prim, change, x_first, x_second)
 
 

time: 44.6 us -> 44.1 us (0.989); the launches traced: 43.9 us -> 43.9 us
  no operation moved by 1% of the time
where the time goes in v6:
time: 44.1 us; the launch traced here: 43.9 us
  starting transfers between devices  22.8 us (52%)
  Pallas kernels  12.1 us (27%)
  waiting for transfers between devices  6.93 us (16%)
  local copies, waits for them, and re-layouts  1.97 us (4%)
    ppermute x14, starting transfers between devices, shifted(): return lax.ppermute(value, axes, [pair for pair in pairs if pair[1] >= 0])  22.8 us
    ppermute x14, waiting for transfers between devices, shifted(): return lax.ppermute(value, axes, [pair for pair in pairs if pair[1] >= 0])  6.93 us
    pallas_call x2, Pallas kernels, stage(): call(kernel, name, jax.ShapeDtypeStruct((ROWS, CZ), jnp.float32), [VMEM]...  5.86 us
    pallas_call x1, Pallas kernels, unpack(): call(unpack_kernel, 'unpack', (grid_rows, grid_rows, x_side, x_side, y_si...  2.82 us
    pallas_call x1, Pallas kernels, finish(): pl.pallas_call(x_kernel, out_shape=jax.ShapeDtypeStruct(shape, jnp.float3...  2.35 us
    unnamed x4, local copies, waits for them, and re-layouts  1.97 us
  transfers between devices with their start and end apart: 14, of which 5 were waited for; matrix products, arithmetic and copies ran while one was open for 0% of the time, Pallas kernels for 15%

profile of v6, /device:TPU:0, one launch (start us, length us, event | category | flops | bytes accessed | tf_op | source)
XLA Modules:
  0.0 43.9 jit_solution(16582051914567535141)
XLA Ops:
  0.0 1.3 %copy-done = f32[128,5,512]{2,0,1:T(8,128)S(1)} copy-done((f32[128,5,512]{2,0,1:T(8,128)S(1)}, f32[128,5,512]{2,0,1:T(8,128)}, u32[]{:S(2)}) %copy-start) | copy-done | bytes 1310744
  1.3 0.7 %copy-done.1 = s32[128]{0:T(128)S(1)} copy-done((s32[128]{0:T(128)S(1)}, s32[128]{0:T(128)}, u32[]{:S(2)}) %copy-start.1) | copy-done | bytes 536
  2.0 0.5 %pack_early.1 = (f32[21,8,128]{2,1,0:T(8,128)S(1)}, f32[21,8,128]{2,1,0:T(8,128)S(1)}, f32[21,8,128]{2,1,0:T(8,128)S(1)}, f32[21,8,128]{2,1,0:T(8,128)S(1)}, f32[2,21,8,128]{3,2,1,0:T(8,128)S(1)}) custom-call(s32[1,128]{1,0:T(1,128)S(1)} %bitcast.5, f32[5,128,512]{2,1,0:T(8,128)S(1)} %bitcast.2), custom_call_target="tpu_custom_call" | custom-call | tf_op jit(solution)/shard_map/pack_early/pallas_call | solution.py:151
  2.5 3.1 %collective-permute-start = (f32[2,21,8,128]{3,2,1,0:T(8,128)S(1)}, f32[2,21,8,128]{3,2,1,0:T(8,128)S(1)}, u32[]{:S(2)}, u32[]{:S(2)}) collective-permute-start(f32[2,21,8,128]{3,2,1,0:T(8,128)S(1)} %get-tuple-element.21), channel_id=1, source_target_pairs={{0,6},{1,7},{2,4},{3,5},{4,12},{5,13},{6,14},{7,15},{8,0},{9,1},{1... | collective-permute-start | bytes 516104 | tf_op jit(solution)/shard_map/ppermute | solution.py:458
  5.6 1.9 %collective-permute-start.1 = (f32[21,8,128]{2,1,0:T(8,128)S(1)}, f32[21,8,128]{2,1,0:T(8,128)S(1)}, u32[]{:S(2)}, u32[]{:S(2)}) collective-permute-start(f32[21,8,128]{2,1,0:T(8,128)S(1)} %get-tuple-element.22), channel_id=1, source_target_pairs={{0,6},{1,7},{2,4},{3,5},{4,2},{5,3},{6,0},{7,1},{8,14},{9,15},{10,... | collective-permute-start | bytes 258056 | tf_op jit(solution)/shard_map/ppermute | solution.py:458
  7.6 0.2 collective-permute-start.2
  7.8 0.0 collective-permute-start.4
  7.8 2.6 %collective-permute-start.5 = (f32[21,8,128]{2,1,0:T(8,128)S(1)}, f32[21,8,128]{2,1,0:T(8,128)S(1)}, u32[]{:S(2)}, u32[]{:S(2)}) collective-permute-start(f32[21,8,128]{2,1,0:T(8,128)S(1)} %get-tuple-element.26), channel_id=1, source_target_pairs={{0,3},{1,2},{2,1},{3,0},{4,7},{5,6},{6,5},{7,4},{8,11},{9,10},{10,... | collective-permute-start | bytes 258056 | tf_op jit(solution)/shard_map/ppermute | solution.py:458
  10.3 1.7 %collective-permute-done.1.six_ref = f32[21,8,128]{2,1,0:T(8,128)S(1)} collective-permute-done((f32[21,8,128]{2,1,0:T(8,128)S(1)}, f32[21,8,128]{2,1,0:T(8,128)S(1)}, u32[]{:S(2)}, u32[]{:S(2)}) %collective-permute-start.1) | collective-permute-done | bytes 86048 | tf_op jit(solution)/shard_map/ppermute | solution.py:458
  12.0 1.1 %collective-permute-done.2.seven_ref = f32[21,8,128]{2,1,0:T(8,128)S(1)} collective-permute-done((f32[21,8,128]{2,1,0:T(8,128)S(1)}, f32[21,8,128]{2,1,0:T(8,128)S(1)}, u32[]{:S(2)}, u32[]{:S(2)}) %collective-permute-start.2) | collective-permute-done | bytes 86048 | tf_op jit(solution)/shard_map/ppermute | solution.py:458
  13.2 0.0 collective-permute-done.relay_ref
  13.2 0.5 %pack_late.1 = (f32[21,8,128]{2,1,0:T(8,128)S(1)}, f32[2,21,8,128]{3,2,1,0:T(8,128)S(1)}, f32[21,8,128]{2,1,0:T(8,128)S(1)}, f32[21,8,128]{2,1,0:T(8,128)S(1)}, f32[2,21,8,128]{3,2,1,0:T(8,128)S(1)}) custom-call(s32[1,128]{1,0:T(1,128)S(1)} %bitcast.6, f32[5,128,512]{2,1,0:T(8,128)S(1)} %bitcast.3, f32[2,21,8,128]{3,2,1,0:T(8,128)S(1)} %collective-permute-done.relay_ref, ...), custom_call_target="tpu_custom_call" | custom-call | tf_op jit(solution)/shard_map/pack_late/pallas_call | solution.py:155
  13.7 1.6 %collective-permute-start.6 = (f32[2,21,8,128]{3,2,1,0:T(8,128)S(1)}, f32[2,21,8,128]{3,2,1,0:T(8,128)S(1)}, u32[]{:S(2)}, u32[]{:S(2)}) collective-permute-start(f32[2,21,8,128]{3,2,1,0:T(8,128)S(1)} %get-tuple-element.27), channel_id=1, source_target_pairs={{0,4},{1,5},{2,6},{3,7},{4,0},{5,1},{6,2},{7,3},{8,12},{9,13},{10,... | collective-permute-start | bytes 516104 | tf_op jit(solution)/shard_map/ppermute | solution.py:458
  15.3 2.2 %collective-permute-start.9 = (f32[2,21,8,128]{3,2,1,0:T(8,128)S(1)}, f32[2,21,8,128]{3,2,1,0:T(8,128)S(1)}, u32[]{:S(2)}, u32[]{:S(2)}) collective-permute-start(f32[2,21,8,128]{3,2,1,0:T(8,128)S(1)} %get-tuple-element.30), channel_id=1, source_target_pairs={{0,8},{1,9},{2,2},{3,3},{4,4},{5,5},{8,16},{9,17},{10,10},{11,11},... | collective-permute-start | bytes 516104 | tf_op jit(solution)/shard_map/ppermute | solution.py:458
  17.5 0.1 collective-permute-start.3
  17.6 0.0 collective-permute-done.4.two_ref
  17.6 0.6 %collective-permute-start.7 = (f32[21,8,128]{2,1,0:T(8,128)S(1)}, f32[21,8,128]{2,1,0:T(8,128)S(1)}, u32[]{:S(2)}, u32[]{:S(2)}) collective-permute-start(f32[21,8,128]{2,1,0:T(8,128)S(1)} %get-tuple-element.28), channel_id=1, source_target_pairs={{0,5},{1,4},{2,7},{3,6},{4,1},{5,0},{6,3},{7,2},{8,13},{9,12},{10,... | collective-permute-start | bytes 258056 | tf_op jit(solution)/shard_map/ppermute | solution.py:458
  18.2 0.0 collective-permute-done.5.three_ref
  18.2 3.3 %collective-permute-start.8 = (f32[21,8,128]{2,1,0:T(8,128)S(1)}, f32[21,8,128]{2,1,0:T(8,128)S(1)}, u32[]{:S(2)}, u32[]{:S(2)}) collective-permute-start(f32[21,8,128]{2,1,0:T(8,128)S(1)} %get-tuple-element.29), channel_id=1, source_target_pairs={{0,64},{1,65},{2,66},{3,67},{4,68},{5,69},{6,70},{7,71},{8,72},{9,... | collective-permute-start | bytes 258056 | tf_op jit(solution)/shard_map/ppermute | solution.py:458
  21.5 1.9 %collective-permute-done.7.five_ref = f32[21,8,128]{2,1,0:T(8,128)S(1)} collective-permute-done((f32[21,8,128]{2,1,0:T(8,128)S(1)}, f32[21,8,128]{2,1,0:T(8,128)S(1)}, u32[]{:S(2)}, u32[]{:S(2)}) %collective-permute-start.7) | collective-permute-done | bytes 86048 | tf_op jit(solution)/shard_map/ppermute | solution.py:458
  23.4 1.0 %collective-permute-done.8.far_ref = f32[21,8,128]{2,1,0:T(8,128)S(1)} collective-permute-done((f32[21,8,128]{2,1,0:T(8,128)S(1)}, f32[21,8,128]{2,1,0:T(8,128)S(1)}, u32[]{:S(2)}, u32[]{:S(2)}) %collective-permute-start.8) | collective-permute-done | bytes 86048 | tf_op jit(solution)/shard_map/ppermute | solution.py:458
  24.4 2.8 %unpack.1 = (f32[2560,128]{1,0:T(8,128)S(1)}, f32[2560,128]{1,0:T(8,128)S(1)}, f32[480,128]{1,0:T(8,128)S(1)}, f32[480,128]{1,0:T(8,128)S(1)}, f32[240,128]{1,0:T(8,128)S(1)}, /*index=5*/f32[240,128]{1,0:T(8,128)S(1)}) custom-call(s32[1,128]{1,0:T(1,128)S(1)} %bitcast.7, f32[5,128,512]{2,1,0:T(8,128)S(1)} %bitcast.4, ...), custom_call_target="tpu_custom_call" | custom-call | tf_op jit(solution)/shard_map/unpack/pallas_call | solution.py:249
  27.2 1.7 %collective-permute-start.12 = (f32[480,128]{1,0:T(8,128)S(1)}, f32[480,128]{1,0:T(8,128)S(1)}, u32[]{:S(2)}, u32[]{:S(2)}) collective-permute-start(f32[480,128]{1,0:T(8,128)S(1)} %get-tuple-element.35), channel_id=1, source_target_pairs={{0,8},{8,0},{16,24},{24,16},{32,40},{40,32},{48,56},{56,48},{64,72... | collective-permute-start | bytes 737288 | tf_op jit(solution)/shard_map/ppermute | solution.py:458
  28.9 5.0 %collective-permute-start.13 = (f32[480,128]{1,0:T(8,128)S(1)}, f32[480,128]{1,0:T(8,128)S(1)}, u32[]{:S(2)}, u32[]{:S(2)}) collective-permute-start(f32[480,128]{1,0:T(8,128)S(1)} %get-tuple-element.36), channel_id=1, source_target_pairs={{0,120},{8,16},{16,8},{24,32},{32,24},{40,48},{48,40},{56,64},{64,... | collective-permute-start | bytes 737288 | tf_op jit(solution)/shard_map/ppermute | solution.py:458
  33.9 0.0 collective-permute-start.10
  33.9 0.6 %collective-permute-start.11 = (f32[240,128]{1,0:T(8,128)S(1)}, f32[240,128]{1,0:T(8,128)S(1)}, u32[]{:S(2)}, u32[]{:S(2)}) collective-permute-start(f32[240,128]{1,0:T(8,128)S(1)} %get-tuple-element.34), channel_id=1, source_target_pairs={{0,1},{1,0},{2,3},{3,2},{4,5},{5,4},{6,7},{7,6},{8,9},{9,8},{10,11... | collective-permute-start | bytes 368648 | tf_op jit(solution)/shard_map/ppermute | solution.py:458
  34.5 3.7 %flux_inner.1.before_ref = f32[2560,128]{1,0:T(8,128)S(1)} custom-call(f32[2560,128]{1,0:T(8,128)S(1)} %get-tuple-element.31.state_ref, f32[2560,128]{1,0:T(8,128)S(1)} %get-tuple-element.32.prim_ref), custom_call_target="tpu_custom_call" | custom-call | flops 20000000 | bytes 4000000 | tf_op jit(solution)/shard_map/flux_inner/pallas_call | solution.py:434
  38.2 1.2 %collective-permute-done.10.second_ref = f32[240,128]{1,0:T(8,128)S(1)} collective-permute-done((f32[240,128]{1,0:T(8,128)S(1)}, f32[240,128]{1,0:T(8,128)S(1)}, u32[]{:S(2)}, u32[]{:S(2)}) %collective-permute-start.10) | collective-permute-done | bytes 122912 | tf_op jit(solution)/shard_map/ppermute | solution.py:458
  39.4 0.0 collective-permute-done.11.first_ref
  39.4 2.1 %flux_second.1.change_ref = f32[2560,128]{1,0:T(8,128)S(1)} custom-call(f32[2560,128]{1,0:T(8,128)S(1)} %get-tuple-element.32.prim_ref, f32[240,128]{1,0:T(8,128)S(1)} %collective-permute-done.10.second_ref, f32[240,128]{1,0:T(8,128)S(1)} %collective-permute-done.11.first_ref), custom_call_target="tpu_custom_call" | custom-call | flops 20000000 | bytes 4000000 | tf_op jit(solution)/shard_map/flux_second/pallas_call | solution.py:434
  41.5 0.0 collective-permute-done.12.first_ref
  41.5 2.4 %flux_first.1 = f32[5,16,32,128]{3,2,1,0:T(8,128)} custom-call(f32[2560,128]{1,0:T(8,128)S(1)} %flux_inner.1.before_ref, f32[2560,128]{1,0:T(8,128)S(1)} %get-tuple-element.32.prim_ref, f32[2560,128]{1,0:T(8,128)S(1)} %flux_second.1.change_ref, f32[480,128]{1,0:T(8,128)S(1)} %collective-permute-done.12.first_ref, ...), custom_call_target="tpu_custom_call" | custom-call | tf_op jit(solution)/shard_map/flux_first/pallas_call | solution.py:445
  (6 shorter events, 0.0 us)
Async XLA Ops:
  0.0 1.3 %copy-start = (f32[128,5,512]{2,0,1:T(8,128)S(1)}, f32[128,5,512]{2,0,1:T(8,128)}, u32[]{:S(2)}) copy-start(f32[128,5,512]{2,0,1:T(8,128)} %param.2) | copy-start | bytes 3932164
  1.3 0.7 %copy-start.1 = (s32[128]{0:T(128)S(1)}, s32[128]{0:T(128)}, u32[]{:S(2)}) copy-start(s32[128]{0:T(128)} %param.3) | copy-start | bytes 1540
  2.5 10.7 %collective-permute-start = (f32[2,21,8,128]{3,2,1,0:T(8,128)S(1)}, f32[2,21,8,128]{3,2,1,0:T(8,128)S(1)}, u32[]{:S(2)}, u32[]{:S(2)}) collective-permute-start(f32[2,21,8,128]{3,2,1,0:T(8,128)S(1)} %get-tuple-element.21), channel_id=1, source_target_pairs={{0,6},{1,7},{2,4},{3,5},{4,12},{5,13},{6,14},{7,15},{8,0},{9,1},{1... | collective-permute-start | bytes 516104 | tf_op jit(solution)/shard_map/ppermute | solution.py:458
  5.6 6.4 %collective-permute-start.1 = (f32[21,8,128]{2,1,0:T(8,128)S(1)}, f32[21,8,128]{2,1,0:T(8,128)S(1)}, u32[]{:S(2)}, u32[]{:S(2)}) collective-permute-start(f32[21,8,128]{2,1,0:T(8,128)S(1)} %get-tuple-element.22), channel_id=1, source_target_pairs={{0,6},{1,7},{2,4},{3,5},{4,2},{5,3},{6,0},{7,1},{8,14},{9,15},{10,... | collective-permute-start | bytes 258056 | tf_op jit(solution)/shard_map/ppermute | solution.py:458
  7.6 5.6 %collective-permute-start.2 = (f32[21,8,128]{2,1,0:T(8,128)S(1)}, f32[21,8,128]{2,1,0:T(8,128)S(1)}, u32[]{:S(2)}, u32[]{:S(2)}) collective-permute-start(f32[21,8,128]{2,1,0:T(8,128)S(1)} %get-tuple-element.23), channel_id=1, source_target_pairs={{0,7},{1,6},{2,5},{3,4},{4,3},{5,2},{6,1},{7,0},{8,15},{9,14},{10,... | collective-permute-start | bytes 258056 | tf_op jit(solution)/shard_map/ppermute | solution.py:458
  7.8 9.9 %collective-permute-start.4 = (f32[21,8,128]{2,1,0:T(8,128)S(1)}, f32[21,8,128]{2,1,0:T(8,128)S(1)}, u32[]{:S(2)}, u32[]{:S(2)}) collective-permute-start(f32[21,8,128]{2,1,0:T(8,128)S(1)} %get-tuple-element.25), channel_id=1, source_target_pairs={{0,2},{1,3},{2,0},{3,1},{4,6},{5,7},{6,4},{7,5},{8,10},{9,11},{10,... | collective-permute-start | bytes 258056 | tf_op jit(solution)/shard_map/ppermute | solution.py:458
  7.8 10.4 %collective-permute-start.5 = (f32[21,8,128]{2,1,0:T(8,128)S(1)}, f32[21,8,128]{2,1,0:T(8,128)S(1)}, u32[]{:S(2)}, u32[]{:S(2)}) collective-permute-start(f32[21,8,128]{2,1,0:T(8,128)S(1)} %get-tuple-element.26), channel_id=1, source_target_pairs={{0,3},{1,2},{2,1},{3,0},{4,7},{5,6},{6,5},{7,4},{8,11},{9,10},{10,... | collective-permute-start | bytes 258056 | tf_op jit(solution)/shard_map/ppermute | solution.py:458
  13.7 10.7 %collective-permute-start.6 = (f32[2,21,8,128]{3,2,1,0:T(8,128)S(1)}, f32[2,21,8,128]{3,2,1,0:T(8,128)S(1)}, u32[]{:S(2)}, u32[]{:S(2)}) collective-permute-start(f32[2,21,8,128]{3,2,1,0:T(8,128)S(1)} %get-tuple-element.27), channel_id=1, source_target_pairs={{0,4},{1,5},{2,6},{3,7},{4,0},{5,1},{6,2},{7,3},{8,12},{9,13},{10,... | collective-permute-start | bytes 516104 | tf_op jit(solution)/shard_map/ppermute | solution.py:458
  15.3 9.1 %collective-permute-start.9 = (f32[2,21,8,128]{3,2,1,0:T(8,128)S(1)}, f32[2,21,8,128]{3,2,1,0:T(8,128)S(1)}, u32[]{:S(2)}, u32[]{:S(2)}) collective-permute-start(f32[2,21,8,128]{3,2,1,0:T(8,128)S(1)} %get-tuple-element.30), channel_id=1, source_target_pairs={{0,8},{1,9},{2,2},{3,3},{4,4},{5,5},{8,16},{9,17},{10,10},{11,11},... | collective-permute-start | bytes 516104 | tf_op jit(solution)/shard_map/ppermute | solution.py:458
  17.5 4.0 %collective-permute-start.3 = (f32[21,8,128]{2,1,0:T(8,128)S(1)}, f32[21,8,128]{2,1,0:T(8,128)S(1)}, u32[]{:S(2)}, u32[]{:S(2)}) collective-permute-start(f32[21,8,128]{2,1,0:T(8,128)S(1)} %get-tuple-element.24), channel_id=1, source_target_pairs={{0,1},{1,0},{2,3},{3,2},{4,5},{5,4},{6,7},{7,6},{8,9},{9,8},{10,11... | collective-permute-start | bytes 258056 | tf_op jit(solution)/shard_map/ppermute | solution.py:458
  17.6 5.8 %collective-permute-start.7 = (f32[21,8,128]{2,1,0:T(8,128)S(1)}, f32[21,8,128]{2,1,0:T(8,128)S(1)}, u32[]{:S(2)}, u32[]{:S(2)}) collective-permute-start(f32[21,8,128]{2,1,0:T(8,128)S(1)} %get-tuple-element.28), channel_id=1, source_target_pairs={{0,5},{1,4},{2,7},{3,6},{4,1},{5,0},{6,3},{7,2},{8,13},{9,12},{10,... | collective-permute-start | bytes 258056 | tf_op jit(solution)/shard_map/ppermute | solution.py:458
  18.2 6.2 %collective-permute-start.8 = (f32[21,8,128]{2,1,0:T(8,128)S(1)}, f32[21,8,128]{2,1,0:T(8,128)S(1)}, u32[]{:S(2)}, u32[]{:S(2)}) collective-permute-start(f32[21,8,128]{2,1,0:T(8,128)S(1)} %get-tuple-element.29), channel_id=1, source_target_pairs={{0,64},{1,65},{2,66},{3,67},{4,68},{5,69},{6,70},{7,71},{8,72},{9,... | collective-permute-start | bytes 258056 | tf_op jit(solution)/shard_map/ppermute | solution.py:458
  27.2 14.3 %collective-permute-start.12 = (f32[480,128]{1,0:T(8,128)S(1)}, f32[480,128]{1,0:T(8,128)S(1)}, u32[]{:S(2)}, u32[]{:S(2)}) collective-permute-start(f32[480,128]{1,0:T(8,128)S(1)} %get-tuple-element.35), channel_id=1, source_target_pairs={{0,8},{8,0},{16,24},{24,16},{32,40},{40,32},{48,56},{56,48},{64,72... | collective-permute-start | bytes 737288 | tf_op jit(solution)/shard_map/ppermute | solution.py:458
  28.9 12.6 %collective-permute-start.13 = (f32[480,128]{1,0:T(8,128)S(1)}, f32[480,128]{1,0:T(8,128)S(1)}, u32[]{:S(2)}, u32[]{:S(2)}) collective-permute-start(f32[480,128]{1,0:T(8,128)S(1)} %get-tuple-element.36), channel_id=1, source_target_pairs={{0,120},{8,16},{16,8},{24,32},{32,24},{40,48},{48,40},{56,64},{64,... | collective-permute-start | bytes 737288 | tf_op jit(solution)/shard_map/ppermute | solution.py:458
  33.9 5.5 %collective-permute-start.10 = (f32[240,128]{1,0:T(8,128)S(1)}, f32[240,128]{1,0:T(8,128)S(1)}, u32[]{:S(2)}, u32[]{:S(2)}) collective-permute-start(f32[240,128]{1,0:T(8,128)S(1)} %get-tuple-element.33), channel_id=1, source_target_pairs={{0,7},{1,2},{2,1},{3,4},{4,3},{5,6},{6,5},{7,0},{8,15},{9,10},{10,... | collective-permute-start | bytes 368648 | tf_op jit(solution)/shard_map/ppermute | solution.py:458
  33.9 5.5 %collective-permute-start.11 = (f32[240,128]{1,0:T(8,128)S(1)}, f32[240,128]{1,0:T(8,128)S(1)}, u32[]{:S(2)}, u32[]{:S(2)}) collective-permute-start(f32[240,128]{1,0:T(8,128)S(1)} %get-tuple-element.34), channel_id=1, source_target_pairs={{0,1},{1,0},{2,3},{3,2},{4,5},{5,4},{6,7},{7,6},{8,9},{9,8},{10,11... | collective-permute-start | bytes 368648 | tf_op jit(solution)/shard_map/ppermute | solution.py:458

commit v7 on v6

--- a/solution.py
+++ b/solution.py
@@ -396,9 +396,12 @@
 def x_kernel(before_ref, prim_ref, change_ref, first_ref, second_ref, out_hbm, out_ref, sems):
     odd = lax.axis_index("node") % 2 == 1
 
-    def leaving(block, field):
-        part = (field, slice(None), pl.ds(pl.multiple_of(block * 8, 8), 8))
-        return pltpu.make_async_copy(out_ref.at[part], out_hbm.at[part], sems.at[block, field])
+    spans = ((3, CX - 6), (0, 3), (CX - 3, 3))
+
+    def leaving(block, field, span):
+        first, count = spans[span]
+        part = (field, pl.ds(first, count), pl.ds(pl.multiple_of(block * 8, 8), 8))
+        return pltpu.make_async_copy(out_ref.at[part], out_hbm.at[part], sems.at[block, field, span])
 
     def step(block, carry):
         def load(cell):
@@ -416,18 +419,22 @@
                 value = before_ref[block_rows(f, cell, block), :] - 0.1 * total
                 out_ref[f, cell, pl.ds(pl.multiple_of(block * 8, 8), 8), :] = value
 
-        sweep(load, 0, 2, 1, emit)
         for cell in range(3, CX - 3):
             emit(cell)
+        for field in range(FIELDS):
+            leaving(block, field, 0).start()
+        sweep(load, 0, 2, 1, emit)
         sweep(load, CX - 3, CX - 1, 1, emit)
         for field in range(FIELDS):
-            leaving(block, field).start()
+            leaving(block, field, 1).start()
+            leaving(block, field, 2).start()
         return carry
 
     lax.fori_loop(0, CY // 8, step, 0)
     for block in range(CY // 8):
         for field in range(FIELDS):
-            leaving(block, field).wait()
+            for span in range(3):
+                leaving(block, field, span).wait()
 
 
 def stage(kernel, name, *operands):
@@ -447,7 +454,7 @@
         out_shape=jax.ShapeDtypeStruct(shape, jnp.float32),
         in_specs=[VMEM] * len(operands),
         out_specs=pl.BlockSpec(memory_space=pl.ANY),
-        scratch_shapes=[pltpu.VMEM(shape, jnp.float32), pltpu.SemaphoreType.DMA((CY // 8, FIELDS))],
+        scratch_shapes=[pltpu.VMEM(shape, jnp.float32), pltpu.SemaphoreType.DMA((CY // 8, FIELDS, 3))],
         compiler_params=pltpu.CompilerParams(vmem_limit_bytes=VMEM_LIMIT),
         name="flux_first",
     )(*operands)

time: 44.1 us -> 44.4 us (level)
  transfers between devices with their start and end apart: 14 -> 14, of which waited for: 5 -> 5; matrix products, arithmetic and copies ran while one was open for 0% -> 0% of each run, Pallas kernels for 15% -> 14%
where the time goes in v7:
time: 44.4 us; the launch traced here: 44.3 us
  starting transfers between devices  22.8 us (51%)
  Pallas kernels  12.5 us (28%)
  waiting for transfers between devices  6.93 us (16%)
  local copies, waits for them, and re-layouts  1.97 us (4%)
    ppermute x14, starting transfers between devices, shifted(): return lax.ppermute(value, axes, [pair for pair in pairs if pair[1] >= 0])  22.8 us
    ppermute x14, waiting for transfers between devices, shifted(): return lax.ppermute(value, axes, [pair for pair in pairs if pair[1] >= 0])  6.93 us
    pallas_call x2, Pallas kernels, stage(): call(kernel, name, jax.ShapeDtypeStruct((ROWS, CZ), jnp.float32), [VMEM]...  5.86 us
    pallas_call x1, Pallas kernels, unpack(): call(unpack_kernel, 'unpack', (grid_rows, grid_rows, x_side, x_side, y_si...  2.82 us
    pallas_call x1, Pallas kernels, finish(): pl.pallas_call(x_kernel, out_shape=jax.ShapeDtypeStruct(shape, jnp.float3...  2.74 us
    unnamed x4, local copies, waits for them, and re-layouts  1.97 us
  transfers between devices with their start and end apart: 14, of which 5 were waited for; matrix products, arithmetic and copies ran while one was open for 0% of the time, Pallas kernels for 14%

profile of v7, /device:TPU:0, one launch (start us, length us, event | category | flops | bytes accessed | tf_op | source)
XLA Modules:
  0.0 44.3 jit_solution(14163335498281756651)
XLA Ops:
  0.0 1.3 %copy-done = f32[128,5,512]{2,0,1:T(8,128)S(1)} copy-done((f32[128,5,512]{2,0,1:T(8,128)S(1)}, f32[128,5,512]{2,0,1:T(8,128)}, u32[]{:S(2)}) %copy-start) | copy-done | bytes 1310744
  1.3 0.7 %copy-done.1 = s32[128]{0:T(128)S(1)} copy-done((s32[128]{0:T(128)S(1)}, s32[128]{0:T(128)}, u32[]{:S(2)}) %copy-start.1) | copy-done | bytes 536
  2.0 0.5 %pack_early.1 = (f32[21,8,128]{2,1,0:T(8,128)S(1)}, f32[21,8,128]{2,1,0:T(8,128)S(1)}, f32[21,8,128]{2,1,0:T(8,128)S(1)}, f32[21,8,128]{2,1,0:T(8,128)S(1)}, f32[2,21,8,128]{3,2,1,0:T(8,128)S(1)}) custom-call(s32[1,128]{1,0:T(1,128)S(1)} %bitcast.5, f32[5,128,512]{2,1,0:T(8,128)S(1)} %bitcast.2), custom_call_target="tpu_custom_call" | custom-call | tf_op jit(solution)/shard_map/pack_early/pallas_call | solution.py:151
  2.5 3.1 %collective-permute-start = (f32[2,21,8,128]{3,2,1,0:T(8,128)S(1)}, f32[2,21,8,128]{3,2,1,0:T(8,128)S(1)}, u32[]{:S(2)}, u32[]{:S(2)}) collective-permute-start(f32[2,21,8,128]{3,2,1,0:T(8,128)S(1)} %get-tuple-element.21), channel_id=1, source_target_pairs={{0,6},{1,7},{2,4},{3,5},{4,12},{5,13},{6,14},{7,15},{8,0},{9,1},{1... | collective-permute-start | bytes 516104 | tf_op jit(solution)/shard_map/ppermute | solution.py:465
  5.6 1.9 %collective-permute-start.1 = (f32[21,8,128]{2,1,0:T(8,128)S(1)}, f32[21,8,128]{2,1,0:T(8,128)S(1)}, u32[]{:S(2)}, u32[]{:S(2)}) collective-permute-start(f32[21,8,128]{2,1,0:T(8,128)S(1)} %get-tuple-element.22), channel_id=1, source_target_pairs={{0,6},{1,7},{2,4},{3,5},{4,2},{5,3},{6,0},{7,1},{8,14},{9,15},{10,... | collective-permute-start | bytes 258056 | tf_op jit(solution)/shard_map/ppermute | solution.py:465
  7.6 0.2 collective-permute-start.2
  7.8 0.0 collective-permute-start.4
  7.8 2.6 %collective-permute-start.5 = (f32[21,8,128]{2,1,0:T(8,128)S(1)}, f32[21,8,128]{2,1,0:T(8,128)S(1)}, u32[]{:S(2)}, u32[]{:S(2)}) collective-permute-start(f32[21,8,128]{2,1,0:T(8,128)S(1)} %get-tuple-element.26), channel_id=1, source_target_pairs={{0,3},{1,2},{2,1},{3,0},{4,7},{5,6},{6,5},{7,4},{8,11},{9,10},{10,... | collective-permute-start | bytes 258056 | tf_op jit(solution)/shard_map/ppermute | solution.py:465
  10.3 1.7 %collective-permute-done.1.six_ref = f32[21,8,128]{2,1,0:T(8,128)S(1)} collective-permute-done((f32[21,8,128]{2,1,0:T(8,128)S(1)}, f32[21,8,128]{2,1,0:T(8,128)S(1)}, u32[]{:S(2)}, u32[]{:S(2)}) %collective-permute-start.1) | collective-permute-done | bytes 86048 | tf_op jit(solution)/shard_map/ppermute | solution.py:465
  12.0 1.1 %collective-permute-done.2.seven_ref = f32[21,8,128]{2,1,0:T(8,128)S(1)} collective-permute-done((f32[21,8,128]{2,1,0:T(8,128)S(1)}, f32[21,8,128]{2,1,0:T(8,128)S(1)}, u32[]{:S(2)}, u32[]{:S(2)}) %collective-permute-start.2) | collective-permute-done | bytes 86048 | tf_op jit(solution)/shard_map/ppermute | solution.py:465
  13.2 0.0 collective-permute-done.relay_ref
  13.2 0.5 %pack_late.1 = (f32[21,8,128]{2,1,0:T(8,128)S(1)}, f32[2,21,8,128]{3,2,1,0:T(8,128)S(1)}, f32[21,8,128]{2,1,0:T(8,128)S(1)}, f32[21,8,128]{2,1,0:T(8,128)S(1)}, f32[2,21,8,128]{3,2,1,0:T(8,128)S(1)}) custom-call(s32[1,128]{1,0:T(1,128)S(1)} %bitcast.6, f32[5,128,512]{2,1,0:T(8,128)S(1)} %bitcast.3, f32[2,21,8,128]{3,2,1,0:T(8,128)S(1)} %collective-permute-done.relay_ref, ...), custom_call_target="tpu_custom_call" | custom-call | tf_op jit(solution)/shard_map/pack_late/pallas_call | solution.py:155
  13.7 1.6 %collective-permute-start.6 = (f32[2,21,8,128]{3,2,1,0:T(8,128)S(1)}, f32[2,21,8,128]{3,2,1,0:T(8,128)S(1)}, u32[]{:S(2)}, u32[]{:S(2)}) collective-permute-start(f32[2,21,8,128]{3,2,1,0:T(8,128)S(1)} %get-tuple-element.27), channel_id=1, source_target_pairs={{0,4},{1,5},{2,6},{3,7},{4,0},{5,1},{6,2},{7,3},{8,12},{9,13},{10,... | collective-permute-start | bytes 516104 | tf_op jit(solution)/shard_map/ppermute | solution.py:465
  15.3 2.2 %collective-permute-start.9 = (f32[2,21,8,128]{3,2,1,0:T(8,128)S(1)}, f32[2,21,8,128]{3,2,1,0:T(8,128)S(1)}, u32[]{:S(2)}, u32[]{:S(2)}) collective-permute-start(f32[2,21,8,128]{3,2,1,0:T(8,128)S(1)} %get-tuple-element.30), channel_id=1, source_target_pairs={{0,8},{1,9},{2,2},{3,3},{4,4},{5,5},{8,16},{9,17},{10,10},{11,11},... | collective-permute-start | bytes 516104 | tf_op jit(solution)/shard_map/ppermute | solution.py:465
  17.5 0.1 collective-permute-start.3
  17.6 0.0 collective-permute-done.4.two_ref
  17.6 0.6 %collective-permute-start.7 = (f32[21,8,128]{2,1,0:T(8,128)S(1)}, f32[21,8,128]{2,1,0:T(8,128)S(1)}, u32[]{:S(2)}, u32[]{:S(2)}) collective-permute-start(f32[21,8,128]{2,1,0:T(8,128)S(1)} %get-tuple-element.28), channel_id=1, source_target_pairs={{0,5},{1,4},{2,7},{3,6},{4,1},{5,0},{6,3},{7,2},{8,13},{9,12},{10,... | collective-permute-start | bytes 258056 | tf_op jit(solution)/shard_map/ppermute | solution.py:465
  18.2 0.0 collective-permute-done.5.three_ref
  18.2 3.3 %collective-permute-start.8 = (f32[21,8,128]{2,1,0:T(8,128)S(1)}, f32[21,8,128]{2,1,0:T(8,128)S(1)}, u32[]{:S(2)}, u32[]{:S(2)}) collective-permute-start(f32[21,8,128]{2,1,0:T(8,128)S(1)} %get-tuple-element.29), channel_id=1, source_target_pairs={{0,64},{1,65},{2,66},{3,67},{4,68},{5,69},{6,70},{7,71},{8,72},{9,... | collective-permute-start | bytes 258056 | tf_op jit(solution)/shard_map/ppermute | solution.py:465
  21.5 1.9 %collective-permute-done.7.five_ref = f32[21,8,128]{2,1,0:T(8,128)S(1)} collective-permute-done((f32[21,8,128]{2,1,0:T(8,128)S(1)}, f32[21,8,128]{2,1,0:T(8,128)S(1)}, u32[]{:S(2)}, u32[]{:S(2)}) %collective-permute-start.7) | collective-permute-done | bytes 86048 | tf_op jit(solution)/shard_map/ppermute | solution.py:465
  23.4 1.0 %collective-permute-done.8.far_ref = f32[21,8,128]{2,1,0:T(8,128)S(1)} collective-permute-done((f32[21,8,128]{2,1,0:T(8,128)S(1)}, f32[21,8,128]{2,1,0:T(8,128)S(1)}, u32[]{:S(2)}, u32[]{:S(2)}) %collective-permute-start.8) | collective-permute-done | bytes 86048 | tf_op jit(solution)/shard_map/ppermute | solution.py:465
  24.4 2.8 %unpack.1 = (f32[2560,128]{1,0:T(8,128)S(1)}, f32[2560,128]{1,0:T(8,128)S(1)}, f32[480,128]{1,0:T(8,128)S(1)}, f32[480,128]{1,0:T(8,128)S(1)}, f32[240,128]{1,0:T(8,128)S(1)}, /*index=5*/f32[240,128]{1,0:T(8,128)S(1)}) custom-call(s32[1,128]{1,0:T(1,128)S(1)} %bitcast.7, f32[5,128,512]{2,1,0:T(8,128)S(1)} %bitcast.4, ...), custom_call_target="tpu_custom_call" | custom-call | tf_op jit(solution)/shard_map/unpack/pallas_call | solution.py:249
  27.2 1.7 %collective-permute-start.12 = (f32[480,128]{1,0:T(8,128)S(1)}, f32[480,128]{1,0:T(8,128)S(1)}, u32[]{:S(2)}, u32[]{:S(2)}) collective-permute-start(f32[480,128]{1,0:T(8,128)S(1)} %get-tuple-element.35), channel_id=1, source_target_pairs={{0,8},{8,0},{16,24},{24,16},{32,40},{40,32},{48,56},{56,48},{64,72... | collective-permute-start | bytes 737288 | tf_op jit(solution)/shard_map/ppermute | solution.py:465
  28.9 5.0 %collective-permute-start.13 = (f32[480,128]{1,0:T(8,128)S(1)}, f32[480,128]{1,0:T(8,128)S(1)}, u32[]{:S(2)}, u32[]{:S(2)}) collective-permute-start(f32[480,128]{1,0:T(8,128)S(1)} %get-tuple-element.36), channel_id=1, source_target_pairs={{0,120},{8,16},{16,8},{24,32},{32,24},{40,48},{48,40},{56,64},{64,... | collective-permute-start | bytes 737288 | tf_op jit(solution)/shard_map/ppermute | solution.py:465
  33.9 0.0 collective-permute-start.10
  33.9 0.6 %collective-permute-start.11 = (f32[240,128]{1,0:T(8,128)S(1)}, f32[240,128]{1,0:T(8,128)S(1)}, u32[]{:S(2)}, u32[]{:S(2)}) collective-permute-start(f32[240,128]{1,0:T(8,128)S(1)} %get-tuple-element.34), channel_id=1, source_target_pairs={{0,1},{1,0},{2,3},{3,2},{4,5},{5,4},{6,7},{7,6},{8,9},{9,8},{10,11... | collective-permute-start | bytes 368648 | tf_op jit(solution)/shard_map/ppermute | solution.py:465
  34.5 3.7 %flux_inner.1.before_ref = f32[2560,128]{1,0:T(8,128)S(1)} custom-call(f32[2560,128]{1,0:T(8,128)S(1)} %get-tuple-element.31.state_ref, f32[2560,128]{1,0:T(8,128)S(1)} %get-tuple-element.32.prim_ref), custom_call_target="tpu_custom_call" | custom-call | flops 20000000 | bytes 4000000 | tf_op jit(solution)/shard_map/flux_inner/pallas_call | solution.py:441
  38.2 1.2 %collective-permute-done.10.second_ref = f32[240,128]{1,0:T(8,128)S(1)} collective-permute-done((f32[240,128]{1,0:T(8,128)S(1)}, f32[240,128]{1,0:T(8,128)S(1)}, u32[]{:S(2)}, u32[]{:S(2)}) %collective-permute-start.10) | collective-permute-done | bytes 122912 | tf_op jit(solution)/shard_map/ppermute | solution.py:465
  39.4 0.0 collective-permute-done.11.first_ref
  39.4 2.1 %flux_second.1.change_ref = f32[2560,128]{1,0:T(8,128)S(1)} custom-call(f32[2560,128]{1,0:T(8,128)S(1)} %get-tuple-element.32.prim_ref, f32[240,128]{1,0:T(8,128)S(1)} %collective-permute-done.10.second_ref, f32[240,128]{1,0:T(8,128)S(1)} %collective-permute-done.11.first_ref), custom_call_target="tpu_custom_call" | custom-call | flops 20000000 | bytes 4000000 | tf_op jit(solution)/shard_map/flux_second/pallas_call | solution.py:441
  41.5 0.0 collective-permute-done.12.first_ref
  41.5 2.7 %flux_first.1 = f32[5,16,32,128]{3,2,1,0:T(8,128)} custom-call(f32[2560,128]{1,0:T(8,128)S(1)} %flux_inner.1.before_ref, f32[2560,128]{1,0:T(8,128)S(1)} %get-tuple-element.32.prim_ref, f32[2560,128]{1,0:T(8,128)S(1)} %flux_second.1.change_ref, f32[480,128]{1,0:T(8,128)S(1)} %collective-permute-done.12.first_ref, ...), custom_call_target="tpu_custom_call" | custom-call | tf_op jit(solution)/shard_map/flux_first/pallas_call | solution.py:452
  (6 shorter events, 0.0 us)
Async XLA Ops:
  0.0 1.3 %copy-start = (f32[128,5,512]{2,0,1:T(8,128)S(1)}, f32[128,5,512]{2,0,1:T(8,128)}, u32[]{:S(2)}) copy-start(f32[128,5,512]{2,0,1:T(8,128)} %param.2) | copy-start | bytes 3932164
  1.3 0.7 %copy-start.1 = (s32[128]{0:T(128)S(1)}, s32[128]{0:T(128)}, u32[]{:S(2)}) copy-start(s32[128]{0:T(128)} %param.3) | copy-start | bytes 1540
  2.5 10.7 %collective-permute-start = (f32[2,21,8,128]{3,2,1,0:T(8,128)S(1)}, f32[2,21,8,128]{3,2,1,0:T(8,128)S(1)}, u32[]{:S(2)}, u32[]{:S(2)}) collective-permute-start(f32[2,21,8,128]{3,2,1,0:T(8,128)S(1)} %get-tuple-element.21), channel_id=1, source_target_pairs={{0,6},{1,7},{2,4},{3,5},{4,12},{5,13},{6,14},{7,15},{8,0},{9,1},{1... | collective-permute-start | bytes 516104 | tf_op jit(solution)/shard_map/ppermute | solution.py:465
  5.6 6.4 %collective-permute-start.1 = (f32[21,8,128]{2,1,0:T(8,128)S(1)}, f32[21,8,128]{2,1,0:T(8,128)S(1)}, u32[]{:S(2)}, u32[]{:S(2)}) collective-permute-start(f32[21,8,128]{2,1,0:T(8,128)S(1)} %get-tuple-element.22), channel_id=1, source_target_pairs={{0,6},{1,7},{2,4},{3,5},{4,2},{5,3},{6,0},{7,1},{8,14},{9,15},{10,... | collective-permute-start | bytes 258056 | tf_op jit(solution)/shard_map/ppermute | solution.py:465
  7.6 5.6 %collective-permute-start.2 = (f32[21,8,128]{2,1,0:T(8,128)S(1)}, f32[21,8,128]{2,1,0:T(8,128)S(1)}, u32[]{:S(2)}, u32[]{:S(2)}) collective-permute-start(f32[21,8,128]{2,1,0:T(8,128)S(1)} %get-tuple-element.23), channel_id=1, source_target_pairs={{0,7},{1,6},{2,5},{3,4},{4,3},{5,2},{6,1},{7,0},{8,15},{9,14},{10,... | collective-permute-start | bytes 258056 | tf_op jit(solution)/shard_map/ppermute | solution.py:465
  7.8 9.9 %collective-permute-start.4 = (f32[21,8,128]{2,1,0:T(8,128)S(1)}, f32[21,8,128]{2,1,0:T(8,128)S(1)}, u32[]{:S(2)}, u32[]{:S(2)}) collective-permute-start(f32[21,8,128]{2,1,0:T(8,128)S(1)} %get-tuple-element.25), channel_id=1, source_target_pairs={{0,2},{1,3},{2,0},{3,1},{4,6},{5,7},{6,4},{7,5},{8,10},{9,11},{10,... | collective-permute-start | bytes 258056 | tf_op jit(solution)/shard_map/ppermute | solution.py:465
  7.8 10.4 %collective-permute-start.5 = (f32[21,8,128]{2,1,0:T(8,128)S(1)}, f32[21,8,128]{2,1,0:T(8,128)S(1)}, u32[]{:S(2)}, u32[]{:S(2)}) collective-permute-start(f32[21,8,128]{2,1,0:T(8,128)S(1)} %get-tuple-element.26), channel_id=1, source_target_pairs={{0,3},{1,2},{2,1},{3,0},{4,7},{5,6},{6,5},{7,4},{8,11},{9,10},{10,... | collective-permute-start | bytes 258056 | tf_op jit(solution)/shard_map/ppermute | solution.py:465
  13.7 10.7 %collective-permute-start.6 = (f32[2,21,8,128]{3,2,1,0:T(8,128)S(1)}, f32[2,21,8,128]{3,2,1,0:T(8,128)S(1)}, u32[]{:S(2)}, u32[]{:S(2)}) collective-permute-start(f32[2,21,8,128]{3,2,1,0:T(8,128)S(1)} %get-tuple-element.27), channel_id=1, source_target_pairs={{0,4},{1,5},{2,6},{3,7},{4,0},{5,1},{6,2},{7,3},{8,12},{9,13},{10,... | collective-permute-start | bytes 516104 | tf_op jit(solution)/shard_map/ppermute | solution.py:465
  15.3 9.1 %collective-permute-start.9 = (f32[2,21,8,128]{3,2,1,0:T(8,128)S(1)}, f32[2,21,8,128]{3,2,1,0:T(8,128)S(1)}, u32[]{:S(2)}, u32[]{:S(2)}) collective-permute-start(f32[2,21,8,128]{3,2,1,0:T(8,128)S(1)} %get-tuple-element.30), channel_id=1, source_target_pairs={{0,8},{1,9},{2,2},{3,3},{4,4},{5,5},{8,16},{9,17},{10,10},{11,11},... | collective-permute-start | bytes 516104 | tf_op jit(solution)/shard_map/ppermute | solution.py:465
  17.5 4.0 %collective-permute-start.3 = (f32[21,8,128]{2,1,0:T(8,128)S(1)}, f32[21,8,128]{2,1,0:T(8,128)S(1)}, u32[]{:S(2)}, u32[]{:S(2)}) collective-permute-start(f32[21,8,128]{2,1,0:T(8,128)S(1)} %get-tuple-element.24), channel_id=1, source_target_pairs={{0,1},{1,0},{2,3},{3,2},{4,5},{5,4},{6,7},{7,6},{8,9},{9,8},{10,11... | collective-permute-start | bytes 258056 | tf_op jit(solution)/shard_map/ppermute | solution.py:465
  17.6 5.8 %collective-permute-start.7 = (f32[21,8,128]{2,1,0:T(8,128)S(1)}, f32[21,8,128]{2,1,0:T(8,128)S(1)}, u32[]{:S(2)}, u32[]{:S(2)}) collective-permute-start(f32[21,8,128]{2,1,0:T(8,128)S(1)} %get-tuple-element.28), channel_id=1, source_target_pairs={{0,5},{1,4},{2,7},{3,6},{4,1},{5,0},{6,3},{7,2},{8,13},{9,12},{10,... | collective-permute-start | bytes 258056 | tf_op jit(solution)/shard_map/ppermute | solution.py:465
  18.2 6.2 %collective-permute-start.8 = (f32[21,8,128]{2,1,0:T(8,128)S(1)}, f32[21,8,128]{2,1,0:T(8,128)S(1)}, u32[]{:S(2)}, u32[]{:S(2)}) collective-permute-start(f32[21,8,128]{2,1,0:T(8,128)S(1)} %get-tuple-element.29), channel_id=1, source_target_pairs={{0,64},{1,65},{2,66},{3,67},{4,68},{5,69},{6,70},{7,71},{8,72},{9,... | collective-permute-start | bytes 258056 | tf_op jit(solution)/shard_map/ppermute | solution.py:465
  27.2 14.3 %collective-permute-start.12 = (f32[480,128]{1,0:T(8,128)S(1)}, f32[480,128]{1,0:T(8,128)S(1)}, u32[]{:S(2)}, u32[]{:S(2)}) collective-permute-start(f32[480,128]{1,0:T(8,128)S(1)} %get-tuple-element.35), channel_id=1, source_target_pairs={{0,8},{8,0},{16,24},{24,16},{32,40},{40,32},{48,56},{56,48},{64,72... | collective-permute-start | bytes 737288 | tf_op jit(solution)/shard_map/ppermute | solution.py:465
  28.9 12.6 %collective-permute-start.13 = (f32[480,128]{1,0:T(8,128)S(1)}, f32[480,128]{1,0:T(8,128)S(1)}, u32[]{:S(2)}, u32[]{:S(2)}) collective-permute-start(f32[480,128]{1,0:T(8,128)S(1)} %get-tuple-element.36), channel_id=1, source_target_pairs={{0,120},{8,16},{16,8},{24,32},{32,24},{40,48},{48,40},{56,64},{64,... | collective-permute-start | bytes 737288 | tf_op jit(solution)/shard_map/ppermute | solution.py:465
  33.9 5.5 %collective-permute-start.10 = (f32[240,128]{1,0:T(8,128)S(1)}, f32[240,128]{1,0:T(8,128)S(1)}, u32[]{:S(2)}, u32[]{:S(2)}) collective-permute-start(f32[240,128]{1,0:T(8,128)S(1)} %get-tuple-element.33), channel_id=1, source_target_pairs={{0,7},{1,2},{2,1},{3,4},{4,3},{5,6},{6,5},{7,0},{8,15},{9,10},{10,... | collective-permute-start | bytes 368648 | tf_op jit(solution)/shard_map/ppermute | solution.py:465
  33.9 5.5 %collective-permute-start.11 = (f32[240,128]{1,0:T(8,128)S(1)}, f32[240,128]{1,0:T(8,128)S(1)}, u32[]{:S(2)}, u32[]{:S(2)}) collective-permute-start(f32[240,128]{1,0:T(8,128)S(1)} %get-tuple-element.34), channel_id=1, source_target_pairs={{0,1},{1,0},{2,3},{3,2},{4,5},{5,4},{6,7},{7,6},{8,9},{9,8},{10,11... | collective-permute-start | bytes 368648 | tf_op jit(solution)/shard_map/ppermute | solution.py:465
